TPU v7x, 256 devices: a whole 4x4x8 slice. The times are simulated.
256 devices in a mesh: group: 16 (over x, z_hi, core), rows: 16 (over z_lo, y).
Axes of the slice: x: 4, y: 4, z: 8 (z_hi: 2, z_lo: 4; z = z_hi * 4 + z_lo), core: 2. Of those that a mesh axis runs over, the one named last changes fastest.
Arguments:
- image: bfloat16 [2048, 128, 352], P(('group', 'rows')), parts along dimension 0, may hold values from -6 to 6
- visible: int32 [256, 16], P(('group', 'rows')), parts along dimension 0, may hold values 0 or 1
- layer_norm_gain: float32 [352], replicated, may hold values from 0.5 to 1.5
- reducer_weight: bfloat16 [1408, 704], replicated, may hold values from -0.15625 to 0.15625
- reducer_bias: float32 [704], replicated, may hold values from -3 to 3
- depth_kernel: float32 [49, 704], replicated, may hold values from -0.875 to 0.875
- depth_bias: float32 [704], replicated, may hold values from -3 to 3
- cotangent: bfloat16 [1024, 64, 704], P(('group', 'rows')), parts along dimension 0, may hold values from -6 to 6
Outputs:
- features: bfloat16 [1024, 64, 704], P(('group', 'rows')), parts along dimension 0
- image_grad: bfloat16 [2048, 128, 352], P(('group', 'rows')), parts along dimension 0
- down_weight_grad: float32 [22528, 704], P(('group', 'rows')), parts along dimension 0
- gain_grad: float32 [5632], P('group'), parts along dimension 0
- down_bias_grad: float32 [11264], P('group'), parts along dimension 0
- kernel_grad: float32 [784, 704], P('group'), parts along dimension 0
- depth_bias_grad: float32 [11264], P('group'), parts along dimension 0
There are 16 independent parts, one for each index of `group`. A program takes and returns all parts, laid end to end along the dimension named above; an argument that names none is the same for every part. Nothing has to cross between parts.
Inputs may be any that keep to these rules, and one draw needn't show every extreme that they name: visible holds one 0 or 1 for each patch of 4 x 4 output pixels.
All inputs are finite; a program needn't handle non-finite values. No bound on the sum of `visible` on one device may be relied on, other than what follows from the above.
Results may differ from a plain program's by a relative error of at most 0.024.
Values may be sent and summed in bfloat16 or wider, within the bound.
No kernel may reach another device: no remote copies, remote signals or barrier semaphores. Data moves between devices by JAX's collectives and lax.ppermute only.
A program may use at most 64 MiB of HBM per device.

v0:
```python
import math

import jax
import jax.numpy as jnp
from jax import lax
from jax.sharding import PartitionSpec as P

KS = 7
PATCH = 4


def with_halo(value, sides, width):
    for axis, dim in sides:
        size, length = (lax.axis_size(axis), value.shape[dim])
        up = [(i, (i + 1) % size) for i in range(size - 1)]
        down = [(j, i) for i, j in up]
        last = lax.slice_in_dim(value, length - width, length, axis=dim)
        first = lax.slice_in_dim(value, 0, width, axis=dim)
        before = lax.ppermute(last, axis, up)
        after = lax.ppermute(first, axis, down)
        value = jnp.concatenate([before, value, after], axis=dim)
    return value


def standardize(image):
    xf = image.astype(jnp.float32)
    center = jnp.mean(xf, axis=-1, keepdims=True)
    spread = jnp.mean((xf - center) ** 2, axis=-1, keepdims=True)
    reciprocal_spread = 1.0 / jnp.sqrt(spread + 1e-06)
    return ((xf - center) * reciprocal_spread, reciprocal_spread)


def to_patches(scaled):
    height, width, chans = scaled.shape
    split = scaled.reshape(height // 2, 2, width // 2, 2, chans)
    return split.transpose(0, 2, 1, 3, 4).reshape(height // 2 * (width // 2), 4 * chans)


def from_patches(flat, height, width, chans):
    split = flat.reshape(height, width, 2, 2, chans)
    return split.transpose(0, 2, 1, 3, 4).reshape(2 * height, 2 * width, chans)


def expand_mask(visible):
    return jnp.repeat(jnp.repeat(visible, PATCH, 0), PATCH, 1).astype(jnp.float32)[:, :, None]


def shrink_resolution(image, visibility_mask_lines, layer_norm_gain, reducer_weight, reducer_bias):
    normalized_input, reciprocal_spread = standardize(image)
    patch_tiles = to_patches((normalized_input * layer_norm_gain).astype(jnp.bfloat16))
    height = image.shape[0] // 2
    width = image.shape[1] // 2
    pre = jnp.dot(patch_tiles, reducer_weight, preferred_element_type=jnp.float32) + reducer_bias
    reduce_step = (
        pre.reshape(height, width, reducer_weight.shape[1]) * visibility_mask_lines
    ).astype(jnp.bfloat16)
    return (normalized_input, reciprocal_spread, patch_tiles, reduce_step)


def body(
    image,
    visible,
    layer_norm_gain,
    reducer_weight,
    reducer_bias,
    depth_kernel,
    depth_bias,
    cotangent,
):
    height, width, chans = cotangent.shape
    in_chans = image.shape[2]
    bands = lax.axis_size("rows")
    scale = 1.0 / math.sqrt(height * bands * width)
    pixel_mask = expand_mask(visible)
    normalized_input, reciprocal_spread, patch_tiles, reduce_step = shrink_resolution(
        image, pixel_mask, layer_norm_gain, reducer_weight, reducer_bias
    )
    banded = with_halo(reduce_step, (("rows", 0),), 3)
    padded = jnp.pad(banded, ((0, 0), (3, 3), (0, 0)))
    acc = jnp.zeros((height, width, chans), jnp.float32)
    for i in range(KS):
        for j in range(KS):
            acc = (
                acc
                + padded[i : i + height, j : j + width].astype(jnp.float32)
                * depth_kernel[KS * i + j]
            )
    depth = pixel_mask * (acc + depth_bias)
    features = (reduce_step.astype(jnp.float32) + depth).astype(jnp.bfloat16)
    masked_cot = (pixel_mask * cotangent.astype(jnp.float32)).astype(jnp.bfloat16)
    cot_band = with_halo(masked_cot, (("rows", 0),), 3)
    cot_pad = jnp.pad(cot_band, ((0, 0), (3, 3), (0, 0)))
    masked_f = masked_cot.astype(jnp.float32)
    back = jnp.zeros((height, width, chans), jnp.float32)
    kernel_terms = []
    for i in range(KS):
        for j in range(KS):
            back = (
                back
                + cot_pad[6 - i : 6 - i + height, 6 - j : 6 - j + width].astype(jnp.float32)
                * depth_kernel[KS * i + j]
            )
            kernel_terms.append(
                jnp.sum(
                    padded[i : i + height, j : j + width].astype(jnp.float32) * masked_f,
                    axis=(0, 1),
                )
            )
    kernel_term = jnp.stack(kernel_terms) * scale
    depth_bias_term = jnp.sum(masked_f, axis=(0, 1)) * scale
    down_cot = cotangent.astype(jnp.float32) + back
    pre_cot = (pixel_mask * down_cot).astype(jnp.bfloat16).reshape(height * width, chans)
    flat_cot = lax.dot_general(
        pre_cot, reducer_weight, (((1,), (1,)), ((), ())), preferred_element_type=jnp.float32
    )
    scaled_cot = from_patches(flat_cot, height, width, in_chans)
    product = lax.dot_general(
        patch_tiles, pre_cot, (((0,), (0,)), ((), ())), preferred_element_type=jnp.float32
    )
    down_weight_grad = lax.psum_scatter(
        (product * scale).astype(jnp.bfloat16), "rows", scatter_dimension=0, tiled=True
    ).astype(jnp.float32)
    gain_term = jnp.sum(normalized_input * scaled_cot, axis=(0, 1)) * scale
    bias_term = jnp.sum(pre_cot.astype(jnp.float32), axis=0) * scale
    gathered = scaled_cot * layer_norm_gain
    image_grad = reciprocal_spread * (
        gathered
        - jnp.mean(gathered, axis=-1, keepdims=True)
        - normalized_input * jnp.mean(gathered * normalized_input, axis=-1, keepdims=True)
    )
    gain_grad, down_bias_grad, kernel_grad, depth_bias_grad = (
        lax.psum(gain_term.astype(jnp.bfloat16), "rows").astype(jnp.float32),
        lax.psum(bias_term.astype(jnp.bfloat16), "rows").astype(jnp.float32),
        lax.psum(kernel_term.astype(jnp.bfloat16), "rows").astype(jnp.float32),
        lax.psum(depth_bias_term.astype(jnp.bfloat16), "rows").astype(jnp.float32),
    )
    return (
        features,
        image_grad.astype(jnp.bfloat16),
        down_weight_grad,
        gain_grad,
        down_bias_grad,
        kernel_grad,
        depth_bias_grad,
    )


def solution(mesh):
    placed = (
        P(("group", "rows"), None, None),
        P(("group", "rows"), None),
        P(),
        P(),
        P(),
        P(),
        P(),
        P(("group", "rows"), None, None),
    )
    return jax.shard_map(
        body,
        mesh=mesh,
        in_specs=placed,
        out_specs=(
            P(("group", "rows"), None, None),
            P(("group", "rows"), None, None),
            P(("group", "rows"), None),
            P("group"),
            P("group"),
            P("group", None),
            P("group"),
        ),
        check_vma=False,
    )
```

profile of v0, /device:TPU:2, one launch (start us, length us, event | category | flops | bytes accessed | tf_op | source)
XLA Modules:
  0.0 331.1 jit_solution(11005840433627912586)
XLA Ops:
  8.1 1.5 copy.30
  12.1 0.8 copy-done.4
  12.9 2.3 convolution_add_fusion
  15.7 3.6 %collective-permute-start = (bf16[3,64,704]{2,1,0:T(8,128)(2,1)S(1)}, bf16[3,64,704]{2,1,0:T(8,128)(2,1)S(1)}, u32[]{:S(2)}, u32[]{:S(2)}) collective-permute-start(bf16[3,64,704]{2,1,0:T(8,128)(2,1)S(1)} %get-tuple-element.140), channel_id=1, source_target_pairs={{0,1},{1,2},{2,3},{3,4},{4,5},{5,6},{6,7},{7,8},{8,9},{9,10},{10,1... | collective-permute-start | bytes 811016 | tf_op jit(solution)/shard_map/ppermute | solution.py:19
  19.3 1.3 collective-permute-start.1
  20.7 0.8 slice_reduce_fusion.47
  21.5 0.8 slice_reduce_fusion.48
  22.2 3.3 %collective-permute-done = bf16[3,64,704]{2,1,0:T(8,128)(2,1)S(1)} collective-permute-done((bf16[3,64,704]{2,1,0:T(8,128)(2,1)S(1)}, bf16[3,64,704]{2,1,0:T(8,128)(2,1)S(1)}, u32[]{:S(2)}, u32[]{:S(2)}) %collective-permute-start) | collective-permute-done | bytes 270368 | tf_op jit(solution)/shard_map/ppermute | solution.py:19
  25.6 4.1 %collective-permute-done.1 = bf16[3,64,704]{2,1,0:T(8,128)(2,1)S(1)} collective-permute-done((bf16[3,64,704]{2,1,0:T(8,128)(2,1)S(1)}, bf16[3,64,704]{2,1,0:T(8,128)(2,1)S(1)}, u32[]{:S(2)}, u32[]{:S(2)}) %collective-permute-start.1) | collective-permute-done | bytes 270368 | tf_op jit(solution)/shard_map/ppermute | solution.py:20
  30.0 2.3 fusion.139
  32.3 2.2 fusion.140
  34.5 0.9 fusion.152
  35.3 4.2 %collective-permute-start.2 = (bf16[3,64,704]{2,1,0:T(8,128)(2,1)}, bf16[3,64,704]{2,1,0:T(8,128)(2,1)}, u32[]{:S(2)}, u32[]{:S(2)}) collective-permute-start(bf16[3,64,704]{2,1,0:T(8,128)(2,1)} %get-tuple-element.138), channel_id=1, source_target_pairs={{0,1},{1,2},{2,3},{3,4},{4,5},{5,6},{6,7},{7,8},{8,9},{9,10},{10,1... | collective-permute-start | bytes 811016 | tf_op jit(solution)/shard_map/ppermute | solution.py:19
  39.5 1.3 collective-permute-start.3
  40.8 1.2 fusion.137
  71.5 5.2 %stack.199 = f32[49,704]{1,0:T(8,128)S(1)} concatenate(f32[1,704]{1,0:T(1,128)} %stack.150, f32[1,704]{1,0:T(1,128)} %stack.151, f32[1,704]{1,0:T(1,128)} %stack.152, f32[1,704]{1,0:T(1,128)} %stack.153, f32[1,704]{1,0:T(1,128)} %stack.154, f32[1,704]{1,0:T(1,128)} %stack.155, f32[1,704]{1,0:T(1,128)} %stack.156, f32[1,704]{1,0:T(1,128)} %stack.157, f32[1,704]{1,0:T(1,128)} %stack.158, ...), dimensions={0} | concatenate | bytes 275968 | tf_op jit(solution)/shard_map/stack | solution.py:109
  77.9 1.4 select_maximum_fusion
  79.5 7.4 %convert_reduce_fusion.2 = (f32[704]{0:T(1024)S(1)}, bf16[4,64,704]{2,1,0:T(8,128)(2,1)S(1)}) fusion(f32[704]{0:T(1024)S(1)} %get-tuple-element.130, bf16[10,70,704]{2,1,0:T(8,128)(2,1)S(1)} %select_maximum_fusion, f32[704]{0:T(1024)S(1)} %get-tuple-element.131, f32[704]{0:T(1024)S(1)} %copy-done.14, f32[704]{0:T(1024)S(1)} %copy-done.15, ...), kind=kLoop, calls=%fused_computation.264 | loop fusion | flops 28474688 | bytes 16901888 | tf_op jit(solution)/shard_map/reduce_sum | solution.py:124
  86.9 0.7 copy-done.2
  87.7 2.1 multiply_convert_fusion
  89.9 4.0 %copy.39 = bf16[1408,704]{1,0:T(8,128)(2,1)} copy(bf16[1408,704]{0,1:T(8,128)(2,1)} %param.11) | data formatting | bytes 3964928 | tf_op jit(solution)/shard_map/dot_general | solution.py:113
  93.9 6.7 %fusion.66 = bf16[4,64,704]{2,1,0:T(8,128)(2,1)} fusion(bf16[4,64,704]{2,1,0:T(8,128)(2,1)S(1)} %multiply_convert_fusion.1, f32[704]{0:T(1024)S(1)} %copy-done.35, f32[704]{0:T(1024)S(1)} %get-tuple-element.130, f32[704]{0:T(1024)S(1)} %get-tuple-element.131, f32[704]{0:T(1024)S(1)} %copy-done.14, f32[704]{0:T(1024)S(1)} %copy-done.15, ...), kind=kLoop, calls=%fused_computation.189 | loop fusion | flops 28114944 | bytes 16541440 | tf_op jit(solution)/shard_map/convert_element_type | solution.py:89
  100.7 130.3 %all-reduce.5.cloned.1.call-done = bf16[49,704]{1,0:T(8,128)(2,1)} async-done(((bf16[49,704]{1,0:T(8,128)(2,1)}), bf16[49,704]{1,0:T(8,128)(2,1)}) %all-reduce.5.cloned.1.call-update) | async-done | bytes 69008 | tf_op jit(solution)/shard_map/psum | solution.py:134
  231.0 1.6 convert_element_type.536
  232.5 2.5 multiply_reduce_fusion
  235.4 2.4 copy.34
  237.8 2.4 reshape.122
  240.8 42.6 %all-reduce.2 = (bf16[352]{0:T(512)(128)(2,1)S(1)}, bf16[704]{0:T(1024)(128)(2,1)S(1)}, bf16[704]{0:T(1024)(128)(2,1)S(1)}) all-reduce(bf16[352]{0:T(512)(128)(2,1)S(1)} %multiply_convert_fusion.5, bf16[704]{0:T(1024)(128)(2,1)S(1)} %multiply_convert_fusion.4, ...), channel_id=1, replica_groups=mesh['group'=16,'rows'=16] {'rows'}, use_global_device_ids=true, to_apply=%region_6.7 | all-reduce | flops 1760 | bytes 7040 | tf_op jit(solution)/shard_map/psum | solution.py:132
  285.2 0.7 fusion.11
  285.9 1.1 copy.37
  287.0 35.6 %reduce-scatter.2.cloned.1.call-done = bf16[88,704]{1,0:T(8,128)(2,1)} async-done(((bf16[1408,704]{1,0:T(8,128)(2,1)}), bf16[88,704]{1,0:T(8,128)(2,1)}) %reduce-scatter.2.cloned.1.call-update) | async-done | bytes 123920 | tf_op jit(solution)/shard_map/reduce_scatter | solution.py:120
  322.6 1.6 convert_element_type.529
  (156 shorter events, 37.5 us)
Async XLA Ops:
  7.2 3.1 copy-start.7
  7.2 223.8 %all-reduce.5.cloned.1.call-start = ((), (), s32[]{:S(2)}) async-start(), calls=%async_computation.2 | async-start | bytes 172032 | tf_op jit(solution)/shard_map/psum | solution.py:134
  8.0 22.0 %copy-start.33 = (f32[64]{0:T(128)}, f32[64]{0:T(128)S(1)}, u32[]{:S(2)}) copy-start(f32[64]{0:T(128)S(1)} %convert_element_type.423) | copy-start | bytes 772
  10.9 2.0 copy-start.36
  15.2 5.4 %copy-start.6 = (f32[49,704]{1,0:T(8,128)S(1)}, f32[49,704]{1,0:T(8,128)}, u32[]{:S(2)}) copy-start(f32[49,704]{1,0:T(8,128)} %param.13) | copy-start | bytes 413956
  15.6 14.4 %copy-start = (bf16[4,64,704]{2,1,0:T(8,128)(2,1)S(1)}, bf16[4,64,704]{2,1,0:T(8,128)(2,1)}, u32[]{:S(2)}) copy-start(bf16[4,64,704]{2,1,0:T(8,128)(2,1)} %param.15) | copy-start | bytes 1081348
  15.7 9.9 %collective-permute-start = (bf16[3,64,704]{2,1,0:T(8,128)(2,1)S(1)}, bf16[3,64,704]{2,1,0:T(8,128)(2,1)S(1)}, u32[]{:S(2)}, u32[]{:S(2)}) collective-permute-start(bf16[3,64,704]{2,1,0:T(8,128)(2,1)S(1)} %get-tuple-element.140), channel_id=1, source_target_pairs={{0,1},{1,2},{2,3},{3,4},{4,5},{5,6},{6,7},{7,8},{8,9},{9,10},{10,1... | collective-permute-start | bytes 811016 | tf_op jit(solution)/shard_map/ppermute | solution.py:19
  19.3 10.4 %collective-permute-start.1 = (bf16[3,64,704]{2,1,0:T(8,128)(2,1)S(1)}, bf16[3,64,704]{2,1,0:T(8,128)(2,1)S(1)}, u32[]{:S(2)}, u32[]{:S(2)}) collective-permute-start(bf16[3,64,704]{2,1,0:T(8,128)(2,1)S(1)} %get-tuple-element.141), channel_id=1, source_target_pairs={{1,0},{2,1},{3,2},{4,3},{5,4},{6,5},{7,6},{8,7},{9,8},{10,9},{11,1... | collective-permute-start | bytes 811016 | tf_op jit(solution)/shard_map/ppermute | solution.py:20
  35.3 42.5 %collective-permute-start.2 = (bf16[3,64,704]{2,1,0:T(8,128)(2,1)}, bf16[3,64,704]{2,1,0:T(8,128)(2,1)}, u32[]{:S(2)}, u32[]{:S(2)}) collective-permute-start(bf16[3,64,704]{2,1,0:T(8,128)(2,1)} %get-tuple-element.138), channel_id=1, source_target_pairs={{0,1},{1,2},{2,3},{3,4},{4,5},{5,6},{6,7},{7,8},{8,9},{9,10},{10,1... | collective-permute-start | bytes 811016 | tf_op jit(solution)/shard_map/ppermute | solution.py:19
  39.5 38.3 %collective-permute-start.3 = (bf16[3,64,704]{2,1,0:T(8,128)(2,1)}, bf16[3,64,704]{2,1,0:T(8,128)(2,1)}, u32[]{:S(2)}, u32[]{:S(2)}) collective-permute-start(bf16[3,64,704]{2,1,0:T(8,128)(2,1)} %get-tuple-element.139), channel_id=1, source_target_pairs={{1,0},{2,1},{3,2},{4,3},{5,4},{6,5},{7,6},{8,7},{9,8},{10,9},{11,1... | collective-permute-start | bytes 811016 | tf_op jit(solution)/shard_map/ppermute | solution.py:20
  77.4 1.9 copy-start.11
  77.4 2.0 copy-start.12
  77.4 2.0 copy-start.13
  77.4 2.0 copy-start.14
  77.4 1.9 copy-start.15
  77.4 1.9 copy-start.16
  77.4 1.9 copy-start.17
  77.4 1.9 copy-start.18
  77.4 1.9 copy-start.19
  77.4 1.9 copy-start.20
  77.5 1.9 copy-start.21
  77.5 1.9 copy-start.22
  77.5 1.9 copy-start.23
  77.5 1.9 copy-start.24
  77.5 1.9 copy-start.25
  77.5 1.9 copy-start.26
  77.6 245.0 %reduce-scatter.2.cloned.1.call-start = ((), (), s32[]{:S(2)}) async-start(), calls=%async_computation.1 | async-start | bytes 2297856 | tf_op jit(solution)/shard_map/reduce_scatter | solution.py:120
  79.5 8.1 %copy-start.5 = (bf16[256,1408]{1,0:T(8,128)(2,1)S(1)}, bf16[256,1408]{1,0:T(8,128)(2,1)}, u32[]{:S(2)}) copy-start(bf16[256,1408]{1,0:T(8,128)(2,1)} %copy-done.4) | copy-start | bytes 2162692
  89.8 4.1 %copy-start.32 = (f32[704]{0:T(1024)S(1)}, f32[704]{0:T(1024)}, u32[]{:S(2)}) copy-start(f32[704]{0:T(1024)} %get-tuple-element.82) | copy-start | bytes 8452
  89.8 4.1 %copy-start.34 = (f32[64]{0:T(128)S(1)}, f32[64]{0:T(128)}, u32[]{:S(2)}) copy-start(f32[64]{0:T(128)} %copy-done.33) | copy-start | bytes 772
  89.9 4.0 %copy-start.35 = (f32[704]{0:T(1024)S(1)}, f32[704]{0:T(1024)}, u32[]{:S(2)}) copy-start(f32[704]{0:T(1024)} %param.14) | copy-start | bytes 8452
  93.9 138.6 %copy-start.3 = (bf16[4,64,704]{2,1,0:T(8,128)(2,1)S(1)}, bf16[4,64,704]{2,1,0:T(8,128)(2,1)}, u32[]{:S(2)}) copy-start(bf16[4,64,704]{2,1,0:T(8,128)(2,1)} %copy-done.2) | copy-start | bytes 1081348
  (11 other events, 18.8 us)
Sparse Core Ops, SparseCore 0:
  77.7 153.2 all-reduce.4
  233.7 88.8 reduce-scatter.1
where the time goes:
time: 332 us; the launch traced here: 331 us
  waiting for transfers between devices  173 us (52%)
  local copies, waits for them, and re-layouts  51.8 us (16%)
  blocking collectives  42.6 us (13%)
  other arithmetic  30.9 us (9%)
  between operations  14.8 us (4%)
  starting transfers between devices  10.6 us (3%)
  matrix products  6.95 us (2%)
    psum x1, waiting for transfers between devices, body(): lax.psum(kernel_term.astype(jnp.bfloat16), 'rows').astype(jnp.float32)  130 us
    psum x1, blocking collectives, body(): lax.psum(gain_term.astype(jnp.bfloat16), 'rows').astype(jnp.float32)  42.6 us
    reduce_scatter x1, waiting for transfers between devices, body(): lax.psum_scatter((product * scale).astype(jnp.bfloat16), 'rows', scatter_...  35.6 us
    another operation x50, local copies, waits for them, and re-layouts, body(): kernel_term = jnp.stack(kernel_terms) * scale  34 us
    ppermute x2, starting transfers between devices, with_halo(): before = lax.ppermute(last, axis, up)  7.8 us
    reduce_sum x1, other arithmetic, body(): bias_term = jnp.sum(pre_cot.astype(jnp.float32), axis=0) * scale  7.37 us
    convert_element_type x1, other arithmetic, body(): features = (reduce_step.astype(jnp.float32) + depth).astype(jnp.bfloat16)  6.73 us
  transfers between devices with their start and end apart: 6, of which 4 were waited for; matrix products, arithmetic and copies ran while one was open for 22% of the time, Pallas kernels for 0%

commit v1 on v0

v1 whole, which is shorter than its diff:
```python
import math

import jax
import jax.numpy as jnp
from jax import lax
from jax.experimental import pallas as pl
from jax.experimental.pallas import tpu as pltpu
from jax.sharding import PartitionSpec as P

KS = 7
PATCH = 4
LANES = 128
F32 = jnp.float32
BF16 = jnp.bfloat16
VM = pl.BlockSpec(memory_space=pltpu.VMEM)
SM = pl.BlockSpec(memory_space=pltpu.SMEM)


def tiles_of(chans):
    return [(t, min(LANES, chans - t * LANES)) for t in range(-(-chans // LANES))]


def column_mask(vis_ref, width):
    row = lax.broadcasted_iota(jnp.int32, (width, LANES), 0) // PATCH
    mask = jnp.zeros((width, LANES), F32)
    for k in range(width // PATCH):
        mask = jnp.where(row == k, vis_ref[0, k].astype(F32), mask)
    return mask


def call(kernel, out_shape, in_specs, scratch, flops, size, name):
    return pl.pallas_call(
        kernel,
        out_shape=out_shape,
        in_specs=in_specs,
        out_specs=jax.tree.map(lambda _: VM, out_shape),
        scratch_shapes=scratch,
        compiler_params=pltpu.CompilerParams(vmem_limit_bytes=48 * 2**20),
        cost_estimate=pl.CostEstimate(flops=flops, bytes_accessed=size, transcendentals=0),
        name=name,
    )


def edge_kernel(vis, cot, first, last):
    height, width, chans = cot.shape
    mask = column_mask(vis, width)
    for t, wd in tiles_of(chans):
        lanes = slice(t * LANES, t * LANES + wd)
        for p in range(height):
            row = (cot[p, :, lanes].astype(F32) * mask[:, :wd]).astype(BF16)
            if p < 3:
                first[p, :, lanes] = row
            if p >= height - 3:
                last[p - (height - 3), :, lanes] = row


def reduce_kernel(vis, image, gain, weight, bias, patches, normed, rstd, down, first, last, spread):
    rows, cols, chans = image.shape
    height, width = rows // 2, cols // 2
    mask = column_mask(vis, width)
    wide = tiles_of(chans)
    for r in range(rows):
        p, a = r // 2, r % 2
        x = image[r].astype(F32)
        center = jnp.sum(x, axis=-1, keepdims=True) * (1.0 / chans)
        x = x - center
        var = jnp.sum(x * x, axis=-1, keepdims=True) * (1.0 / chans)
        inv = 1.0 / jnp.sqrt(var + 1e-06)
        x = x * inv
        for t, wd in wide:
            spread[r, t, :, 0:wd] = x[:, t * LANES : t * LANES + wd]
        spread[r, len(wide)] = jnp.broadcast_to(inv, (cols, LANES))
        for b in range(2):
            at = pl.ds(p * width, width)
            for t, wd in wide:
                lanes = slice(t * LANES, t * LANES + wd)
                part = spread[r, t, pl.ds(b, width, stride=2), :][:, :wd]
                normed[2 * a + b, at, lanes] = part.astype(BF16)
                patches[2 * a + b, at, lanes] = (part * gain[:, lanes]).astype(BF16)
            rstd[2 * a + b, at, :] = spread[r, len(wide), pl.ds(b, width, stride=2), :]
    acc = jnp.zeros((height * width, weight.shape[1]), F32)
    for k in range(4):
        acc = acc + jnp.dot(
            patches[k], weight[k * chans : (k + 1) * chans, :], preferred_element_type=F32
        )
    acc = acc + bias[...]
    for t, wd in tiles_of(weight.shape[1]):
        lanes = slice(t * LANES, t * LANES + wd)
        for p in range(height):
            row = (acc[p * width : (p + 1) * width, lanes] * mask[:, :wd]).astype(BF16)
            down[p, :, lanes] = row
            if p < 3:
                first[p, :, lanes] = row
            if p >= height - 3:
                last[p - (height - 3), :, lanes] = row


def fill_band(dst, before, own, after, scale):
    count, width, chans = own.shape
    parts = [(before, k) for k in range(3)] + [(own, k) for k in range(count)]
    parts += [(after, k) for k in range(3)]
    tiles = tiles_of(chans)
    edge = jnp.zeros((len(tiles), len(parts), 8, LANES), F32)
    dst[:, :, 0:8, :] = edge
    dst[:, :, 8 + width : 16 + width, :] = edge
    for t, wd in tiles:
        if wd < LANES:
            dst[t, :, 8 : 8 + width, wd:LANES] = jnp.zeros((len(parts), width, LANES - wd), F32)
        for k, (ref, at) in enumerate(parts):
            value = ref[at, :, t * LANES : t * LANES + wd].astype(F32)
            if scale is not None and ref is own:
                value = value * scale[:, :wd]
            dst[t, k, 8 : 8 + width, 0:wd] = value


def fill_taps(dst, kernel):
    taps, chans = kernel.shape
    for t, wd in tiles_of(chans):
        dst[t, :, :, 0:wd] = jnp.broadcast_to(
            kernel[:, t * LANES : t * LANES + wd][:, None, :], (taps, 8, wd)
        )
        if wd < LANES:
            dst[t, :, :, wd:LANES] = jnp.zeros((taps, 8, LANES - wd), F32)


def back_kernel(place, vis, cot, before, after, kernel, patches, pre, *rest):
    chunks, (band, taps, mask_s, total, prod) = rest[:4], rest[4:]
    height, width, chans = cot.shape
    mask = column_mask(vis, width)
    mask_s[...] = mask
    fill_band(band, before, cot, after, mask)
    fill_taps(taps, kernel)
    half = width // 2
    groups = half // 8

    def step(u, carry):
        t, h = u // 2, (u % 2) * half
        acc = [jnp.zeros((groups, 8, LANES), F32) for _ in range(height)]
        for s in range(height + 6):
            for j in range(KS):
                value = band[t, s, pl.ds(h + 5 + j, half), :].reshape(groups, 8, LANES)
                for p in range(height):
                    i = s - p
                    if 0 <= i < KS:
                        acc[p] = acc[p] + value * taps[t, 48 - (KS * i + j)][None]
        here = pl.ds(pl.multiple_of(h, 8), half)
        keep = mask_s[here, :]
        lanes = pl.ds(pl.multiple_of(t * LANES, LANES), LANES)
        for p in range(height):
            own = band[t, 3 + p, pl.ds(pl.multiple_of(h + 8, 8), half), :]
            value = own + keep * acc[p].reshape(half, LANES)
            total[pl.ds(pl.multiple_of(p * width + h, 8), half), lanes] = value
        return carry

    lax.fori_loop(0, 2 * len(tiles_of(chans)), step, 0)
    pre[...] = total[:, :chans].astype(BF16)
    scale = 1.0 / math.sqrt(height * 16 * width)
    share = patches.shape[2] // 4
    for k in range(4):
        prod[...] = (
            lax.dot_general(
                patches[k], pre[...], (((0,), (0,)), ((), ())), preferred_element_type=F32
            )
            * scale
        )
        for d in range(4):
            to = lax.rem(place[0] + d, 4)
            at = pl.ds(pl.multiple_of(to * share, 8), share)
            chunks[d][k] = prod[at, :].astype(BF16)


def front_kernel(vis, down, before, after, kernel, bias, cot, features, grads, band, taps, cots, outs, kg):
    height, width, chans = cot.shape
    mask = column_mask(vis, width)
    fill_band(band, before, down, after, None)
    fill_taps(taps, kernel)
    for t, wd in tiles_of(chans):
        if wd < LANES:
            cots[t, :, :, wd:LANES] = jnp.zeros((height, width, LANES - wd), F32)
        for p in range(height):
            value = cot[p, :, t * LANES : t * LANES + wd].astype(F32)
            cots[t, p, :, 0:wd] = value * mask[:, :wd]
    half = width // 2
    groups = half // 8

    def step(u, carry):
        t, h = u // 2, (u % 2) * half
        here = pl.ds(pl.multiple_of(h, 8), half)
        acc = [jnp.zeros((groups, 8, LANES), F32) for _ in range(height)]
        mine = [cots[t, p, here, :].reshape(groups, 8, LANES) for p in range(height)]
        for j in range(KS):
            part = [jnp.zeros((8, LANES), F32) for _ in range(KS)]
            for s in range(height + 6):
                value = band[t, s, pl.ds(h + 5 + j, half), :].reshape(groups, 8, LANES)
                for p in range(height):
                    i = s - p
                    if 0 <= i < KS:
                        acc[p] = acc[p] + value * taps[t, KS * i + j][None]
                        part[i] = part[i] + jnp.sum(value * mine[p], axis=0)
            for i in range(KS):
                kg[u, KS * i + j] = part[i]
        kg[u, KS * KS] = sum(jnp.sum(m, axis=0) for m in mine)
        for p in range(height):
            outs[t, p, here, :] = acc[p].reshape(half, LANES)
        return carry

    tiles = tiles_of(chans)
    lax.fori_loop(0, 2 * len(tiles), step, 0)
    scale = 1.0 / math.sqrt(height * 16 * width)
    for t, wd in tiles:
        lanes = slice(t * LANES, t * LANES + wd)
        for p in range(height):
            value = (outs[t, p, :, 0:wd] + bias[:, lanes]) * mask[:, :wd]
            own = band[t, 3 + p, 8 : 8 + width, 0:wd]
            features[p, :, lanes] = (own + value).astype(BF16)
        term = jnp.sum(kg[2 * t] + kg[2 * t + 1], axis=1) * scale
        grads[0 : KS * KS + 1, lanes] = term[:, :wd]


def image_kernel(pre, weight, normed, rstd, gain, grads, image_grad, small, spread, sums):
    rows, cols, chans = image_grad.shape
    height, width = rows // 2, cols // 2
    wide = tiles_of(chans)
    scale = 1.0 / math.sqrt(height * 16 * width)
    gain_sum = jnp.zeros((1, chans), F32)
    for k in range(4):
        a, b = k // 2, k % 2
        flat = lax.dot_general(
            pre[...],
            weight[k * chans : (k + 1) * chans, :],
            (((1,), (1,)), ((), ())),
            preferred_element_type=F32,
        )
        norm = normed[k].astype(F32)
        gain_sum = gain_sum + jnp.sum(norm * flat, axis=0, keepdims=True)
        g = flat * gain[...]
        mean_g = jnp.sum(g, axis=-1, keepdims=True) * (1.0 / chans)
        mean_n = jnp.sum(g * norm, axis=-1, keepdims=True) * (1.0 / chans)
        g = g - mean_g - norm * mean_n
        for t, wd in wide:
            part = g[:, t * LANES : t * LANES + wd] * rstd[k][:, :wd]
            for p in range(height):
                spread[2 * p + a, t, pl.ds(b, width, stride=2), 0:wd] = part[
                    p * width : (p + 1) * width
                ]
    for r in range(rows):
        for t, wd in wide:
            image_grad[r, :, t * LANES : t * LANES + wd] = spread[r, t, :, 0:wd].astype(BF16)
    bias_sum = jnp.sum(pre[...].astype(F32), axis=0, keepdims=True)
    taps = KS * KS + 1
    sums[...] = jnp.zeros(sums.shape, F32)
    sums[0:taps, :] = grads[0:taps, :]
    sums[taps : taps + 1, :] = bias_sum * scale
    sums[taps + 1 : taps + 2, 0:chans] = gain_sum * scale
    small[...] = sums[...].astype(BF16)


def sd(shape, dtype):
    return jax.ShapeDtypeStruct(shape, dtype)


def sum_four(own, one, two, three):
    return (own.astype(F32) + two.astype(F32)) + (one.astype(F32) + three.astype(F32))


def body(image, visible, layer_norm_gain, reducer_weight, reducer_bias, depth_kernel, depth_bias, cotangent):
    height, width, chans = cotangent.shape
    rows, cols, in_chans = image.shape
    pixels = height * width
    bands = lax.axis_size("rows")
    index = lax.axis_index("rows")
    place_y, place_z = index % 4, index // 4
    up = [(i, i + 1) for i in range(bands - 1)]
    down_perm = [(j, i) for i, j in up]
    along_y = [[(4 * z + y, 4 * z + (y + k) % 4) for z in range(4) for y in range(4)] for k in range(4)]
    along_z = [[(4 * z + y, 4 * ((z + k) % 4) + y) for z in range(4) for y in range(4)] for k in range(4)]
    tiles = len(tiles_of(chans))
    in_tiles = len(tiles_of(in_chans))
    halo = sd((3, width, chans), BF16)
    macs = pixels * chans * 4 * in_chans
    taps = pixels * chans * KS * KS
    gain = layer_norm_gain.reshape(1, in_chans)

    cot_first, cot_last = call(
        edge_kernel, (halo, halo), [SM, VM], [], pixels * chans, 10**6, "edge"
    )(visible, cotangent)
    cot_before = lax.ppermute(cot_last, "rows", up)
    cot_after = lax.ppermute(cot_first, "rows", down_perm)

    patches, normed, rstd, down, first, last = call(
        reduce_kernel,
        (
            sd((4, pixels, in_chans), BF16),
            sd((4, pixels, in_chans), BF16),
            sd((4, pixels, LANES), F32),
            sd((height, width, chans), BF16),
            halo,
            halo,
        ),
        [SM, VM, VM, VM, VM],
        [pltpu.VMEM((rows, in_tiles + 1, cols, LANES), F32)],
        2 * macs,
        8 * 10**6,
        "reduce",
    )(visible, image, gain, reducer_weight, reducer_bias.reshape(1, chans))
    down_before = lax.ppermute(last, "rows", up)
    down_after = lax.ppermute(first, "rows", down_perm)

    share = in_chans // 4
    band = pltpu.VMEM((tiles, height + 6, width + 16, LANES), F32)
    taps_s = pltpu.VMEM((tiles, KS * KS, 8, LANES), F32)
    pre, *chunks = call(
        back_kernel,
        (sd((pixels, chans), BF16),) + (sd((4, share, chans), BF16),) * 4,
        [SM, SM, VM, VM, VM, VM, VM],
        [
            band,
            taps_s,
            pltpu.VMEM((width, LANES), F32),
            pltpu.VMEM((pixels, tiles * LANES), F32),
            pltpu.VMEM((in_chans, chans), F32),
        ],
        2 * macs + 40 * taps,
        6 * 10**6,
        "back",
    )(place_y.reshape(1).astype(jnp.int32), visible, cotangent, cot_before, cot_after, depth_kernel, patches)

    got = [lax.ppermute(chunks[k], "rows", along_y[k]) for k in (1, 2, 3)]

    features, grads = call(
        front_kernel,
        (sd((height, width, chans), BF16), sd((56, chans), F32)),
        [SM, VM, VM, VM, VM, VM, VM],
        [
            band,
            taps_s,
            pltpu.VMEM((tiles, height, width, LANES), F32),
            pltpu.VMEM((tiles, height, width, LANES), F32),
            pltpu.VMEM((2 * tiles, KS * KS + 1, 8, LANES), F32),
        ],
        80 * taps,
        6 * 10**6,
        "front",
    )(visible, down, down_before, down_after, depth_kernel, depth_bias.reshape(1, chans), cotangent)

    image_grad, small = call(
        image_kernel,
        (sd((rows, cols, in_chans), BF16), sd((64, chans), BF16)),
        [VM] * 6,
        [pltpu.VMEM((rows, in_tiles, cols, LANES), F32), pltpu.VMEM((64, chans), F32)],
        2 * macs,
        8 * 10**6,
        "image",
    )(pre, reducer_weight, normed, rstd, gain, grads)

    tiny = [lax.ppermute(small, "rows", along_y[k]) for k in (1, 2, 3)]
    small = sum_four(small, *tiny).astype(BF16)

    half = sum_four(chunks[0], *got).astype(BF16)
    parts = [lax.dynamic_index_in_dim(half, (place_z + k) % 4, 0, False) for k in range(4)]
    got = [lax.ppermute(parts[k], "rows", along_z[k]) for k in (1, 2, 3)]
    tiny = [lax.ppermute(small, "rows", along_z[k]) for k in (1, 2, 3)]
    down_weight_grad = sum_four(parts[0], *got)
    small = sum_four(small, *tiny)
    n = KS * KS
    return (
        features,
        image_grad,
        down_weight_grad,
        small[n + 2, :in_chans],
        small[n + 1],
        small[:n],
        small[n],
    )


def solution(mesh):
    placed = (
        P(("group", "rows"), None, None),
        P(("group", "rows"), None),
        P(),
        P(),
        P(),
        P(),
        P(),
        P(("group", "rows"), None, None),
    )
    return jax.shard_map(
        body,
        mesh=mesh,
        in_specs=placed,
        out_specs=(
            P(("group", "rows"), None, None),
            P(("group", "rows"), None, None),
            P(("group", "rows"), None),
            P("group"),
            P("group"),
            P("group", None),
            P("group"),
        ),
        check_vma=False,
    )
```

time: 332 us -> 97.6 us (0.29)
  waiting for transfers between devices: 173 us -> 21.2 us
  blocking collectives: 42.6 us -> 0 us
  local copies, waits for them, and re-layouts: 51.8 us -> 17.3 us
  other arithmetic: 30.9 us -> 1.14 us
  starting transfers between devices: 10.6 us -> 36.1 us
  Pallas kernels: 0 us -> 19.6 us
  between operations: 14.8 us -> 0.87 us
  matrix products: 6.95 us -> 0 us
    psum x1 -> x0, waiting for transfers between devices: 130 us -> none  [body(): lax.psum(kernel_term.astype(jnp.bfloat16), 'rows').astype(jnp.float32)]
    psum x1 -> x0, blocking collectives: 42.6 us -> none  [body(): lax.psum(gain_term.astype(jnp.bfloat16), 'rows').astype(jnp.float32)]
    reduce_scatter x1 -> x0, waiting for transfers between devices: 35.6 us -> none  [body(): lax.psum_scatter((product * scale).astype(jnp.bfloat16), 'rows', scatter_...]
    another operation x50 -> x0, local copies, waits for them, and re-layouts: 34 us -> none  [body(): kernel_term = jnp.stack(kernel_terms) * scale]
    ppermute x4 -> x16, starting transfers between devices: 10.4 us -> 36.1 us  [the longest x3 6.76 us: body(): got = [lax.ppermute(chunks[k], 'rows', along_y[k]) for k in (1, 2, 3)]]
    pallas_call x0 -> x5, Pallas kernels: none -> 19.6 us  [the longest x1 6.99 us: body(): call(front_kernel, (sd((height, width, chans), BF16), sd((56, chans), F32...]
    reduce_sum x8 -> x0, other arithmetic: 15 us -> none  [the longest x1 7.37 us: body(): bias_term = jnp.sum(pre_cot.astype(jnp.float32), axis=0) * scale]
    convert_element_type x14 -> x2, other arithmetic: 14.2 us -> 0.32 us  [the longest x1 0.27 us: body(): half = sum_four(chunks[0], *got).astype(BF16)]
  transfers between devices with their start and end apart: 6 -> 16, of which waited for: 4 -> 8; matrix products, arithmetic and copies ran while one was open for 22% -> 3% of each run, Pallas kernels for 0% -> 9%
where the time goes in v1:
time: 97.6 us; the launch traced here: 96.2 us
  starting transfers between devices  36.1 us (37%)
  waiting for transfers between devices  21.2 us (22%)
  Pallas kernels  19.6 us (20%)
  local copies, waits for them, and re-layouts  17.3 us (18%)
  other arithmetic  1.14 us (1%)
    unnamed x37, local copies, waits for them, and re-layouts  14 us
    ppermute x3, waiting for transfers between devices, body(): tiny = [lax.ppermute(small, 'rows', along_y[k]) for k in (1, 2, 3)]  10.6 us
    pallas_call x1, Pallas kernels, body(): call(front_kernel, (sd((height, width, chans), BF16), sd((56, chans), F32...  6.99 us
    pallas_call x1, Pallas kernels, body(): call(back_kernel, (sd((pixels, chans), BF16),) + (sd((4, share, chans), B...  6.89 us
    ppermute x3, starting transfers between devices, body(): got = [lax.ppermute(chunks[k], 'rows', along_y[k]) for k in (1, 2, 3)]  6.76 us
    ppermute x3, starting transfers between devices, body(): tiny = [lax.ppermute(small, 'rows', along_y[k]) for k in (1, 2, 3)]  6.74 us
    ppermute x3, starting transfers between devices, body(): tiny = [lax.ppermute(small, 'rows', along_z[k]) for k in (1, 2, 3)]  6.19 us
    ppermute x3, waiting for transfers between devices, body(): got = [lax.ppermute(parts[k], 'rows', along_z[k]) for k in (1, 2, 3)]  5.82 us
  transfers between devices with their start and end apart: 16, of which 8 were waited for; matrix products, arithmetic and copies ran while one was open for 3% of the time, Pallas kernels for 9%

profile of v1, /device:TPU:2, one launch (start us, length us, event | category | flops | bytes accessed | tf_op | source)
XLA Modules:
  0.0 96.2 jit_solution(8730780728359525215)
XLA Ops:
  2.0 1.5 %copy.15.image = bf16[8,128,352]{2,1,0:T(8,128)(2,1)S(1)} copy(bf16[8,128,352]{1,2,0:T(8,128)(2,1)} %param.8) | data formatting | bytes 1441792 | tf_op args[0]
  3.5 2.7 %copy.16.weight = bf16[1408,704]{1,0:T(8,128)(2,1)S(1)} copy(bf16[1408,704]{0,1:T(8,128)(2,1)} %param.11) | data formatting | bytes 3964928 | tf_op args[3]
  6.3 3.0 %reduce.7 = (bf16[4,256,352]{2,1,0:T(8,128)(2,1)S(1)}, bf16[4,256,352]{2,1,0:T(8,128)(2,1)S(1)}, f32[4,256,128]{2,1,0:T(8,128)S(1)}, bf16[4,64,704]{2,1,0:T(8,12...) custom-call(s32[1,16]{1,0:T(1,128)S(1)} %copy-done.6, bf16[8,128,352]{2,1,0:T(8,128)(2,1)S(1)} %copy.15.image, ...), custom_call_target="tpu_custom_call" | custom-call | flops 507510784 | bytes 8000000 | tf_op jit(solution)/shard_map/reduce/pallas_call | solution.py:290
  9.2 0.9 copy-done
  10.9 0.9 copy-done.7
  12.5 3.5 %collective-permute-start = (bf16[3,64,704]{2,1,0:T(8,128)(2,1)}, bf16[3,64,704]{2,1,0:T(8,128)(2,1)S(1)}, u32[]{:S(2)}, u32[]{:S(2)}) collective-permute-start(bf16[3,64,704]{2,1,0:T(8,128)(2,1)} %get-tuple-element.25), channel_id=1, source_target_pairs={{0,1},{1,2},{2,3},{3,4},{4,5},{5,6},{6,7},{7,8},{8,9},{9,10},{10,1... | collective-permute-start | bytes 811016 | tf_op jit(solution)/shard_map/ppermute | solution.py:306
  16.0 1.3 %collective-permute-start.1 = (bf16[3,64,704]{2,1,0:T(8,128)(2,1)}, bf16[3,64,704]{2,1,0:T(8,128)(2,1)S(1)}, u32[]{:S(2)}, u32[]{:S(2)}) collective-permute-start(bf16[3,64,704]{2,1,0:T(8,128)(2,1)} %get-tuple-element.26), channel_id=1, source_target_pairs={{1,0},{2,1},{3,2},{4,3},{5,4},{6,5},{7,6},{8,7},{9,8},{10,9},{11,1... | collective-permute-start | bytes 811016 | tf_op jit(solution)/shard_map/ppermute | solution.py:307
  17.3 1.5 %edge.1 = (bf16[3,64,704]{2,1,0:T(8,128)(2,1)}, bf16[3,64,704]{2,1,0:T(8,128)(2,1)}) custom-call(s32[1,16]{1,0:T(1,128)S(1)} %copy-done.6, bf16[4,64,704]{2,1,0:T(8,128)(2,1)S(1)} %copy-done.4), custom_call_target="tpu_custom_call" | custom-call | flops 180224 | bytes 1000000 | tf_op jit(solution)/shard_map/edge/pallas_call | solution.py:284
  18.8 5.3 %collective-permute-start.2 = (bf16[3,64,704]{2,1,0:T(8,128)(2,1)}, bf16[3,64,704]{2,1,0:T(8,128)(2,1)}, u32[]{:S(2)}, u32[]{:S(2)}) collective-permute-start(bf16[3,64,704]{2,1,0:T(8,128)(2,1)} %get-tuple-element.28), channel_id=1, source_target_pairs={{0,1},{1,2},{2,3},{3,4},{4,5},{5,6},{6,7},{7,8},{8,9},{9,10},{10,1... | collective-permute-start | bytes 811016 | tf_op jit(solution)/shard_map/ppermute | solution.py:287
  24.1 1.3 %collective-permute-start.3 = (bf16[3,64,704]{2,1,0:T(8,128)(2,1)}, bf16[3,64,704]{2,1,0:T(8,128)(2,1)}, u32[]{:S(2)}, u32[]{:S(2)}) collective-permute-start(bf16[3,64,704]{2,1,0:T(8,128)(2,1)} %get-tuple-element.29), channel_id=1, source_target_pairs={{1,0},{2,1},{3,2},{4,3},{5,4},{6,5},{7,6},{8,7},{9,8},{10,9},{11,1... | collective-permute-start | bytes 811016 | tf_op jit(solution)/shard_map/ppermute | solution.py:288
  27.3 1.0 %copy-done.10 = bf16[4,64,704]{2,1,0:T(8,128)(2,1)S(1)} copy-done((bf16[4,64,704]{2,1,0:T(8,128)(2,1)S(1)}, bf16[4,64,704]{2,1,0:T(8,128)(2,1)}, u32[]{:S(2)}) %copy-start.10) | copy-done | bytes 360472
  28.3 1.0 copy-done.12
  29.3 1.0 copy-done.14
  30.2 0.9 copy-done.15
  31.2 7.0 %front.1 = (bf16[4,64,704]{2,1,0:T(8,128)(2,1)}, f32[56,704]{1,0:T(8,128)S(1)}) custom-call(s32[1,16]{1,0:T(1,128)S(1)} %copy-done.6, bf16[4,64,704]{2,1,0:T(8,128)(2,1)S(1)} %copy-done.10, bf16[3,64,704]{2,1,0:T(8,128)(2,1)S(1)} %copy-done.12, bf16[3,64,704]{2,1,0:T(8,128)(2,1)S(1)} %copy-done.14, f32[49,704]{1,0:T(8,128)S(1)} %copy-done.15, ...), custom_call_target="tpu_custom_call" | custom-call | flops 706478080 | bytes 6000000 | tf_op jit(solution)/shard_map/front/pallas_call | solution.py:330
  38.2 6.9 %back.1 = (bf16[256,704]{1,0:T(8,128)(2,1)S(1)}, bf16[4,88,704]{2,1,0:T(8,128)(2,1)S(1)}, bf16[4,88,704]{2,1,0:T(8,128)(2,1)}, bf16[4,88,704]{2,1,0:T(8,128)(2,1)}, bf16[4,88,704]{2,1,0:T(8,128)(2,1)}) custom-call(s32[1]{0:T(128)} %bitcast.place, s32[1,16]{1,0:T(1,128)S(1)} %copy-done.6, bf16[4,64,704]{2,1,0:T(8,128)(2,1)S(1)} %copy-done.5, ...), custom_call_target="tpu_custom_call" | custom-call | flops 860749824 | bytes 6000000 | tf_op jit(solution)/shard_map/back/pallas_call | solution.py:312
  45.1 1.3 %image.2 = (bf16[8,128,352]{2,1,0:T(8,128)(2,1)S(1)}, bf16[64,704]{1,0:T(8,128)(2,1)S(1)}) custom-call(bf16[256,704]{1,0:T(8,128)(2,1)S(1)} %get-tuple-element.31.pre, bf16[1408,704]{1,0:T(8,128)(2,1)S(1)} %copy.16.weight, bf16[4,256,352]{2,1,0:T(8,128)(2,1)S(1)} %copy-done.1, f32[4,256,128]{2,1,0:T(8,128)S(1)} %copy-done.3, f32[1,352]{1,0:T(1,128)S(1)} %reshape.28.gain, ...), custom_call_target="tpu_custom_call" | custom-call | flops 507510784 | bytes 8000000 | tf_op jit(solution)/shard_map/image/pallas_call | solution.py:346
  46.4 5.2 %collective-permute-start.12 = (bf16[64,704]{1,0:T(8,128)(2,1)S(1)}, bf16[64,704]{1,0:T(8,128)(2,1)S(1)}, u32[]{:S(2)}, u32[]{:S(2)}) collective-permute-start(bf16[64,704]{1,0:T(8,128)(2,1)S(1)} %get-tuple-element.40), channel_id=1, source_target_pairs={{0,3},{1,0},{2,1},{3,2},{4,7},{5,4},{6,5},{7,6},{8,11},{9,8},{10,9... | collective-permute-start | bytes 270344 | tf_op jit(solution)/shard_map/ppermute | solution.py:356
  51.6 1.6 %collective-permute-start.10 = (bf16[64,704]{1,0:T(8,128)(2,1)S(1)}, bf16[64,704]{1,0:T(8,128)(2,1)S(1)}, u32[]{:S(2)}, u32[]{:S(2)}) collective-permute-start(bf16[64,704]{1,0:T(8,128)(2,1)S(1)} %get-tuple-element.40), channel_id=1, source_target_pairs={{0,2},{1,3},{2,0},{3,1},{4,6},{5,7},{6,4},{7,5},{8,10},{9,11},{10,... | collective-permute-start | bytes 270344 | tf_op jit(solution)/shard_map/ppermute | solution.py:356
  53.2 2.0 %collective-permute-start.4 = (bf16[4,88,704]{2,1,0:T(8,128)(2,1)}, bf16[4,88,704]{2,1,0:T(8,128)(2,1)S(1)}, u32[]{:S(2)}, u32[]{:S(2)}) collective-permute-start(bf16[4,88,704]{2,1,0:T(8,128)(2,1)} %get-tuple-element.37), channel_id=1, source_target_pairs={{0,2},{1,3},{2,0},{3,1},{4,6},{5,7},{6,4},{7,5},{8,10},{9,11},{10,... | collective-permute-start | bytes 1486856 | tf_op jit(solution)/shard_map/ppermute | solution.py:328
  55.7 9.1 %collective-permute-done.12 = bf16[64,704]{1,0:T(8,128)(2,1)S(1)} collective-permute-done((bf16[64,704]{1,0:T(8,128)(2,1)S(1)}, bf16[64,704]{1,0:T(8,128)(2,1)S(1)}, u32[]{:S(2)}, u32[]{:S(2)}) %collective-permute-start.12) | collective-permute-done | bytes 90144 | tf_op jit(solution)/shard_map/ppermute | solution.py:356
  64.9 4.2 %collective-permute-start.6 = (bf16[4,88,704]{2,1,0:T(8,128)(2,1)}, bf16[4,88,704]{2,1,0:T(8,128)(2,1)S(1)}, u32[]{:S(2)}, u32[]{:S(2)}) collective-permute-start(bf16[4,88,704]{2,1,0:T(8,128)(2,1)} %get-tuple-element.39), channel_id=1, source_target_pairs={{0,3},{1,0},{2,1},{3,2},{4,7},{5,4},{6,5},{7,6},{8,11},{9,8},{10,9... | collective-permute-start | bytes 1486856 | tf_op jit(solution)/shard_map/ppermute | solution.py:328
  69.1 1.5 %collective-permute-done.11 = bf16[64,704]{1,0:T(8,128)(2,1)S(1)} collective-permute-done((bf16[64,704]{1,0:T(8,128)(2,1)S(1)}, bf16[64,704]{1,0:T(8,128)(2,1)S(1)}, u32[]{:S(2)}, u32[]{:S(2)}) %collective-permute-start.11) | collective-permute-done | bytes 90144 | tf_op jit(solution)/shard_map/ppermute | solution.py:356
  70.6 3.9 %collective-permute-start.15 = (bf16[64,704]{1,0:T(8,128)(2,1)S(1)}, bf16[64,704]{1,0:T(8,128)(2,1)S(1)}, u32[]{:S(2)}, u32[]{:S(2)}) collective-permute-start(bf16[64,704]{1,0:T(8,128)(2,1)S(1)} %add_convert_fusion.1), channel_id=1, source_target_pairs={{0,12},{1,13},{2,14},{3,15},{4,0},{5,1},{6,2},{7,3},{8,4},{9,5},{1... | collective-permute-start | bytes 270344 | tf_op jit(solution)/shard_map/ppermute | solution.py:362
  74.5 2.2 %collective-permute-done.15 = bf16[64,704]{1,0:T(8,128)(2,1)S(1)} collective-permute-done((bf16[64,704]{1,0:T(8,128)(2,1)S(1)}, bf16[64,704]{1,0:T(8,128)(2,1)S(1)}, u32[]{:S(2)}, u32[]{:S(2)}) %collective-permute-start.15) | collective-permute-done | bytes 90144 | tf_op jit(solution)/shard_map/ppermute | solution.py:362
  76.7 2.3 %collective-permute-start.13 = (bf16[64,704]{1,0:T(8,128)(2,1)S(1)}, bf16[64,704]{1,0:T(8,128)(2,1)S(1)}, u32[]{:S(2)}, u32[]{:S(2)}) collective-permute-start(bf16[64,704]{1,0:T(8,128)(2,1)S(1)} %add_convert_fusion.1), channel_id=1, source_target_pairs={{0,8},{1,9},{2,10},{3,11},{4,12},{5,13},{6,14},{7,15},{8,0},{9,1},... | collective-permute-start | bytes 270344 | tf_op jit(solution)/shard_map/ppermute | solution.py:362
  79.0 1.1 %copy.18 = bf16[8,128,352]{1,2,0:T(8,128)(2,1)} copy(bf16[8,128,352]{2,1,0:T(8,128)(2,1)S(1)} %get-tuple-element.42) | data formatting | bytes 1441792
  80.9 1.3 %collective-permute-done.13 = bf16[64,704]{1,0:T(8,128)(2,1)S(1)} collective-permute-done((bf16[64,704]{1,0:T(8,128)(2,1)S(1)}, bf16[64,704]{1,0:T(8,128)(2,1)S(1)}, u32[]{:S(2)}, u32[]{:S(2)}) %collective-permute-start.13) | collective-permute-done | bytes 90144 | tf_op jit(solution)/shard_map/ppermute | solution.py:362
  82.6 3.0 %collective-permute-start.7 = (bf16[88,704]{1,0:T(8,128)(2,1)S(1)}, bf16[88,704]{1,0:T(8,128)(2,1)S(1)}, u32[]{:S(2)}, u32[]{:S(2)}) collective-permute-start(bf16[88,704]{1,0:T(8,128)(2,1)S(1)} %get-tuple-element.50), channel_id=1, source_target_pairs={{0,8},{1,9},{2,10},{3,11},{4,12},{5,13},{6,14},{7,15},{8,0},{9,1},... | collective-permute-start | bytes 371720 | tf_op jit(solution)/shard_map/ppermute | solution.py:361
  85.6 1.5 %collective-permute-start.9 = (bf16[88,704]{1,0:T(8,128)(2,1)S(1)}, bf16[88,704]{1,0:T(8,128)(2,1)S(1)}, u32[]{:S(2)}, u32[]{:S(2)}) collective-permute-start(bf16[88,704]{1,0:T(8,128)(2,1)S(1)} %get-tuple-element.51), channel_id=1, source_target_pairs={{0,12},{1,13},{2,14},{3,15},{4,0},{5,1},{6,2},{7,3},{8,4},{9,5},{1... | collective-permute-start | bytes 371720 | tf_op jit(solution)/shard_map/ppermute | solution.py:361
  89.6 4.3 %collective-permute-done.7 = bf16[88,704]{1,0:T(8,128)(2,1)S(1)} collective-permute-done((bf16[88,704]{1,0:T(8,128)(2,1)S(1)}, bf16[88,704]{1,0:T(8,128)(2,1)S(1)}, u32[]{:S(2)}, u32[]{:S(2)}) %collective-permute-start.7) | collective-permute-done | bytes 123936 | tf_op jit(solution)/shard_map/ppermute | solution.py:361
  93.9 1.5 %collective-permute-done.8 = bf16[88,704]{1,0:T(8,128)(2,1)S(1)} collective-permute-done((bf16[88,704]{1,0:T(8,128)(2,1)S(1)}, bf16[88,704]{1,0:T(8,128)(2,1)S(1)}, u32[]{:S(2)}, u32[]{:S(2)}) %collective-permute-start.8) | collective-permute-done | bytes 123936 | tf_op jit(solution)/shard_map/ppermute | solution.py:361
  (53 shorter events, 9.8 us)
Async XLA Ops:
  3.5 2.8 %copy-start.6 = (s32[1,16]{1,0:T(1,128)S(1)}, s32[1,16]{1,0:T(1,128)}, u32[]{:S(2)}) copy-start(s32[1,16]{1,0:T(1,128)} %vis.7) | copy-start | bytes 196
  6.2 11.1 %copy-start.4 = (bf16[4,64,704]{2,1,0:T(8,128)(2,1)S(1)}, bf16[4,64,704]{2,1,0:T(8,128)(2,1)}, u32[]{:S(2)}) copy-start(bf16[4,64,704]{2,1,0:T(8,128)(2,1)} %cot.5) | copy-start | bytes 1081348
  6.2 19.1 %copy-start.16 = (f32[704]{0:T(1024)S(1)}, f32[704]{0:T(1024)}, u32[]{:S(2)}) copy-start(f32[704]{0:T(1024)} %param.14) | copy-start | bytes 8452
  9.2 0.9 copy-start
  10.1 0.8 copy-start.2
  10.9 0.9 copy-start.7
  11.8 0.7 copy-start.9
  12.5 12.9 %collective-permute-start = (bf16[3,64,704]{2,1,0:T(8,128)(2,1)}, bf16[3,64,704]{2,1,0:T(8,128)(2,1)S(1)}, u32[]{:S(2)}, u32[]{:S(2)}) collective-permute-start(bf16[3,64,704]{2,1,0:T(8,128)(2,1)} %get-tuple-element.25), channel_id=1, source_target_pairs={{0,1},{1,2},{2,3},{3,4},{4,5},{5,6},{6,7},{7,8},{8,9},{9,10},{10,1... | collective-permute-start | bytes 811016 | tf_op jit(solution)/shard_map/ppermute | solution.py:306
  16.0 10.6 %collective-permute-start.1 = (bf16[3,64,704]{2,1,0:T(8,128)(2,1)}, bf16[3,64,704]{2,1,0:T(8,128)(2,1)S(1)}, u32[]{:S(2)}, u32[]{:S(2)}) collective-permute-start(bf16[3,64,704]{2,1,0:T(8,128)(2,1)} %get-tuple-element.26), channel_id=1, source_target_pairs={{1,0},{2,1},{3,2},{4,3},{5,4},{6,5},{7,6},{8,7},{9,8},{10,9},{11,1... | collective-permute-start | bytes 811016 | tf_op jit(solution)/shard_map/ppermute | solution.py:307
  18.8 19.4 %collective-permute-start.2 = (bf16[3,64,704]{2,1,0:T(8,128)(2,1)}, bf16[3,64,704]{2,1,0:T(8,128)(2,1)}, u32[]{:S(2)}, u32[]{:S(2)}) collective-permute-start(bf16[3,64,704]{2,1,0:T(8,128)(2,1)} %get-tuple-element.28), channel_id=1, source_target_pairs={{0,1},{1,2},{2,3},{3,4},{4,5},{5,6},{6,7},{7,8},{8,9},{9,10},{10,1... | collective-permute-start | bytes 811016 | tf_op jit(solution)/shard_map/ppermute | solution.py:287
  24.1 14.1 %collective-permute-start.3 = (bf16[3,64,704]{2,1,0:T(8,128)(2,1)}, bf16[3,64,704]{2,1,0:T(8,128)(2,1)}, u32[]{:S(2)}, u32[]{:S(2)}) collective-permute-start(bf16[3,64,704]{2,1,0:T(8,128)(2,1)} %get-tuple-element.29), channel_id=1, source_target_pairs={{1,0},{2,1},{3,2},{4,3},{5,4},{6,5},{7,6},{8,7},{9,8},{10,9},{11,1... | collective-permute-start | bytes 811016 | tf_op jit(solution)/shard_map/ppermute | solution.py:288
  25.4 0.7 copy-start.11
  27.3 1.0 %copy-start.10 = (bf16[4,64,704]{2,1,0:T(8,128)(2,1)S(1)}, bf16[4,64,704]{2,1,0:T(8,128)(2,1)}, u32[]{:S(2)}) copy-start(bf16[4,64,704]{2,1,0:T(8,128)(2,1)} %copy-done.9) | copy-start | bytes 1081348
  28.3 1.0 copy-start.12
  29.3 1.0 copy-start.14
  30.2 0.9 copy-start.15
  31.2 7.0 %copy-start.5 = (bf16[4,64,704]{2,1,0:T(8,128)(2,1)S(1)}, bf16[4,64,704]{2,1,0:T(8,128)(2,1)}, u32[]{:S(2)}) copy-start(bf16[4,64,704]{2,1,0:T(8,128)(2,1)} %cot.5) | copy-start | bytes 1081348
  31.2 7.0 %copy-start.8 = (bf16[4,256,352]{2,1,0:T(8,128)(2,1)S(1)}, bf16[4,256,352]{2,1,0:T(8,128)(2,1)}, u32[]{:S(2)}) copy-start(bf16[4,256,352]{2,1,0:T(8,128)(2,1)} %copy-done.7) | copy-start | bytes 2162692
  38.2 6.9 %copy-start.1 = (bf16[4,256,352]{2,1,0:T(8,128)(2,1)S(1)}, bf16[4,256,352]{2,1,0:T(8,128)(2,1)}, u32[]{:S(2)}) copy-start(bf16[4,256,352]{2,1,0:T(8,128)(2,1)} %copy-done) | copy-start | bytes 2162692
  38.2 6.9 %copy-start.3 = (f32[4,256,128]{2,1,0:T(8,128)S(1)}, f32[4,256,128]{2,1,0:T(8,128)}, u32[]{:S(2)}) copy-start(f32[4,256,128]{2,1,0:T(8,128)} %copy-done.2) | copy-start | bytes 1572868
  46.4 18.4 %collective-permute-start.12 = (bf16[64,704]{1,0:T(8,128)(2,1)S(1)}, bf16[64,704]{1,0:T(8,128)(2,1)S(1)}, u32[]{:S(2)}, u32[]{:S(2)}) collective-permute-start(bf16[64,704]{1,0:T(8,128)(2,1)S(1)} %get-tuple-element.40), channel_id=1, source_target_pairs={{0,3},{1,0},{2,1},{3,2},{4,7},{5,4},{6,5},{7,6},{8,11},{9,8},{10,9... | collective-permute-start | bytes 270344 | tf_op jit(solution)/shard_map/ppermute | solution.py:356
  51.6 18.9 %collective-permute-start.11 = (bf16[64,704]{1,0:T(8,128)(2,1)S(1)}, bf16[64,704]{1,0:T(8,128)(2,1)S(1)}, u32[]{:S(2)}, u32[]{:S(2)}) collective-permute-start(bf16[64,704]{1,0:T(8,128)(2,1)S(1)} %get-tuple-element.40), channel_id=1, source_target_pairs={{0,1},{1,2},{2,3},{3,0},{4,5},{5,6},{6,7},{7,4},{8,9},{9,10},{10,1... | collective-permute-start | bytes 270344 | tf_op jit(solution)/shard_map/ppermute | solution.py:356
  51.6 18.9 %collective-permute-start.10 = (bf16[64,704]{1,0:T(8,128)(2,1)S(1)}, bf16[64,704]{1,0:T(8,128)(2,1)S(1)}, u32[]{:S(2)}, u32[]{:S(2)}) collective-permute-start(bf16[64,704]{1,0:T(8,128)(2,1)S(1)} %get-tuple-element.40), channel_id=1, source_target_pairs={{0,2},{1,3},{2,0},{3,1},{4,6},{5,7},{6,4},{7,5},{8,10},{9,11},{10,... | collective-permute-start | bytes 270344 | tf_op jit(solution)/shard_map/ppermute | solution.py:356
  53.2 29.1 %collective-permute-start.4 = (bf16[4,88,704]{2,1,0:T(8,128)(2,1)}, bf16[4,88,704]{2,1,0:T(8,128)(2,1)S(1)}, u32[]{:S(2)}, u32[]{:S(2)}) collective-permute-start(bf16[4,88,704]{2,1,0:T(8,128)(2,1)} %get-tuple-element.37), channel_id=1, source_target_pairs={{0,2},{1,3},{2,0},{3,1},{4,6},{5,7},{6,4},{7,5},{8,10},{9,11},{10,... | collective-permute-start | bytes 1486856 | tf_op jit(solution)/shard_map/ppermute | solution.py:328
  55.1 27.1 %collective-permute-start.5 = (bf16[4,88,704]{2,1,0:T(8,128)(2,1)}, bf16[4,88,704]{2,1,0:T(8,128)(2,1)S(1)}, u32[]{:S(2)}, u32[]{:S(2)}) collective-permute-start(bf16[4,88,704]{2,1,0:T(8,128)(2,1)} %get-tuple-element.38), channel_id=1, source_target_pairs={{0,1},{1,2},{2,3},{3,0},{4,5},{5,6},{6,7},{7,4},{8,9},{9,10},{10,1... | collective-permute-start | bytes 1486856 | tf_op jit(solution)/shard_map/ppermute | solution.py:328
  64.9 17.4 %collective-permute-start.6 = (bf16[4,88,704]{2,1,0:T(8,128)(2,1)}, bf16[4,88,704]{2,1,0:T(8,128)(2,1)S(1)}, u32[]{:S(2)}, u32[]{:S(2)}) collective-permute-start(bf16[4,88,704]{2,1,0:T(8,128)(2,1)} %get-tuple-element.39), channel_id=1, source_target_pairs={{0,3},{1,0},{2,1},{3,2},{4,7},{5,4},{6,5},{7,6},{8,11},{9,8},{10,9... | collective-permute-start | bytes 1486856 | tf_op jit(solution)/shard_map/ppermute | solution.py:328
  70.6 6.1 %collective-permute-start.15 = (bf16[64,704]{1,0:T(8,128)(2,1)S(1)}, bf16[64,704]{1,0:T(8,128)(2,1)S(1)}, u32[]{:S(2)}, u32[]{:S(2)}) collective-permute-start(bf16[64,704]{1,0:T(8,128)(2,1)S(1)} %add_convert_fusion.1), channel_id=1, source_target_pairs={{0,12},{1,13},{2,14},{3,15},{4,0},{5,1},{6,2},{7,3},{8,4},{9,5},{1... | collective-permute-start | bytes 270344 | tf_op jit(solution)/shard_map/ppermute | solution.py:362
  74.5 6.4 %collective-permute-start.14 = (bf16[64,704]{1,0:T(8,128)(2,1)S(1)}, bf16[64,704]{1,0:T(8,128)(2,1)S(1)}, u32[]{:S(2)}, u32[]{:S(2)}) collective-permute-start(bf16[64,704]{1,0:T(8,128)(2,1)S(1)} %add_convert_fusion.1), channel_id=1, source_target_pairs={{0,4},{1,5},{2,6},{3,7},{4,8},{5,9},{6,10},{7,11},{8,12},{9,13},{1... | collective-permute-start | bytes 270344 | tf_op jit(solution)/shard_map/ppermute | solution.py:362
  76.7 5.5 %collective-permute-start.13 = (bf16[64,704]{1,0:T(8,128)(2,1)S(1)}, bf16[64,704]{1,0:T(8,128)(2,1)S(1)}, u32[]{:S(2)}, u32[]{:S(2)}) collective-permute-start(bf16[64,704]{1,0:T(8,128)(2,1)S(1)} %add_convert_fusion.1), channel_id=1, source_target_pairs={{0,8},{1,9},{2,10},{3,11},{4,12},{5,13},{6,14},{7,15},{8,0},{9,1},... | collective-permute-start | bytes 270344 | tf_op jit(solution)/shard_map/ppermute | solution.py:362
  82.6 11.3 %collective-permute-start.7 = (bf16[88,704]{1,0:T(8,128)(2,1)S(1)}, bf16[88,704]{1,0:T(8,128)(2,1)S(1)}, u32[]{:S(2)}, u32[]{:S(2)}) collective-permute-start(bf16[88,704]{1,0:T(8,128)(2,1)S(1)} %get-tuple-element.50), channel_id=1, source_target_pairs={{0,8},{1,9},{2,10},{3,11},{4,12},{5,13},{6,14},{7,15},{8,0},{9,1},... | collective-permute-start | bytes 371720 | tf_op jit(solution)/shard_map/ppermute | solution.py:361
  85.6 8.3 %collective-permute-start.9 = (bf16[88,704]{1,0:T(8,128)(2,1)S(1)}, bf16[88,704]{1,0:T(8,128)(2,1)S(1)}, u32[]{:S(2)}, u32[]{:S(2)}) collective-permute-start(bf16[88,704]{1,0:T(8,128)(2,1)S(1)} %get-tuple-element.51), channel_id=1, source_target_pairs={{0,12},{1,13},{2,14},{3,15},{4,0},{5,1},{6,2},{7,3},{8,4},{9,5},{1... | collective-permute-start | bytes 371720 | tf_op jit(solution)/shard_map/ppermute | solution.py:361
  87.1 8.2 %collective-permute-start.8 = (bf16[88,704]{1,0:T(8,128)(2,1)S(1)}, bf16[88,704]{1,0:T(8,128)(2,1)S(1)}, u32[]{:S(2)}, u32[]{:S(2)}) collective-permute-start(bf16[88,704]{1,0:T(8,128)(2,1)S(1)} %get-tuple-element.52), channel_id=1, source_target_pairs={{0,4},{1,5},{2,6},{3,7},{4,8},{5,9},{6,10},{7,11},{8,12},{9,13},{1... | collective-permute-start | bytes 371720 | tf_op jit(solution)/shard_map/ppermute | solution.py:361
  (1 other events, 0.7 us)

commit v2 on v1

--- a/solution.py
+++ b/solution.py
@@ -14,6 +14,7 @@
 BF16 = jnp.bfloat16
 VM = pl.BlockSpec(memory_space=pltpu.VMEM)
 SM = pl.BlockSpec(memory_space=pltpu.SMEM)
+ANY = pl.BlockSpec(memory_space=pl.ANY)
 
 
 def tiles_of(chans):
@@ -35,7 +36,7 @@
         in_specs=in_specs,
         out_specs=jax.tree.map(lambda _: VM, out_shape),
         scratch_shapes=scratch,
-        compiler_params=pltpu.CompilerParams(vmem_limit_bytes=48 * 2**20),
+        compiler_params=pltpu.CompilerParams(vmem_limit_bytes=20 * 2**20),
         cost_estimate=pl.CostEstimate(flops=flops, bytes_accessed=size, transcendentals=0),
         name=name,
     )
@@ -54,37 +55,48 @@
                 last[p - (height - 3), :, lanes] = row
 
 
-def reduce_kernel(vis, image, gain, weight, bias, patches, normed, rstd, down, first, last, spread):
-    rows, cols, chans = image.shape
+def sorter(width, back):
+    size = 4 * width
+    row = lax.broadcasted_iota(jnp.int32, (size, size), 1 if back else 0)
+    col = lax.broadcasted_iota(jnp.int32, (size, size), 0 if back else 1)
+    half, rest = col // (2 * width), col % (2 * width)
+    source = (rest // width) * (2 * width) + 2 * (rest % width) + half
+    return jnp.where(row == source, 1.0, 0.0).astype(BF16)
+
+
+def gain_column(gain, column):
+    column[...] = jnp.transpose(jnp.broadcast_to(gain[...][None], (LANES, gain.shape[0])))
+
+
+def reduce_kernel(
+    vis, image, gain, weight, bias, order, patches, normed, rstd, down, first, last, column, sort
+):
+    rows, chans, cols = image.shape
     height, width = rows // 2, cols // 2
     mask = column_mask(vis, width)
-    wide = tiles_of(chans)
-    for r in range(rows):
-        p, a = r // 2, r % 2
-        x = image[r].astype(F32)
-        center = jnp.sum(x, axis=-1, keepdims=True) * (1.0 / chans)
-        x = x - center
-        var = jnp.sum(x * x, axis=-1, keepdims=True) * (1.0 / chans)
-        inv = 1.0 / jnp.sqrt(var + 1e-06)
-        x = x * inv
-        for t, wd in wide:
-            spread[r, t, :, 0:wd] = x[:, t * LANES : t * LANES + wd]
-        spread[r, len(wide)] = jnp.broadcast_to(inv, (cols, LANES))
-        for b in range(2):
-            at = pl.ds(p * width, width)
-            for t, wd in wide:
-                lanes = slice(t * LANES, t * LANES + wd)
-                part = spread[r, t, pl.ds(b, width, stride=2), :][:, :wd]
-                normed[2 * a + b, at, lanes] = part.astype(BF16)
-                patches[2 * a + b, at, lanes] = (part * gain[:, lanes]).astype(BF16)
-            rstd[2 * a + b, at, :] = spread[r, len(wide), pl.ds(b, width, stride=2), :]
-    acc = jnp.zeros((height * width, weight.shape[1]), F32)
-    for k in range(4):
-        acc = acc + jnp.dot(
-            patches[k], weight[k * chans : (k + 1) * chans, :], preferred_element_type=F32
-        )
-    acc = acc + bias[...]
-    for t, wd in tiles_of(weight.shape[1]):
+    gain_column(gain, column)
+    sort[...] = sorter(width, False)
+    for a in range(2):
+        for pair in range(height // 2):
+            top = 4 * pair + a
+            two = jnp.concatenate([image[top], image[top + 2]], axis=1)
+            x = jnp.dot(two, sort[...], preferred_element_type=F32)
+            center = jnp.sum(x, axis=0, keepdims=True) * (1.0 / chans)
+            x = x - center
+            var = jnp.sum(x * x, axis=0, keepdims=True) * (1.0 / chans)
+            inv = 1.0 / jnp.sqrt(var + 1e-06)
+            x = x * inv
+            lanes = slice(pair * LANES, (pair + 1) * LANES)
+            for b in range(2):
+                k = 2 * a + b
+                here = slice(k * chans, (k + 1) * chans)
+                part = x[:, b * LANES : (b + 1) * LANES]
+                normed[here, lanes] = part.astype(BF16)
+                patches[here, lanes] = (part * column[...]).astype(BF16)
+                rstd[k : k + 1, lanes] = inv[:, b * LANES : (b + 1) * LANES]
+    acc = jnp.dot(weight[...], patches[...], preferred_element_type=F32)
+    acc = jnp.transpose(acc) + bias[...][None]
+    for t, wd in tiles_of(weight.shape[0]):
         lanes = slice(t * LANES, t * LANES + wd)
         for p in range(height):
             row = (acc[p * width : (p + 1) * width, lanes] * mask[:, :wd]).astype(BF16)
@@ -155,13 +167,11 @@
     lax.fori_loop(0, 2 * len(tiles_of(chans)), step, 0)
     pre[...] = total[:, :chans].astype(BF16)
     scale = 1.0 / math.sqrt(height * 16 * width)
-    share = patches.shape[2] // 4
+    depth = patches.shape[0] // 4
+    share = depth // 4
     for k in range(4):
-        prod[...] = (
-            lax.dot_general(
-                patches[k], pre[...], (((0,), (0,)), ((), ())), preferred_element_type=F32
-            )
-            * scale
+        prod[...] = scale * jnp.dot(
+            patches[k * depth : (k + 1) * depth, :], pre[...], preferred_element_type=F32
         )
         for d in range(4):
             to = lax.rem(place[0] + d, 4)
@@ -169,7 +179,9 @@
             chunks[d][k] = prod[at, :].astype(BF16)
 
 
-def front_kernel(vis, down, before, after, kernel, bias, cot, features, grads, band, taps, cots, outs, kg):
+def front_kernel(
+    vis, down, before, after, kernel, bias, cot, order, features, grads, band, taps, cots, outs, kg
+):
     height, width, chans = cot.shape
     mask = column_mask(vis, width)
     fill_band(band, before, down, after, None)
@@ -210,49 +222,61 @@
     for t, wd in tiles:
         lanes = slice(t * LANES, t * LANES + wd)
         for p in range(height):
-            value = (outs[t, p, :, 0:wd] + bias[:, lanes]) * mask[:, :wd]
+            value = (outs[t, p, :, 0:wd] + bias[lanes][None]) * mask[:, :wd]
             own = band[t, 3 + p, 8 : 8 + width, 0:wd]
             features[p, :, lanes] = (own + value).astype(BF16)
         term = jnp.sum(kg[2 * t] + kg[2 * t + 1], axis=1) * scale
         grads[0 : KS * KS + 1, lanes] = term[:, :wd]
 
 
-def image_kernel(pre, weight, normed, rstd, gain, grads, image_grad, small, spread, sums):
-    rows, cols, chans = image_grad.shape
+def image_kernel(
+    pre, weight, normed, rstd, gain, grads, image_grad, small, column, sort, flat, sums
+):
+    rows, chans, cols = image_grad.shape
     height, width = rows // 2, cols // 2
-    wide = tiles_of(chans)
     scale = 1.0 / math.sqrt(height * 16 * width)
-    gain_sum = jnp.zeros((1, chans), F32)
-    for k in range(4):
-        a, b = k // 2, k % 2
-        flat = lax.dot_general(
-            pre[...],
-            weight[k * chans : (k + 1) * chans, :],
-            (((1,), (1,)), ((), ())),
-            preferred_element_type=F32,
-        )
-        norm = normed[k].astype(F32)
-        gain_sum = gain_sum + jnp.sum(norm * flat, axis=0, keepdims=True)
-        g = flat * gain[...]
-        mean_g = jnp.sum(g, axis=-1, keepdims=True) * (1.0 / chans)
-        mean_n = jnp.sum(g * norm, axis=-1, keepdims=True) * (1.0 / chans)
-        g = g - mean_g - norm * mean_n
-        for t, wd in wide:
-            part = g[:, t * LANES : t * LANES + wd] * rstd[k][:, :wd]
-            for p in range(height):
-                spread[2 * p + a, t, pl.ds(b, width, stride=2), 0:wd] = part[
-                    p * width : (p + 1) * width
-                ]
-    for r in range(rows):
-        for t, wd in wide:
-            image_grad[r, :, t * LANES : t * LANES + wd] = spread[r, t, :, 0:wd].astype(BF16)
-    bias_sum = jnp.sum(pre[...].astype(F32), axis=0, keepdims=True)
+    gain_column(gain, column)
+    sort[...] = sorter(width, True)
+    flat[...] = jnp.transpose(jnp.dot(pre[...], weight[...], preferred_element_type=F32))
+    gain_sum = jnp.zeros((chans, LANES), F32)
+    for a in range(2):
+        for pair in range(height // 2):
+            top = 4 * pair + a
+            lanes = slice(pair * LANES, (pair + 1) * LANES)
+            two = []
+            for b in range(2):
+                k = 2 * a + b
+                here = slice(k * chans, (k + 1) * chans)
+                value = flat[here, lanes]
+                norm = normed[here, lanes].astype(F32)
+                gain_sum = gain_sum + norm * value
+                g = value * column[...]
+                mean_g = jnp.sum(g, axis=0, keepdims=True) * (1.0 / chans)
+                mean_n = jnp.sum(g * norm, axis=0, keepdims=True) * (1.0 / chans)
+                g = (g - mean_g - norm * mean_n) * rstd[k : k + 1, lanes]
+                two.append(g.astype(BF16))
+            out = jnp.dot(jnp.concatenate(two, axis=1), sort[...], preferred_element_type=F32)
+            image_grad[top] = out[:, :cols].astype(BF16)
+            image_grad[top + 2] = out[:, cols:].astype(BF16)
+    ones = jnp.ones((8, pre.shape[0]), BF16)
+    bias_sum = jnp.dot(ones, pre[...], preferred_element_type=F32)[0:1]
+    gain_row = jnp.sum(jnp.transpose(gain_sum), axis=0, keepdims=True)
     taps = KS * KS + 1
     sums[...] = jnp.zeros(sums.shape, F32)
     sums[0:taps, :] = grads[0:taps, :]
     sums[taps : taps + 1, :] = bias_sum * scale
-    sums[taps + 1 : taps + 2, 0:chans] = gain_sum * scale
+    sums[taps + 1 : taps + 2, 0:chans] = gain_row * scale
     small[...] = sums[...].astype(BF16)
+
+
+def last_kernel(w0, w1, w2, w3, t0, t1, t2, t3, weight, gain, bias, kernel, depth_bias):
+    weight[...] = sum_four(w0[...], w1[...], w2[...], w3[...])
+    total = sum_four(t0[...], t1[...], t2[...], t3[...])
+    taps = KS * KS
+    kernel[...] = total[:taps]
+    depth_bias[...] = total[taps]
+    bias[...] = total[taps + 1]
+    gain[...] = total[taps + 2, : gain.shape[0]]
 
 
 def sd(shape, dtype):
@@ -266,6 +290,8 @@
 def body(image, visible, layer_norm_gain, reducer_weight, reducer_bias, depth_kernel, depth_bias, cotangent):
     height, width, chans = cotangent.shape
     rows, cols, in_chans = image.shape
+    image = jnp.transpose(image, (0, 2, 1))
+    weight = jnp.transpose(reducer_weight)
     pixels = height * width
     bands = lax.axis_size("rows")
     index = lax.axis_index("rows")
@@ -279,7 +305,7 @@
     halo = sd((3, width, chans), BF16)
     macs = pixels * chans * 4 * in_chans
     taps = pixels * chans * KS * KS
-    gain = layer_norm_gain.reshape(1, in_chans)
+    gain = layer_norm_gain
 
     cot_first, cot_last = call(
         edge_kernel, (halo, halo), [SM, VM], [], pixels * chans, 10**6, "edge"
@@ -287,22 +313,24 @@
     cot_before = lax.ppermute(cot_last, "rows", up)
     cot_after = lax.ppermute(cot_first, "rows", down_perm)
 
+    column = pltpu.VMEM((in_chans, LANES), F32)
+    sort = pltpu.VMEM((4 * width, 4 * width), BF16)
     patches, normed, rstd, down, first, last = call(
         reduce_kernel,
         (
-            sd((4, pixels, in_chans), BF16),
-            sd((4, pixels, in_chans), BF16),
-            sd((4, pixels, LANES), F32),
+            sd((4 * in_chans, pixels), BF16),
+            sd((4 * in_chans, pixels), BF16),
+            sd((8, pixels), F32),
             sd((height, width, chans), BF16),
             halo,
             halo,
         ),
-        [SM, VM, VM, VM, VM],
-        [pltpu.VMEM((rows, in_tiles + 1, cols, LANES), F32)],
+        [SM, VM, VM, VM, VM, ANY],
+        [column, sort],
         2 * macs,
         8 * 10**6,
         "reduce",
-    )(visible, image, gain, reducer_weight, reducer_bias.reshape(1, chans))
+    )(visible, image, gain, weight, reducer_bias, cot_first)
     down_before = lax.ppermute(last, "rows", up)
     down_after = lax.ppermute(first, "rows", down_perm)
 
@@ -330,7 +358,7 @@
     features, grads = call(
         front_kernel,
         (sd((height, width, chans), BF16), sd((56, chans), F32)),
-        [SM, VM, VM, VM, VM, VM, VM],
+        [SM, VM, VM, VM, VM, VM, VM, ANY],
         [
             band,
             taps_s,
@@ -338,21 +366,23 @@
             pltpu.VMEM((tiles, height, width, LANES), F32),
             pltpu.VMEM((2 * tiles, KS * KS + 1, 8, LANES), F32),
         ],
-        80 * taps,
-        6 * 10**6,
+        10**6,
+        10**5,
         "front",
-    )(visible, down, down_before, down_after, depth_kernel, depth_bias.reshape(1, chans), cotangent)
+    )(visible, down, down_before, down_after, depth_kernel, depth_bias, cotangent, pre)
 
     image_grad, small = call(
         image_kernel,
-        (sd((rows, cols, in_chans), BF16), sd((64, chans), BF16)),
+        (sd((rows, in_chans, cols), BF16), sd((64, chans), BF16)),
         [VM] * 6,
-        [pltpu.VMEM((rows, in_tiles, cols, LANES), F32), pltpu.VMEM((64, chans), F32)],
-        2 * macs,
-        8 * 10**6,
+        [column, sort, pltpu.VMEM((4 * in_chans, pixels), F32), pltpu.VMEM((64, chans), F32)],
+        10**6,
+        10**5,
         "image",
-    )(pre, reducer_weight, normed, rstd, gain, grads)
-
+    )(pre, weight, normed, rstd, gain, grads)
+    image_grad = jnp.transpose(image_grad, (0, 2, 1))
+
+    small, _ = lax.optimization_barrier((small, got[0]))
     tiny = [lax.ppermute(small, "rows", along_y[k]) for k in (1, 2, 3)]
     small = sum_four(small, *tiny).astype(BF16)
 
@@ -360,17 +390,29 @@
     parts = [lax.dynamic_index_in_dim(half, (place_z + k) % 4, 0, False) for k in range(4)]
     got = [lax.ppermute(parts[k], "rows", along_z[k]) for k in (1, 2, 3)]
     tiny = [lax.ppermute(small, "rows", along_z[k]) for k in (1, 2, 3)]
-    down_weight_grad = sum_four(parts[0], *got)
-    small = sum_four(small, *tiny)
-    n = KS * KS
+    down_weight_grad, gain_grad, bias_grad, kernel_grad, depth_bias_grad = call(
+        last_kernel,
+        (
+            sd((share, chans), F32),
+            sd((in_chans,), F32),
+            sd((chans,), F32),
+            sd((KS * KS, chans), F32),
+            sd((chans,), F32),
+        ),
+        [VM] * 8,
+        [],
+        10**6,
+        10**6,
+        "last",
+    )(parts[0], *got, small, *tiny)
     return (
         features,
         image_grad,
         down_weight_grad,
-        small[n + 2, :in_chans],
-        small[n + 1],
-        small[:n],
-        small[n],
+        gain_grad,
+        bias_grad,
+        kernel_grad,
+        depth_bias_grad,
     )
 
 

time: 97.6 us -> 101 us (1.035)
  waiting for transfers between devices: 21.2 us -> 37.6 us
  local copies, waits for them, and re-layouts: 17.3 us -> 9.12 us
  starting transfers between devices: 36.1 us -> 30.4 us
    ppermute x1, waiting for transfers between devices: 0.01 us -> 17.9 us  [body(): down_before = lax.ppermute(last, 'rows', up)]
    ppermute x3, waiting for transfers between devices: 10.6 us -> 0.01 us  [body(): tiny = [lax.ppermute(small, 'rows', along_y[k]) for k in (1, 2, 3)]]
    unnamed x37 -> x36, local copies, waits for them, and re-layouts: 14 us -> 9.07 us
    ppermute x3, waiting for transfers between devices: 5.82 us -> 10.4 us  [body(): got = [lax.ppermute(parts[k], 'rows', along_z[k]) for k in (1, 2, 3)]]
    ppermute x1, waiting for transfers between devices: 0.46 us -> 4.49 us  [body(): down_after = lax.ppermute(first, 'rows', down_perm)]
    ppermute x3, starting transfers between devices: 6.74 us -> 3.41 us  [body(): tiny = [lax.ppermute(small, 'rows', along_y[k]) for k in (1, 2, 3)]]
    ppermute x3, starting transfers between devices: 6.19 us -> 4.2 us  [body(): tiny = [lax.ppermute(small, 'rows', along_z[k]) for k in (1, 2, 3)]]
    slice x3 -> x0, local copies, waits for them, and re-layouts: 1.89 us -> none  [the longest x1 0.68 us: body(): small[:n]]
  transfers between devices with their start and end apart: 16 -> 16, of which waited for: 8 -> 5; matrix products, arithmetic and copies ran while one was open for 3% -> 2% of each run, Pallas kernels for 9% -> 13%
where the time goes in v2:
time: 101 us; the launch traced here: 100 us
  waiting for transfers between devices  37.6 us (37%)
  starting transfers between devices  30.4 us (30%)
  Pallas kernels  20.5 us (20%)
  local copies, waits for them, and re-layouts  9.12 us (9%)
  other arithmetic  1.71 us (2%)
    ppermute x1, waiting for transfers between devices, body(): down_before = lax.ppermute(last, 'rows', up)  17.9 us
    ppermute x3, waiting for transfers between devices, body(): got = [lax.ppermute(parts[k], 'rows', along_z[k]) for k in (1, 2, 3)]  10.4 us
    unnamed x36, local copies, waits for them, and re-layouts  9.07 us
    pallas_call x1, Pallas kernels, body(): call(front_kernel, (sd((height, width, chans), BF16), sd((56, chans), F32...  7.51 us
    ppermute x3, starting transfers between devices, body(): got = [lax.ppermute(chunks[k], 'rows', along_y[k]) for k in (1, 2, 3)]  6.58 us
    pallas_call x1, Pallas kernels, body(): call(back_kernel, (sd((pixels, chans), BF16),) + (sd((4, share, chans), B...  6.3 us
    ppermute x3, starting transfers between devices, body(): got = [lax.ppermute(parts[k], 'rows', along_z[k]) for k in (1, 2, 3)]  5.54 us
    ppermute x1, starting transfers between devices, body(): down_before = lax.ppermute(last, 'rows', up)  4.64 us
  transfers between devices with their start and end apart: 16, of which 5 were waited for; matrix products, arithmetic and copies ran while one was open for 2% of the time, Pallas kernels for 13%

profile of v2, /device:TPU:2, one launch (start us, length us, event | category | flops | bytes accessed | tf_op | source)
XLA Modules:
  0.0 100.2 jit_solution(16116316908375642977)
XLA Ops:
  0.6 1.0 copy-done.2
  2.9 3.5 %collective-permute-start.2 = (bf16[3,64,704]{2,1,0:T(8,128)(2,1)S(1)}, bf16[3,64,704]{2,1,0:T(8,128)(2,1)S(1)}, u32[]{:S(2)}, u32[]{:S(2)}) collective-permute-start(bf16[3,64,704]{2,1,0:T(8,128)(2,1)S(1)} %get-tuple-element.34), channel_id=1, source_target_pairs={{0,1},{1,2},{2,3},{3,4},{4,5},{5,6},{6,7},{7,8},{8,9},{9,10},{10,1... | collective-permute-start | bytes 811016 | tf_op jit(solution)/shard_map/ppermute | solution.py:313
  6.4 1.3 %collective-permute-start.3 = (bf16[3,64,704]{2,1,0:T(8,128)(2,1)S(1)}, bf16[3,64,704]{2,1,0:T(8,128)(2,1)S(1)}, u32[]{:S(2)}, u32[]{:S(2)}) collective-permute-start(bf16[3,64,704]{2,1,0:T(8,128)(2,1)S(1)} %get-tuple-element.30.order), channel_id=1, source_target_pairs={{1,0},{2,1},{3,2},{4,3},{5,4},{6,5},{7,6},{8,7},{9,8},{10,9},{11,1... | collective-permute-start | bytes 811016 | tf_op jit(solution)/shard_map/ppermute | solution.py:314
  7.8 1.5 %copy-done = bf16[1408,704]{0,1:T(8,128)(2,1)S(1)} copy-done((bf16[1408,704]{0,1:T(8,128)(2,1)S(1)}, bf16[1408,704]{0,1:T(8,128)(2,1)}, u32[]{:S(2)}) %copy-start) | copy-done | bytes 1982488
  9.3 1.1 %copy-done.4 = bf16[8,128,352]{1,2,0:T(8,128)(2,1)S(1)} copy-done((bf16[8,128,352]{1,2,0:T(8,128)(2,1)S(1)}, bf16[8,128,352]{1,2,0:T(8,128)(2,1)}, u32[]{:S(2)}) %copy-start.4) | copy-done | bytes 720920
  10.4 0.7 copy-done.11
  11.8 0.7 copy-done.16
  12.4 3.0 %reduce.1 = (bf16[1408,256]{1,0:T(8,128)(2,1)S(1)}, bf16[1408,256]{1,0:T(8,128)(2,1)S(1)}, f32[8,256]{1,0:T(8,128)S(1)}, bf16[4,64,704]{2,1,0:T(8,128)(2,1)S(1)}...) custom-call(s32[1,16]{1,0:T(1,128)S(1)} %copy-done.14, bf16[8,352,128]{2,1,0:T(8,128)(2,1)S(1)} %bitcast.14, ...), custom_call_target="tpu_custom_call" | custom-call | flops 507510784 | bytes 8000000 | tf_op jit(solution)/shard_map/reduce/pallas_call | solution.py:318
  15.4 1.4 %collective-permute-done.3.after = bf16[3,64,704]{2,1,0:T(8,128)(2,1)S(1)} collective-permute-done((bf16[3,64,704]{2,1,0:T(8,128)(2,1)S(1)}, bf16[3,64,704]{2,1,0:T(8,128)(2,1)S(1)}, u32[]{:S(2)}, u32[]{:S(2)}) %collective-permute-start.3) | collective-permute-done | bytes 270368 | tf_op jit(solution)/shard_map/ppermute | solution.py:314
  16.8 6.3 %back.1 = (bf16[256,704]{1,0:T(8,128)(2,1)S(1)}, bf16[4,88,704]{2,1,0:T(8,128)(2,1)S(1)}, bf16[4,88,704]{2,1,0:T(8,128)(2,1)}, bf16[4,88,704]{2,1,0:T(8,128)(2,1)}, bf16[4,88,704]{2,1,0:T(8,128)(2,1)}) custom-call(s32[1]{0:T(128)} %bitcast.2.place, s32[1,16]{1,0:T(1,128)S(1)} %copy-done.14, bf16[4,64,704]{2,1,0:T(8,128)(2,1)S(1)} %copy-done.3, ...), custom_call_target="tpu_custom_call" | custom-call | flops 860749824 | bytes 6000000 | tf_op jit(solution)/shard_map/back/pallas_call | solution.py:340
  23.1 0.8 copy-done.5
  23.9 1.6 %collective-permute-start.5 = (bf16[4,88,704]{2,1,0:T(8,128)(2,1)}, bf16[4,88,704]{2,1,0:T(8,128)(2,1)}, u32[]{:S(2)}, u32[]{:S(2)}) collective-permute-start(bf16[4,88,704]{2,1,0:T(8,128)(2,1)} %get-tuple-element.44), channel_id=1, source_target_pairs={{0,1},{1,2},{2,3},{3,0},{4,5},{5,6},{6,7},{7,4},{8,9},{9,10},{10,1... | collective-permute-start | bytes 1486856 | tf_op jit(solution)/shard_map/ppermute | solution.py:356
  25.5 5.0 %collective-permute-start.4 = (bf16[4,88,704]{2,1,0:T(8,128)(2,1)}, bf16[4,88,704]{2,1,0:T(8,128)(2,1)}, u32[]{:S(2)}, u32[]{:S(2)}) collective-permute-start(bf16[4,88,704]{2,1,0:T(8,128)(2,1)} %get-tuple-element.43), channel_id=1, source_target_pairs={{0,2},{1,3},{2,0},{3,1},{4,6},{5,7},{6,4},{7,5},{8,10},{9,11},{10,... | collective-permute-start | bytes 1486856 | tf_op jit(solution)/shard_map/ppermute | solution.py:356
  30.5 4.6 %collective-permute-start = (bf16[3,64,704]{2,1,0:T(8,128)(2,1)}, bf16[3,64,704]{2,1,0:T(8,128)(2,1)}, u32[]{:S(2)}, u32[]{:S(2)}) collective-permute-start(bf16[3,64,704]{2,1,0:T(8,128)(2,1)} %get-tuple-element.32), channel_id=1, source_target_pairs={{0,1},{1,2},{2,3},{3,4},{4,5},{5,6},{6,7},{7,8},{8,9},{9,10},{10,1... | collective-permute-start | bytes 811016 | tf_op jit(solution)/shard_map/ppermute | solution.py:334
  35.1 1.3 %collective-permute-start.1 = (bf16[3,64,704]{2,1,0:T(8,128)(2,1)}, bf16[3,64,704]{2,1,0:T(8,128)(2,1)}, u32[]{:S(2)}, u32[]{:S(2)}) collective-permute-start(bf16[3,64,704]{2,1,0:T(8,128)(2,1)} %get-tuple-element.33), channel_id=1, source_target_pairs={{1,0},{2,1},{3,2},{4,3},{5,4},{6,5},{7,6},{8,7},{9,8},{10,9},{11,1... | collective-permute-start | bytes 811016 | tf_op jit(solution)/shard_map/ppermute | solution.py:335
  36.5 17.9 %collective-permute-done.before = bf16[3,64,704]{2,1,0:T(8,128)(2,1)} collective-permute-done((bf16[3,64,704]{2,1,0:T(8,128)(2,1)}, bf16[3,64,704]{2,1,0:T(8,128)(2,1)}, u32[]{:S(2)}, u32[]{:S(2)}) %collective-permute-start) | collective-permute-done | bytes 270368 | tf_op jit(solution)/shard_map/ppermute | solution.py:334
  54.5 4.5 %collective-permute-done.1.after = bf16[3,64,704]{2,1,0:T(8,128)(2,1)} collective-permute-done((bf16[3,64,704]{2,1,0:T(8,128)(2,1)}, bf16[3,64,704]{2,1,0:T(8,128)(2,1)}, u32[]{:S(2)}, u32[]{:S(2)}) %collective-permute-start.1) | collective-permute-done | bytes 270368 | tf_op jit(solution)/shard_map/ppermute | solution.py:335
  59.0 1.0 copy-done.8
  60.0 0.9 copy-done.10
  60.9 7.5 %front.1 = (bf16[4,64,704]{2,1,0:T(8,128)(2,1)}, f32[56,704]{1,0:T(8,128)S(1)}) custom-call(s32[1,16]{1,0:T(1,128)S(1)} %copy-done.15, bf16[4,64,704]{2,1,0:T(8,128)(2,1)S(1)} %copy-done.8, bf16[3,64,704]{2,1,0:T(8,128)(2,1)} %collective-permute-done.before, bf16[3,64,704]{2,1,0:T(8,128)(2,1)} %collective-permute-done.1.after, f32[49,704]{1,0:T(8,128)S(1)} %copy-done.10, ...), custom_call_target="tpu_custom_call" | custom-call | flops 1000000 | bytes 100000 | tf_op jit(solution)/shard_map/front/pallas_call | solution.py:358
  68.4 2.3 %image.1 = (bf16[8,352,128]{2,1,0:T(8,128)(2,1)}, bf16[64,704]{1,0:T(8,128)(2,1)S(1)}) custom-call(bf16[256,704]{1,0:T(8,128)(2,1)S(1)} %get-tuple-element.36.order.pre, bf16[704,1408]{1,0:T(8,128)(2,1)S(1)} %bitcast.13, bf16[1408,256]{1,0:T(8,128)(2,1)S(1)} %get-tuple-element.38.normed, f32[8,256]{1,0:T(8,128)S(1)} %get-tuple-element.39.rstd, ...), custom_call_target="tpu_custom_call" | custom-call | flops 1000000 | bytes 100000 | tf_op jit(solution)/shard_map/image/pallas_call | solution.py:374
  70.7 1.1 %collective-permute-start.12 = (bf16[64,704]{1,0:T(8,128)(2,1)S(1)}, bf16[64,704]{1,0:T(8,128)(2,1)S(1)}, u32[]{:S(2)}, u32[]{:S(2)}) collective-permute-start(bf16[64,704]{1,0:T(8,128)(2,1)S(1)} %get-tuple-element.47), channel_id=1, source_target_pairs={{0,3},{1,0},{2,1},{3,2},{4,7},{5,4},{6,5},{7,6},{8,11},{9,8},{10,9... | collective-permute-start | bytes 270344 | tf_op jit(solution)/shard_map/ppermute | solution.py:386
  71.8 0.9 collective-permute-start.11
  72.7 1.4 %collective-permute-start.10 = (bf16[64,704]{1,0:T(8,128)(2,1)S(1)}, bf16[64,704]{1,0:T(8,128)(2,1)S(1)}, u32[]{:S(2)}, u32[]{:S(2)}) collective-permute-start(bf16[64,704]{1,0:T(8,128)(2,1)S(1)} %get-tuple-element.47), channel_id=1, source_target_pairs={{0,2},{1,3},{2,0},{3,1},{4,6},{5,7},{6,4},{7,5},{8,10},{9,11},{10,... | collective-permute-start | bytes 270344 | tf_op jit(solution)/shard_map/ppermute | solution.py:386
  74.1 1.7 %add_convert_fusion = bf16[4,88,704]{2,1,0:T(8,128)(2,1)S(1)} fusion(bf16[4,88,704]{2,1,0:T(8,128)(2,1)} %collective-permute-done.6, bf16[4,88,704]{2,1,0:T(8,128)(2,1)} %collective-permute-done.5, bf16[4,88,704]{2,1,0:T(8,128)(2,1)} %collective-permute-done.4, bf16[4,88,704]{2,1,0:T(8,128)(2,1)S(1)} %copy-done.6), kind=kLoop, calls=%fused_computation | loop fusion | flops 1982464 | bytes 2478080 | tf_op jit(solution)/shard_map/convert_element_type | solution.py:389
  75.9 4.7 %collective-permute-start.9 = (bf16[88,704]{1,0:T(8,128)(2,1)S(1)}, bf16[88,704]{1,0:T(8,128)(2,1)S(1)}, u32[]{:S(2)}, u32[]{:S(2)}) collective-permute-start(bf16[88,704]{1,0:T(8,128)(2,1)S(1)} %get-tuple-element.53), channel_id=1, source_target_pairs={{0,12},{1,13},{2,14},{3,15},{4,0},{5,1},{6,2},{7,3},{8,4},{9,5},{1... | collective-permute-start | bytes 371720 | tf_op jit(solution)/shard_map/ppermute | solution.py:391
  80.6 0.8 collective-permute-start.7
  81.5 3.1 %collective-permute-start.15 = (bf16[64,704]{1,0:T(8,128)(2,1)S(1)}, bf16[64,704]{1,0:T(8,128)(2,1)S(1)}, u32[]{:S(2)}, u32[]{:S(2)}) collective-permute-start(bf16[64,704]{1,0:T(8,128)(2,1)S(1)} %add_convert_fusion.1.t0), channel_id=1, source_target_pairs={{0,12},{1,13},{2,14},{3,15},{4,0},{5,1},{6,2},{7,3},{8,4},{9,5},{1... | collective-permute-start | bytes 270344 | tf_op jit(solution)/shard_map/ppermute | solution.py:392
  84.5 1.1 %collective-permute-start.14 = (bf16[64,704]{1,0:T(8,128)(2,1)S(1)}, bf16[64,704]{1,0:T(8,128)(2,1)S(1)}, u32[]{:S(2)}, u32[]{:S(2)}) collective-permute-start(bf16[64,704]{1,0:T(8,128)(2,1)S(1)} %add_convert_fusion.1.t0), channel_id=1, source_target_pairs={{0,8},{1,9},{2,10},{3,11},{4,12},{5,13},{6,14},{7,15},{8,0},{9,1},... | collective-permute-start | bytes 270344 | tf_op jit(solution)/shard_map/ppermute | solution.py:392
  85.7 10.4 %collective-permute-done.8.w2 = bf16[88,704]{1,0:T(8,128)(2,1)S(1)} collective-permute-done((bf16[88,704]{1,0:T(8,128)(2,1)S(1)}, bf16[88,704]{1,0:T(8,128)(2,1)S(1)}, u32[]{:S(2)}, u32[]{:S(2)}) %collective-permute-start.8) | collective-permute-done | bytes 123936 | tf_op jit(solution)/shard_map/ppermute | solution.py:391
  96.1 3.4 %collective-permute-done.14.t2 = bf16[64,704]{1,0:T(8,128)(2,1)S(1)} collective-permute-done((bf16[64,704]{1,0:T(8,128)(2,1)S(1)}, bf16[64,704]{1,0:T(8,128)(2,1)S(1)}, u32[]{:S(2)}, u32[]{:S(2)}) %collective-permute-start.14) | collective-permute-done | bytes 90144 | tf_op jit(solution)/shard_map/ppermute | solution.py:392
  99.4 0.8 last.1
  (45 shorter events, 2.1 us)
Async XLA Ops:
  0.6 1.0 copy-start.2
  2.9 12.5 %collective-permute-start.2 = (bf16[3,64,704]{2,1,0:T(8,128)(2,1)S(1)}, bf16[3,64,704]{2,1,0:T(8,128)(2,1)S(1)}, u32[]{:S(2)}, u32[]{:S(2)}) collective-permute-start(bf16[3,64,704]{2,1,0:T(8,128)(2,1)S(1)} %get-tuple-element.34), channel_id=1, source_target_pairs={{0,1},{1,2},{2,3},{3,4},{4,5},{5,6},{6,7},{7,8},{8,9},{9,10},{10,1... | collective-permute-start | bytes 811016 | tf_op jit(solution)/shard_map/ppermute | solution.py:313
  6.4 10.4 %collective-permute-start.3 = (bf16[3,64,704]{2,1,0:T(8,128)(2,1)S(1)}, bf16[3,64,704]{2,1,0:T(8,128)(2,1)S(1)}, u32[]{:S(2)}, u32[]{:S(2)}) collective-permute-start(bf16[3,64,704]{2,1,0:T(8,128)(2,1)S(1)} %get-tuple-element.30.order), channel_id=1, source_target_pairs={{1,0},{2,1},{3,2},{4,3},{5,4},{6,5},{7,6},{8,7},{9,8},{10,9},{11,1... | collective-permute-start | bytes 811016 | tf_op jit(solution)/shard_map/ppermute | solution.py:314
  7.7 1.6 %copy-start = (bf16[1408,704]{0,1:T(8,128)(2,1)S(1)}, bf16[1408,704]{0,1:T(8,128)(2,1)}, u32[]{:S(2)}) copy-start(bf16[1408,704]{0,1:T(8,128)(2,1)} %param.11) | copy-start | bytes 5947396
  9.3 1.1 %copy-start.4 = (bf16[8,128,352]{1,2,0:T(8,128)(2,1)S(1)}, bf16[8,128,352]{1,2,0:T(8,128)(2,1)}, u32[]{:S(2)}) copy-start(bf16[8,128,352]{1,2,0:T(8,128)(2,1)} %param.8) | copy-start | bytes 2162692
  10.4 0.7 copy-start.11
  11.8 0.7 copy-start.16
  12.4 4.4 %copy-start.3 = (bf16[4,64,704]{2,1,0:T(8,128)(2,1)S(1)}, bf16[4,64,704]{2,1,0:T(8,128)(2,1)}, u32[]{:S(2)}) copy-start(bf16[4,64,704]{2,1,0:T(8,128)(2,1)} %cot.5) | copy-start | bytes 1081348
  12.4 4.4 %copy-start.9 = (f32[49,704]{1,0:T(8,128)S(1)}, f32[49,704]{1,0:T(8,128)}, u32[]{:S(2)}) copy-start(f32[49,704]{1,0:T(8,128)} %kernel.3) | copy-start | bytes 413956
  15.4 7.7 %copy-start.7 = (bf16[4,64,704]{2,1,0:T(8,128)(2,1)}, bf16[4,64,704]{2,1,0:T(8,128)(2,1)S(1)}, u32[]{:S(2)}) copy-start(bf16[4,64,704]{2,1,0:T(8,128)(2,1)S(1)} %get-tuple-element.31.down) | copy-start | bytes 1081348
  16.8 42.2 %copy-start.15 = (s32[1,16]{1,0:T(1,128)S(1)}, s32[1,16]{1,0:T(1,128)}, u32[]{:S(2)}) copy-start(s32[1,16]{1,0:T(1,128)} %vis.7) | copy-start | bytes 196
  16.8 42.2 %copy-start.17 = (f32[704]{0:T(1024)S(1)}, f32[704]{0:T(1024)}, u32[]{:S(2)}) copy-start(f32[704]{0:T(1024)} %bias.3) | copy-start | bytes 8452
  16.8 51.6 %copy-start.12 = (f32[352]{0:T(512)S(1)}, f32[352]{0:T(512)}, u32[]{:S(2)}) copy-start(f32[352]{0:T(512)} %gain.3) | copy-start | bytes 4228
  23.1 0.8 copy-start.5
  23.9 44.5 %copy-start.1 = (bf16[1408,704]{0,1:T(8,128)(2,1)S(1)}, bf16[1408,704]{0,1:T(8,128)(2,1)}, u32[]{:S(2)}) copy-start(bf16[1408,704]{0,1:T(8,128)(2,1)} %param.11) | copy-start | bytes 5947396
  23.9 46.8 %collective-permute-start.5 = (bf16[4,88,704]{2,1,0:T(8,128)(2,1)}, bf16[4,88,704]{2,1,0:T(8,128)(2,1)}, u32[]{:S(2)}, u32[]{:S(2)}) collective-permute-start(bf16[4,88,704]{2,1,0:T(8,128)(2,1)} %get-tuple-element.44), channel_id=1, source_target_pairs={{0,1},{1,2},{2,3},{3,0},{4,5},{5,6},{6,7},{7,4},{8,9},{9,10},{10,1... | collective-permute-start | bytes 1486856 | tf_op jit(solution)/shard_map/ppermute | solution.py:356
  25.5 48.6 %collective-permute-start.4 = (bf16[4,88,704]{2,1,0:T(8,128)(2,1)}, bf16[4,88,704]{2,1,0:T(8,128)(2,1)}, u32[]{:S(2)}, u32[]{:S(2)}) collective-permute-start(bf16[4,88,704]{2,1,0:T(8,128)(2,1)} %get-tuple-element.43), channel_id=1, source_target_pairs={{0,2},{1,3},{2,0},{3,1},{4,6},{5,7},{6,4},{7,5},{8,10},{9,11},{10,... | collective-permute-start | bytes 1486856 | tf_op jit(solution)/shard_map/ppermute | solution.py:356
  30.5 43.6 %collective-permute-start.6 = (bf16[4,88,704]{2,1,0:T(8,128)(2,1)}, bf16[4,88,704]{2,1,0:T(8,128)(2,1)}, u32[]{:S(2)}, u32[]{:S(2)}) collective-permute-start(bf16[4,88,704]{2,1,0:T(8,128)(2,1)} %get-tuple-element.45), channel_id=1, source_target_pairs={{0,3},{1,0},{2,1},{3,2},{4,7},{5,4},{6,5},{7,6},{8,11},{9,8},{10,9... | collective-permute-start | bytes 1486856 | tf_op jit(solution)/shard_map/ppermute | solution.py:356
  30.5 24.0 %collective-permute-start = (bf16[3,64,704]{2,1,0:T(8,128)(2,1)}, bf16[3,64,704]{2,1,0:T(8,128)(2,1)}, u32[]{:S(2)}, u32[]{:S(2)}) collective-permute-start(bf16[3,64,704]{2,1,0:T(8,128)(2,1)} %get-tuple-element.32), channel_id=1, source_target_pairs={{0,1},{1,2},{2,3},{3,4},{4,5},{5,6},{6,7},{7,8},{8,9},{9,10},{10,1... | collective-permute-start | bytes 811016 | tf_op jit(solution)/shard_map/ppermute | solution.py:334
  35.1 23.8 %collective-permute-start.1 = (bf16[3,64,704]{2,1,0:T(8,128)(2,1)}, bf16[3,64,704]{2,1,0:T(8,128)(2,1)}, u32[]{:S(2)}, u32[]{:S(2)}) collective-permute-start(bf16[3,64,704]{2,1,0:T(8,128)(2,1)} %get-tuple-element.33), channel_id=1, source_target_pairs={{1,0},{2,1},{3,2},{4,3},{5,4},{6,5},{7,6},{8,7},{9,8},{10,9},{11,1... | collective-permute-start | bytes 811016 | tf_op jit(solution)/shard_map/ppermute | solution.py:335
  59.0 1.0 copy-start.8
  60.0 0.9 copy-start.10
  68.4 5.7 %copy-start.6 = (bf16[4,88,704]{2,1,0:T(8,128)(2,1)S(1)}, bf16[4,88,704]{2,1,0:T(8,128)(2,1)}, u32[]{:S(2)}) copy-start(bf16[4,88,704]{2,1,0:T(8,128)(2,1)} %copy-done.5) | copy-start | bytes 1486852
  70.7 9.8 %collective-permute-start.12 = (bf16[64,704]{1,0:T(8,128)(2,1)S(1)}, bf16[64,704]{1,0:T(8,128)(2,1)S(1)}, u32[]{:S(2)}, u32[]{:S(2)}) collective-permute-start(bf16[64,704]{1,0:T(8,128)(2,1)S(1)} %get-tuple-element.47), channel_id=1, source_target_pairs={{0,3},{1,0},{2,1},{3,2},{4,7},{5,4},{6,5},{7,6},{8,11},{9,8},{10,9... | collective-permute-start | bytes 270344 | tf_op jit(solution)/shard_map/ppermute | solution.py:386
  71.8 9.6 %collective-permute-start.11 = (bf16[64,704]{1,0:T(8,128)(2,1)S(1)}, bf16[64,704]{1,0:T(8,128)(2,1)S(1)}, u32[]{:S(2)}, u32[]{:S(2)}) collective-permute-start(bf16[64,704]{1,0:T(8,128)(2,1)S(1)} %get-tuple-element.47), channel_id=1, source_target_pairs={{0,1},{1,2},{2,3},{3,0},{4,5},{5,6},{6,7},{7,4},{8,9},{9,10},{10,1... | collective-permute-start | bytes 270344 | tf_op jit(solution)/shard_map/ppermute | solution.py:386
  72.7 8.7 %collective-permute-start.10 = (bf16[64,704]{1,0:T(8,128)(2,1)S(1)}, bf16[64,704]{1,0:T(8,128)(2,1)S(1)}, u32[]{:S(2)}, u32[]{:S(2)}) collective-permute-start(bf16[64,704]{1,0:T(8,128)(2,1)S(1)} %get-tuple-element.47), channel_id=1, source_target_pairs={{0,2},{1,3},{2,0},{3,1},{4,6},{5,7},{6,4},{7,5},{8,10},{9,11},{10,... | collective-permute-start | bytes 270344 | tf_op jit(solution)/shard_map/ppermute | solution.py:386
  75.9 9.8 %collective-permute-start.9 = (bf16[88,704]{1,0:T(8,128)(2,1)S(1)}, bf16[88,704]{1,0:T(8,128)(2,1)S(1)}, u32[]{:S(2)}, u32[]{:S(2)}) collective-permute-start(bf16[88,704]{1,0:T(8,128)(2,1)S(1)} %get-tuple-element.53), channel_id=1, source_target_pairs={{0,12},{1,13},{2,14},{3,15},{4,0},{5,1},{6,2},{7,3},{8,4},{9,5},{1... | collective-permute-start | bytes 371720 | tf_op jit(solution)/shard_map/ppermute | solution.py:391
  80.5 15.5 %collective-permute-start.8 = (bf16[88,704]{1,0:T(8,128)(2,1)S(1)}, bf16[88,704]{1,0:T(8,128)(2,1)S(1)}, u32[]{:S(2)}, u32[]{:S(2)}) collective-permute-start(bf16[88,704]{1,0:T(8,128)(2,1)S(1)} %get-tuple-element.54), channel_id=1, source_target_pairs={{0,8},{1,9},{2,10},{3,11},{4,12},{5,13},{6,14},{7,15},{8,0},{9,1},... | collective-permute-start | bytes 371720 | tf_op jit(solution)/shard_map/ppermute | solution.py:391
  80.6 15.5 %collective-permute-start.7 = (bf16[88,704]{1,0:T(8,128)(2,1)S(1)}, bf16[88,704]{1,0:T(8,128)(2,1)S(1)}, u32[]{:S(2)}, u32[]{:S(2)}) collective-permute-start(bf16[88,704]{1,0:T(8,128)(2,1)S(1)} %get-tuple-element.55), channel_id=1, source_target_pairs={{0,4},{1,5},{2,6},{3,7},{4,8},{5,9},{6,10},{7,11},{8,12},{9,13},{1... | collective-permute-start | bytes 371720 | tf_op jit(solution)/shard_map/ppermute | solution.py:391
  81.5 14.6 %collective-permute-start.15 = (bf16[64,704]{1,0:T(8,128)(2,1)S(1)}, bf16[64,704]{1,0:T(8,128)(2,1)S(1)}, u32[]{:S(2)}, u32[]{:S(2)}) collective-permute-start(bf16[64,704]{1,0:T(8,128)(2,1)S(1)} %add_convert_fusion.1.t0), channel_id=1, source_target_pairs={{0,12},{1,13},{2,14},{3,15},{4,0},{5,1},{6,2},{7,3},{8,4},{9,5},{1... | collective-permute-start | bytes 270344 | tf_op jit(solution)/shard_map/ppermute | solution.py:392
  84.5 14.9 %collective-permute-start.14 = (bf16[64,704]{1,0:T(8,128)(2,1)S(1)}, bf16[64,704]{1,0:T(8,128)(2,1)S(1)}, u32[]{:S(2)}, u32[]{:S(2)}) collective-permute-start(bf16[64,704]{1,0:T(8,128)(2,1)S(1)} %add_convert_fusion.1.t0), channel_id=1, source_target_pairs={{0,8},{1,9},{2,10},{3,11},{4,12},{5,13},{6,14},{7,15},{8,0},{9,1},... | collective-permute-start | bytes 270344 | tf_op jit(solution)/shard_map/ppermute | solution.py:392
  85.6 13.8 %collective-permute-start.13 = (bf16[64,704]{1,0:T(8,128)(2,1)S(1)}, bf16[64,704]{1,0:T(8,128)(2,1)S(1)}, u32[]{:S(2)}, u32[]{:S(2)}) collective-permute-start(bf16[64,704]{1,0:T(8,128)(2,1)S(1)} %add_convert_fusion.1.t0), channel_id=1, source_target_pairs={{0,4},{1,5},{2,6},{3,7},{4,8},{5,9},{6,10},{7,11},{8,12},{9,13},{1... | collective-permute-start | bytes 270344 | tf_op jit(solution)/shard_map/ppermute | solution.py:392
  (2 other events, 1.3 us)

commit v3 on v2

v3 whole, which is shorter than its diff:
```python
import functools
import math

import jax
import jax.numpy as jnp
from jax import lax
from jax.experimental import pallas as pl
from jax.experimental.pallas import tpu as pltpu
from jax.sharding import PartitionSpec as P

KS = 7
PATCH = 4
LANES = 128
F32 = jnp.float32
BF16 = jnp.bfloat16
VM = pl.BlockSpec(memory_space=pltpu.VMEM)
SM = pl.BlockSpec(memory_space=pltpu.SMEM)
ANY = pl.BlockSpec(memory_space=pl.ANY)
HBM = pl.BlockSpec(memory_space=pltpu.HBM)
FIRST = 4


def tiles_of(chans):
    return [(t, min(LANES, chans - t * LANES)) for t in range(-(-chans // LANES))]


def lanes_of(t, wd):
    return slice(t * LANES, t * LANES + wd)


def column_mask(vis, width):
    row = lax.broadcasted_iota(jnp.int32, (width, LANES), 0) // PATCH
    mask = jnp.zeros((width, LANES), F32)
    for k in range(width // PATCH):
        mask = jnp.where(row == k, vis[0, k].astype(F32), mask)
    return mask


def fetch(sources, targets, sems):
    copies = [
        pltpu.make_async_copy(source, target, sems.at[k])
        for k, (source, target) in enumerate(zip(sources, targets))
    ]
    for copy in copies:
        copy.start()
    return copies


def call(kernel, out_shape, in_specs, scratch, name, vmem=16, size=10**5):
    return pl.pallas_call(
        kernel,
        out_shape=out_shape,
        in_specs=in_specs,
        out_specs=jax.tree.map(lambda _: VM, out_shape),
        scratch_shapes=scratch,
        compiler_params=pltpu.CompilerParams(vmem_limit_bytes=vmem * 2**20),
        cost_estimate=pl.CostEstimate(flops=10**6, bytes_accessed=size, transcendentals=0),
        name=name,
    )


def edge_kernel(vis_in, cot_in, first, last, mask_out, vis, cot, sems):
    copies = fetch((vis_in, cot_in), (vis, cot), sems)
    height, width, chans = cot.shape
    copies[0].wait()
    mask = column_mask(vis, width)
    mask_out[...] = mask
    copies[1].wait()
    for t, wd in tiles_of(chans):
        lanes = lanes_of(t, wd)
        for p in range(height):
            row = (cot[p, :, lanes].astype(F32) * mask[:, :wd]).astype(BF16)
            if p < 3:
                first[p, :, lanes] = row
            if p >= height - 3:
                last[p - (height - 3), :, lanes] = row


def sorter(width, back):
    size = 4 * width
    row = lax.broadcasted_iota(jnp.int32, (size, size), 1 if back else 0)
    col = lax.broadcasted_iota(jnp.int32, (size, size), 0 if back else 1)
    half, rest = col // (2 * width), col % (2 * width)
    source = (rest // width) * (2 * width) + 2 * (rest % width) + half
    return jnp.where(row == source, 1.0, 0.0).astype(BF16)


def gain_column(gain, column):
    column[...] = jnp.transpose(jnp.broadcast_to(gain[...][None], (LANES, gain.shape[0])))


def reduce_kernel(
    image_in, gain_in, weight_in, bias_in, mask, order,
    patches, normed, rstd, down, first, last,
    column, sort, image, gain, weight, bias, sems,
):
    copies = fetch(
        (image_in, gain_in, weight_in, bias_in), (image, gain, weight, bias), sems
    )
    rows, chans, cols = image.shape
    height, width = rows // 2, cols // 2
    sort[...] = sorter(width, False)
    copies[1].wait()
    gain_column(gain, column)
    copies[0].wait()
    for a in range(2):
        for pair in range(height // 2):
            top = 4 * pair + a
            two = jnp.concatenate([image[top], image[top + 2]], axis=1)
            x = jnp.dot(two, sort[...], preferred_element_type=F32)
            center = jnp.sum(x, axis=0, keepdims=True) * (1.0 / chans)
            x = x - center
            var = jnp.sum(x * x, axis=0, keepdims=True) * (1.0 / chans)
            inv = 1.0 / jnp.sqrt(var + 1e-06)
            x = x * inv
            lanes = lanes_of(pair, LANES)
            for b in range(2):
                k = 2 * a + b
                here = slice(k * chans, (k + 1) * chans)
                part = x[:, lanes_of(b, LANES)]
                normed[here, lanes] = part.astype(BF16)
                patches[here, lanes] = (part * column[...]).astype(BF16)
                rstd[k : k + 1, lanes] = inv[:, lanes_of(b, LANES)]
    copies[2].wait()
    copies[3].wait()
    acc = jnp.dot(weight[...], patches[...], preferred_element_type=F32)
    acc = jnp.transpose(acc) + bias[...][None]
    for t, wd in tiles_of(weight.shape[0]):
        lanes = lanes_of(t, wd)
        for p in range(height):
            row = (acc[p * width : (p + 1) * width, lanes] * mask[:, :wd]).astype(BF16)
            down[p, :, lanes] = row
            if p < 3:
                first[p, :, lanes] = row
            if p >= height - 3:
                last[p - (height - 3), :, lanes] = row


def fill_band(dst, at, ref, tiles, first=0):
    count, width = ref.shape[:2]
    for t, wd in tiles:
        d = t - first
        for k in range(count):
            if wd < LANES:
                dst[d, at + k, 8 : 8 + width, wd:LANES] = jnp.zeros((width, LANES - wd), F32)
            dst[d, at + k, 8 : 8 + width, 0:wd] = ref[k, :, lanes_of(t, wd)].astype(F32)


def clear_edges(dst):
    tiles, count, span = dst.shape[:3]
    edge = jnp.zeros((tiles, count, 8, LANES), F32)
    dst[:, :, 0:8, :] = edge
    dst[:, :, span - 8 : span, :] = edge


def own_kernel(cot_in, kernel_in, mask, order, band, taps, part, cot, kernel, sems):
    copies = fetch((cot_in, kernel_in), (cot, kernel), sems)
    height, width, chans = cot.shape
    tiles = tiles_of(chans)
    clear_edges(band)
    copies[1].wait()
    for t, wd in tiles:
        taps[t, :, :, 0:wd] = jnp.broadcast_to(
            kernel[:, lanes_of(t, wd)][:, None, :], (KS * KS, 8, wd)
        )
        if wd < LANES:
            taps[t, :, :, wd:LANES] = jnp.zeros((KS * KS, 8, LANES - wd), F32)
    copies[0].wait()
    for t, wd in tiles:
        for k in range(height):
            if wd < LANES:
                band[t, k, 8 : 8 + width, wd:LANES] = jnp.zeros((width, LANES - wd), F32)
            band[t, k, 8 : 8 + width, 0:wd] = cot[k, :, lanes_of(t, wd)].astype(F32) * mask[:, :wd]
    half = width // 2

    def step(u, carry):
        t, h = u // 2, (u % 2) * half
        acc = [jnp.zeros((half // 8, 8, LANES), F32) for _ in range(height)]
        for s in range(height):
            for j in range(KS):
                value = band[t, s, pl.ds(h + 5 + j, half), :].reshape(half // 8, 8, LANES)
                for p in range(height):
                    i = s + 3 - p
                    acc[p] = acc[p] + value * taps[t, 48 - (KS * i + j)][None]
        for p in range(height):
            part[t, p, pl.ds(pl.multiple_of(h, 8), half), :] = acc[p].reshape(half, LANES)
        return carry

    lax.fori_loop(0, 2 * len(tiles), step, 0)


def back_kernel(
    base, place, before, after, band, taps, part, mask, patches, order, order_too,
    pre, c0, c1, c2, c3, halo, total, prod,
):
    chunks = (c0, c1, c2, c3)
    height, width = part.shape[1:3]
    chans = pre.shape[1]
    tiles = tiles_of(before.shape[2])[base : base + -(-chans // LANES)]
    clear_edges(halo)
    fill_band(halo, 0, before, tiles, base)
    fill_band(halo, 3, after, tiles, base)
    half = width // 2

    def step(u, carry):
        d, h = u // 2, (u % 2) * half
        t = d + base
        here = pl.ds(pl.multiple_of(h, 8), half)
        acc = [part[t, p, here, :].reshape(half // 8, 8, LANES) for p in range(height)]
        for m in range(6):
            s = m if m < 3 else m + height
            for j in range(KS):
                value = halo[d, m, pl.ds(h + 5 + j, half), :].reshape(half // 8, 8, LANES)
                for p in range(height):
                    i = s - p
                    if 0 <= i < KS:
                        acc[p] = acc[p] + value * taps[t, 48 - (KS * i + j)][None]
        keep = mask[here, :]
        lanes = pl.ds(pl.multiple_of(d * LANES, LANES), LANES)
        for p in range(height):
            own = band[t, p, pl.ds(pl.multiple_of(h + 8, 8), half), :]
            value = own + keep * acc[p].reshape(half, LANES)
            total[pl.ds(pl.multiple_of(p * width + h, 8), half), lanes] = value
        return carry

    lax.fori_loop(0, 2 * len(tiles), step, 0)
    pre[...] = total[:, :chans].astype(BF16)
    scale = 1.0 / math.sqrt(height * 16 * width)
    depth = patches.shape[0] // 4
    share = depth // 4
    for k in range(4):
        prod[...] = scale * jnp.dot(
            patches[k * depth : (k + 1) * depth, :], pre[...], preferred_element_type=F32
        )
        for d in range(4):
            to = lax.rem(place[0] + d, 4)
            at = pl.ds(pl.multiple_of(to * share, 8), share)
            chunks[d][k] = prod[at, :].astype(BF16)


def grad_kernel(down, before, after, cots, order, grads, band, kg):
    height, width, chans = down.shape
    tiles = tiles_of(chans)
    clear_edges(band)
    fill_band(band, 0, before, tiles)
    fill_band(band, 3, down, tiles)
    fill_band(band, 3 + height, after, tiles)
    half = width // 2

    def step(u, carry):
        t, h = u // 2, (u % 2) * half
        here = pl.ds(pl.multiple_of(h + 8, 8), half)
        mine = [cots[t, p, here, :].reshape(half // 8, 8, LANES) for p in range(height)]
        for j in range(KS):
            part = [jnp.zeros((half // 8, 8, LANES), F32) for _ in range(KS)]
            for s in range(height + 6):
                value = band[t, s, pl.ds(h + 5 + j, half), :].reshape(half // 8, 8, LANES)
                for p in range(height):
                    i = s - p
                    if 0 <= i < KS:
                        part[i] = part[i] + value * mine[p]
            for i in range(KS):
                kg[u, KS * i + j] = jnp.sum(part[i], axis=0)
        kg[u, KS * KS] = sum(jnp.sum(m, axis=0) for m in mine)
        return carry

    lax.fori_loop(0, 2 * len(tiles), step, 0)
    scale = 1.0 / math.sqrt(height * 16 * width)
    for t, wd in tiles:
        term = jnp.sum(kg[2 * t] + kg[2 * t + 1], axis=1) * scale
        grads[0 : KS * KS + 1, lanes_of(t, wd)] = term[:, :wd]


def front_kernel(band, taps, bias, mask, order, features, outs):
    height, width, chans = features.shape
    tiles = tiles_of(chans)
    half = width // 2

    def step(u, carry):
        t, h = u // 2, (u % 2) * half
        acc = [jnp.zeros((half // 8, 8, LANES), F32) for _ in range(height)]
        for s in range(height + 6):
            for j in range(KS):
                value = band[t, s, pl.ds(h + 5 + j, half), :].reshape(half // 8, 8, LANES)
                for p in range(height):
                    i = s - p
                    if 0 <= i < KS:
                        acc[p] = acc[p] + value * taps[t, KS * i + j][None]
        for p in range(height):
            outs[t, p, pl.ds(pl.multiple_of(h, 8), half), :] = acc[p].reshape(half, LANES)
        return carry

    lax.fori_loop(0, 2 * len(tiles), step, 0)
    for t, wd in tiles:
        lanes = lanes_of(t, wd)
        for p in range(height):
            value = (outs[t, p, :, 0:wd] + bias[lanes][None]) * mask[:, :wd]
            own = band[t, 3 + p, 8 : 8 + width, 0:wd]
            features[p, :, lanes] = (own + value).astype(BF16)


def image_kernel(
    pre_b, pre_a, weight, normed, rstd, gain, grads, image_grad, small, column, sort, flat, sums
):
    rows, chans, cols = image_grad.shape
    height, width = rows // 2, cols // 2
    scale = 1.0 / math.sqrt(height * 16 * width)
    cut = pre_b.shape[1]
    gain_column(gain, column)
    sort[...] = sorter(width, True)
    value = jnp.dot(pre_b[...], weight[:cut, :], preferred_element_type=F32)
    value = value + jnp.dot(pre_a[...], weight[cut:, :], preferred_element_type=F32)
    flat[...] = jnp.transpose(value)
    gain_sum = jnp.zeros((chans, LANES), F32)
    for a in range(2):
        for pair in range(height // 2):
            top = 4 * pair + a
            lanes = lanes_of(pair, LANES)
            two = []
            for b in range(2):
                k = 2 * a + b
                here = slice(k * chans, (k + 1) * chans)
                value = flat[here, lanes]
                norm = normed[here, lanes].astype(F32)
                gain_sum = gain_sum + norm * value
                g = value * column[...]
                mean_g = jnp.sum(g, axis=0, keepdims=True) * (1.0 / chans)
                mean_n = jnp.sum(g * norm, axis=0, keepdims=True) * (1.0 / chans)
                g = (g - mean_g - norm * mean_n) * rstd[k : k + 1, lanes]
                two.append(g.astype(BF16))
            out = jnp.dot(jnp.concatenate(two, axis=1), sort[...], preferred_element_type=F32)
            image_grad[top] = out[:, :cols].astype(BF16)
            image_grad[top + 2] = out[:, cols:].astype(BF16)
    ones = jnp.ones((8, pre_b.shape[0]), BF16)
    gain_row = jnp.sum(jnp.transpose(gain_sum), axis=0, keepdims=True)
    taps = KS * KS + 1
    sums[...] = jnp.zeros(sums.shape, F32)
    sums[0:taps, :] = grads[0:taps, :]
    for pre, lanes in ((pre_b, slice(0, cut)), (pre_a, slice(cut, weight.shape[0]))):
        bias_sum = jnp.dot(ones, pre[...], preferred_element_type=F32)[0:1]
        sums[taps : taps + 1, lanes] = bias_sum * scale
    sums[taps + 1 : taps + 2, 0:chans] = gain_row * scale
    small[...] = sums[...].astype(BF16)


def middle_kernel(place, c0, c1, c2, c3, order, *outs):
    for k in range(4):
        to = lax.rem(place[0] + k, 4)
        outs[k][...] = sum_four(c0[to], c1[to], c2[to], c3[to]).astype(BF16)


def last_kernel(
    b0, b1, b2, b3, a0, a1, a2, a3, t0, t1, t2, t3, weight, gain, bias, kernel, depth_bias
):
    cut = b0.shape[1]
    weight[:, :cut] = sum_four(b0[...], b1[...], b2[...], b3[...])
    weight[:, cut:] = sum_four(a0[...], a1[...], a2[...], a3[...])
    total = sum_four(t0[...], t1[...], t2[...], t3[...])
    taps = KS * KS
    kernel[...] = total[:taps]
    depth_bias[...] = total[taps]
    bias[...] = total[taps + 1]
    gain[...] = total[taps + 2, : gain.shape[0]]


def sd(shape, dtype):
    return jax.ShapeDtypeStruct(shape, dtype)


def sum_four(own, one, two, three):
    return (own.astype(F32) + two.astype(F32)) + (one.astype(F32) + three.astype(F32))


def send(values, pairs):
    return [lax.ppermute(value, "rows", pair) for value, pair in zip(values, pairs)]


def body(image, visible, layer_norm_gain, reducer_weight, reducer_bias, depth_kernel, depth_bias, cotangent):
    height, width, chans = cotangent.shape
    rows, cols, in_chans = image.shape
    image = jnp.transpose(image, (0, 2, 1))
    weight = jnp.transpose(reducer_weight)
    pixels = height * width
    bands = lax.axis_size("rows")
    index = lax.axis_index("rows")
    place_y = (index % 4).reshape(1).astype(jnp.int32)
    place_z = (index // 4).reshape(1).astype(jnp.int32)
    up = [(i, i + 1) for i in range(bands - 1)]
    low = [(j, i) for i, j in up]
    ring = [(z, y) for z in range(4) for y in range(4)]
    along_y = [[(4 * z + y, 4 * z + (y + k) % 4) for z, y in ring] for k in (1, 2, 3)]
    along_z = [[(4 * z + y, 4 * ((z + k) % 4) + y) for z, y in ring] for k in (1, 2, 3)]
    tiles = len(tiles_of(chans))
    cut = FIRST * LANES
    share = in_chans // 4
    halo = sd((3, width, chans), BF16)
    span = width + 16

    cot_first, cot_last, mask = call(
        edge_kernel,
        (halo, halo, sd((width, LANES), F32)),
        [HBM, HBM],
        [
            pltpu.SMEM((1, width // PATCH), jnp.int32),
            pltpu.VMEM((height, width, chans), BF16),
            pltpu.SemaphoreType.DMA((2,)),
        ],
        "edge",
        60,
        2 * 10**7,
    )(visible, cotangent)
    cot_before = lax.ppermute(cot_last, "rows", up)
    cot_after = lax.ppermute(cot_first, "rows", low)

    column = pltpu.VMEM((in_chans, LANES), F32)
    sort = pltpu.VMEM((4 * width, 4 * width), BF16)
    patches, normed, rstd, down, down_first, down_last = call(
        reduce_kernel,
        (
            sd((4 * in_chans, pixels), BF16),
            sd((4 * in_chans, pixels), BF16),
            sd((8, pixels), F32),
            sd((height, width, chans), BF16),
            halo,
            halo,
        ),
        [HBM, HBM, HBM, HBM, VM, ANY],
        [
            column,
            sort,
            pltpu.VMEM(image.shape, BF16),
            pltpu.VMEM((in_chans,), F32),
            pltpu.VMEM(weight.shape, BF16),
            pltpu.VMEM((chans,), F32),
            pltpu.SemaphoreType.DMA((4,)),
        ],
        "reduce",
        60,
        2 * 10**7,
    )(image, layer_norm_gain, weight, reducer_bias, mask, cot_first)
    down_before = lax.ppermute(down_last, "rows", up)
    down_after = lax.ppermute(down_first, "rows", low)

    band, taps, part = call(
        own_kernel,
        (
            sd((tiles, height, span, LANES), F32),
            sd((tiles, KS * KS, 8, LANES), F32),
            sd((tiles, height, width, LANES), F32),
        ),
        [HBM, HBM, VM, ANY],
        [
            pltpu.VMEM((height, width, chans), BF16),
            pltpu.VMEM((KS * KS, chans), F32),
            pltpu.SemaphoreType.DMA((2,)),
        ],
        "own",
    )(cotangent, depth_kernel, mask, down_first)

    def back(here, *order):
        size = here[1] - here[0]
        count = -(-size // LANES)
        return call(
            functools.partial(back_kernel, here[0] // LANES),
            (sd((pixels, size), BF16),) + (sd((4, share, size), BF16),) * 4,
            [SM] + [VM] * 7 + [ANY] * 2,
            [
                pltpu.VMEM((count, 6, span, LANES), F32),
                pltpu.VMEM((pixels, count * LANES), F32),
                pltpu.VMEM((in_chans, size), F32),
            ],
            "back",
        )(place_y, cot_before, cot_after, band, taps, part, mask, patches, *order)

    pre_b, *chunks_b = back((0, cut), mask, mask)
    chunks_b, down_before, down_after = lax.optimization_barrier(
        (chunks_b, down_before, down_after)
    )
    got_b = send(chunks_b[1:], along_y)
    pre_a, *chunks_a = back((cut, chans), pre_b, mask)

    grads, down_band = call(
        grad_kernel,
        (sd((56, chans), F32), sd((tiles, height + 6, span, LANES), F32)),
        [VM] * 4 + [ANY],
        [pltpu.VMEM((2 * tiles, KS * KS + 1, 8, LANES), F32)],
        "grads",
    )(down, down_before, down_after, band, pre_a)
    image_grad, small = call(
        image_kernel,
        (sd((rows, in_chans, cols), BF16), sd((56, chans), BF16)),
        [VM] * 7,
        [column, sort, pltpu.VMEM((4 * in_chans, pixels), F32), pltpu.VMEM((56, chans), F32)],
        "image",
    )(pre_b, pre_a, weight, normed, rstd, layer_norm_gain, grads)
    image_grad = jnp.transpose(image_grad, (0, 2, 1))
    features = call(
        front_kernel,
        sd((height, width, chans), BF16),
        [VM] * 4 + [ANY],
        [pltpu.VMEM((tiles, height, width, LANES), F32)],
        "front",
    )(down_band, taps, depth_bias, mask, small)

    def middle(own, got, size, order):
        return call(
            middle_kernel,
            (sd((share, size), BF16),) * 4,
            [SM] + [VM] * 4 + [ANY],
            [],
            "middle",
        )(place_z, own, *got, order)

    chunks_a[3], _ = lax.optimization_barrier((chunks_a[3], features))
    got_a = send(chunks_a[1:], along_y)
    small, *got_b = lax.optimization_barrier((small, *got_b))
    got_t = send([small] * 3, along_y)
    parts_b = middle(chunks_b[0], got_b, cut, features)
    last_b = send(parts_b[1:], along_z)
    small, *got_t = lax.optimization_barrier((small, *got_t, last_b[0]))[:4]
    small = sum_four(small, *got_t).astype(BF16)
    got_t = send([small] * 3, along_z)
    parts_a = middle(chunks_a[0], got_a, chans - cut, parts_b[0])
    last_a = send(parts_a[1:], along_z)
    down_weight_grad, gain_grad, bias_grad, kernel_grad, depth_bias_grad = call(
        last_kernel,
        (
            sd((share, chans), F32),
            sd((in_chans,), F32),
            sd((chans,), F32),
            sd((KS * KS, chans), F32),
            sd((chans,), F32),
        ),
        [VM] * 12,
        [],
        "last",
    )(parts_b[0], *last_b, parts_a[0], *last_a, small, *got_t)
    return (
        features,
        image_grad,
        down_weight_grad,
        gain_grad,
        bias_grad,
        kernel_grad,
        depth_bias_grad,
    )


def solution(mesh):
    placed = (
        P(("group", "rows"), None, None),
        P(("group", "rows"), None),
        P(),
        P(),
        P(),
        P(),
        P(),
        P(("group", "rows"), None, None),
    )
    return jax.shard_map(
        body,
        mesh=mesh,
        in_specs=placed,
        out_specs=(
            P(("group", "rows"), None, None),
            P(("group", "rows"), None, None),
            P(("group", "rows"), None),
            P("group"),
            P("group"),
            P("group", None),
            P("group"),
        ),
        check_vma=False,
    )
```

time: 101 us -> 84.6 us (0.84)
  waiting for transfers between devices: 37.6 us -> 10.5 us
  starting transfers between devices: 30.4 us -> 45.1 us
  local copies, waits for them, and re-layouts: 9.12 us -> 3.1 us
  Pallas kernels: 20.5 us -> 24.2 us
  other arithmetic: 1.71 us -> 0.05 us
    ppermute x15 -> x21, waiting for transfers between devices: 37.6 us -> 10.5 us  [the longest x18 9.38 us: send(): lax.ppermute(value, 'rows', pair)]
    ppermute x15 -> x21, starting transfers between devices: 26.9 us -> 41.6 us  [the longest x18 34.5 us: send(): lax.ppermute(value, 'rows', pair)]
    unnamed x36 -> x24, local copies, waits for them, and re-layouts: 9.07 us -> 3.1 us
    pallas_call x4 -> x9, Pallas kernels: 16.7 us -> 18.8 us  [the longest x2 4.6 us: back(): call(functools.partial(back_kernel, here[0] // LANES), (sd((pixels, size)...]
    convert_element_type x2 -> x1, other arithmetic: 1.71 us -> 0.05 us  [body(): small = sum_four(small, *got_t).astype(BF16)]
    pallas_call x1, Pallas kernels: 2.98 us -> 4.57 us  [body(): call(reduce_kernel, (sd((4 * in_chans, pixels), BF16), sd((4 * in_chans,...]
  transfers between devices with their start and end apart: 16 -> 22, of which waited for: 5 -> 6; matrix products, arithmetic and copies ran while one was open for 2% -> 0% of each run, Pallas kernels for 13% -> 26%
where the time goes in v3:
time: 84.6 us; the launch traced here: 83.8 us
  starting transfers between devices  45.1 us (53%)
  Pallas kernels  24.2 us (29%)
  waiting for transfers between devices  10.5 us (12%)
  local copies, waits for them, and re-layouts  3.1 us (4%)
  between operations  0.88 us (1%)
    ppermute x18, starting transfers between devices, send(): lax.ppermute(value, 'rows', pair)  34.5 us
    ppermute x18, waiting for transfers between devices, send(): lax.ppermute(value, 'rows', pair)  9.38 us
    pallas_call x2, Pallas kernels, back(): call(functools.partial(back_kernel, here[0] // LANES), (sd((pixels, size)...  4.6 us
    pallas_call x1, Pallas kernels, body(): call(reduce_kernel, (sd((4 * in_chans, pixels), BF16), sd((4 * in_chans,...  4.57 us
    ppermute x1, starting transfers between devices, body(): down_before = lax.ppermute(down_last, 'rows', up)  4.56 us
    pallas_call x1, Pallas kernels, body(): call(front_kernel, sd((height, width, chans), BF16), [VM] * 4 + [ANY], [p...  3.73 us
    ppermute x1, starting transfers between devices, body(): cot_before = lax.ppermute(cot_last, 'rows', up)  3.5 us
    pallas_call x1, Pallas kernels, body(): call(grad_kernel, (sd((56, chans), F32), sd((tiles, height + 6, span, LAN...  3.15 us
  transfers between devices with their start and end apart: 22, of which 6 were waited for; matrix products, arithmetic and copies ran while one was open for 0% of the time, Pallas kernels for 26%

profile of v3, /device:TPU:2, one launch (start us, length us, event | category | flops | bytes accessed | tf_op | source)
XLA Modules:
  0.0 83.8 jit_solution(348503011883211806)
XLA Ops:
  0.7 2.0 %edge.1 = (bf16[3,64,704]{2,1,0:T(8,128)(2,1)}, bf16[3,64,704]{2,1,0:T(8,128)(2,1)}, f32[64,128]{1,0:T(8,128)}) custom-call(s32[1,16]{1,0:T(1,128)} %vis_in.1, bf16[4,64,704]{2,1,0:T(8,128)(2,1)} %cot_in.3), custom_call_target="tpu_custom_call" | custom-call | flops 1000000 | bytes 20000000 | tf_op jit(solution)/shard_map/edge/pallas_call | solution.py:399
  2.6 3.5 %collective-permute-start = (bf16[3,64,704]{2,1,0:T(8,128)(2,1)}, bf16[3,64,704]{2,1,0:T(8,128)(2,1)S(1)}, u32[]{:S(2)}, u32[]{:S(2)}) collective-permute-start(bf16[3,64,704]{2,1,0:T(8,128)(2,1)} %get-tuple-element.64), channel_id=1, source_target_pairs={{0,1},{1,2},{2,3},{3,4},{4,5},{5,6},{6,7},{7,8},{8,9},{9,10},{10,1... | collective-permute-start | bytes 811016 | tf_op jit(solution)/shard_map/ppermute | solution.py:412
  6.1 1.3 %collective-permute-start.1 = (bf16[3,64,704]{2,1,0:T(8,128)(2,1)}, bf16[3,64,704]{2,1,0:T(8,128)(2,1)S(1)}, u32[]{:S(2)}, u32[]{:S(2)}) collective-permute-start(bf16[3,64,704]{2,1,0:T(8,128)(2,1)} %get-tuple-element.62.order), channel_id=1, source_target_pairs={{1,0},{2,1},{3,2},{4,3},{5,4},{6,5},{7,6},{8,7},{9,8},{10,9},{11,1... | collective-permute-start | bytes 811016 | tf_op jit(solution)/shard_map/ppermute | solution.py:413
  7.4 4.6 %reduce.1 = (bf16[1408,256]{1,0:T(8,128)(2,1)}, bf16[1408,256]{1,0:T(8,128)(2,1)}, f32[8,256]{1,0:T(8,128)}, bf16[4,64,704]{2,1,0:T(8,128)(2,1)}, bf16[3,64,704]...) custom-call(bf16[8,352,128]{2,1,0:T(8,128)(2,1)} %bitcast.7, f32[352]{0:T(512)} %gain.1, bf16[704,1408]{1,0:T(8,128)(2,1)} %bitcast.5, ...), custom_call_target="tpu_custom_call" | custom-call | flops 1000000 | bytes 20000000 | tf_op jit(solution)/shard_map/reduce/pallas_call | solution.py:417
  12.0 4.6 %collective-permute-start.2 = (bf16[3,64,704]{2,1,0:T(8,128)(2,1)}, bf16[3,64,704]{2,1,0:T(8,128)(2,1)S(1)}, u32[]{:S(2)}, u32[]{:S(2)}) collective-permute-start(bf16[3,64,704]{2,1,0:T(8,128)(2,1)} %get-tuple-element.74), channel_id=1, source_target_pairs={{0,1},{1,2},{2,3},{3,4},{4,5},{5,6},{6,7},{7,8},{8,9},{9,10},{10,1... | collective-permute-start | bytes 811016 | tf_op jit(solution)/shard_map/ppermute | solution.py:441
  16.6 1.3 %collective-permute-start.3 = (bf16[3,64,704]{2,1,0:T(8,128)(2,1)}, bf16[3,64,704]{2,1,0:T(8,128)(2,1)S(1)}, u32[]{:S(2)}, u32[]{:S(2)}) collective-permute-start(bf16[3,64,704]{2,1,0:T(8,128)(2,1)} %get-tuple-element.65.order), channel_id=1, source_target_pairs={{1,0},{2,1},{3,2},{4,3},{5,4},{6,5},{7,6},{8,7},{9,8},{10,9},{11,1... | collective-permute-start | bytes 811016 | tf_op jit(solution)/shard_map/ppermute | solution.py:442
  17.9 1.0 %copy-done.7 = bf16[3,64,704]{2,1,0:T(8,128)(2,1)S(1)} copy-done((bf16[3,64,704]{2,1,0:T(8,128)(2,1)S(1)}, bf16[3,64,704]{2,1,0:T(8,128)(2,1)}, u32[]{:S(2)}) %copy-start.7) | copy-done | bytes 270360
  18.9 2.7 %own.1 = (f32[6,4,80,128]{3,2,1,0:T(8,128)S(1)}, f32[6,49,8,128]{3,2,1,0:T(8,128)S(1)}, f32[6,4,64,128]{3,2,1,0:T(8,128)S(1)}) custom-call(bf16[4,64,704]{2,1,0:T(8,128)(2,1)S(1)} %copy-done.3, f32[49,704]{1,0:T(8,128)S(1)} %copy-done.8, f32[64,128]{1,0:T(8,128)S(1)} %copy-done.2, bf16[3,64,704]{2,1,0:T(8,128)(2,1)S(1)} %copy-done.7), custom_call_target="tpu_custom_call" | custom-call | flops 1000000 | bytes 100000 | tf_op jit(solution)/shard_map/own/pallas_call | solution.py:444
  21.6 1.1 %copy-done.1 = bf16[1408,256]{1,0:T(8,128)(2,1)S(1)} copy-done((bf16[1408,256]{1,0:T(8,128)(2,1)S(1)}, bf16[1408,256]{1,0:T(8,128)(2,1)}, u32[]{:S(2)}) %copy-start.1) | copy-done | bytes 720920
  22.7 2.8 %back.2 = (bf16[256,512]{1,0:T(8,128)(2,1)S(1)}, bf16[4,88,512]{2,1,0:T(8,128)(2,1)S(1)}, bf16[4,88,512]{2,1,0:T(8,128)(2,1)S(1)}, bf16[4,88,512]{2,1,0:T(8,128)(2,1)}, bf16[4,88,512]{2,1,0:T(8,128)(2,1)}) custom-call(s32[1]{0:T(128)} %bitcast.2.place, bf16[3,64,704]{2,1,0:T(8,128)(2,1)S(1)} %collective-permute-done.before, ...), custom_call_target="tpu_custom_call" | custom-call | flops 1000000 | bytes 100000 | tf_op jit(solution)/shard_map/back/pallas_call | solution.py:463
  25.5 1.1 %collective-permute-done.3.after = bf16[3,64,704]{2,1,0:T(8,128)(2,1)S(1)} collective-permute-done((bf16[3,64,704]{2,1,0:T(8,128)(2,1)}, bf16[3,64,704]{2,1,0:T(8,128)(2,1)S(1)}, u32[]{:S(2)}, u32[]{:S(2)}) %collective-permute-start.3) | collective-permute-done | bytes 270368 | tf_op jit(solution)/shard_map/ppermute | solution.py:442
  26.6 1.6 %collective-permute-start.4 = (bf16[4,88,512]{2,1,0:T(8,128)(2,1)S(1)}, bf16[4,88,512]{2,1,0:T(8,128)(2,1)S(1)}, u32[]{:S(2)}, u32[]{:S(2)}) collective-permute-start(bf16[4,88,512]{2,1,0:T(8,128)(2,1)S(1)} %get-tuple-element.86), channel_id=1, source_target_pairs={{0,1},{1,2},{2,3},{3,0},{4,5},{5,6},{6,7},{7,4},{8,9},{9,10},{10,1... | collective-permute-start | bytes 1081352 | tf_op jit(solution)/shard_map/ppermute | solution.py:375
  28.2 7.1 %collective-permute-start.5 = (bf16[4,88,512]{2,1,0:T(8,128)(2,1)}, bf16[4,88,512]{2,1,0:T(8,128)(2,1)S(1)}, u32[]{:S(2)}, u32[]{:S(2)}) collective-permute-start(bf16[4,88,512]{2,1,0:T(8,128)(2,1)} %get-tuple-element.87), channel_id=1, source_target_pairs={{0,2},{1,3},{2,0},{3,1},{4,6},{5,7},{6,4},{7,5},{8,10},{9,11},{10,... | collective-permute-start | bytes 1081352 | tf_op jit(solution)/shard_map/ppermute | solution.py:375
  35.3 1.8 %back.3 = (bf16[256,192]{1,0:T(8,128)(2,1)S(1)}, bf16[4,88,192]{2,1,0:T(8,128)(2,1)S(1)}, bf16[4,88,192]{2,1,0:T(8,128)(2,1)}, bf16[4,88,192]{2,1,0:T(8,128)(2,1)}, bf16[4,88,192]{2,1,0:T(8,128)(2,1)S(1)}) custom-call(s32[1]{0:T(128)} %bitcast.2.place, bf16[3,64,704]{2,1,0:T(8,128)(2,1)S(1)} %collective-permute-done.before, ...), custom_call_target="tpu_custom_call" | custom-call | flops 1000000 | bytes 100000 | tf_op jit(solution)/shard_map/back/pallas_call | solution.py:463
  37.1 2.1 %collective-permute-start.10 = (bf16[4,88,192]{2,1,0:T(8,128)(2,1)}, bf16[4,88,192]{2,1,0:T(8,128)(2,1)S(1)}, u32[]{:S(2)}, u32[]{:S(2)}) collective-permute-start(bf16[4,88,192]{2,1,0:T(8,128)(2,1)} %get-tuple-element.97), channel_id=1, source_target_pairs={{0,1},{1,2},{2,3},{3,0},{4,5},{5,6},{6,7},{7,4},{8,9},{9,10},{10,1... | collective-permute-start | bytes 405512 | tf_op jit(solution)/shard_map/ppermute | solution.py:375
  39.2 3.1 %grads.1 = (f32[56,704]{1,0:T(8,128)S(1)}, f32[6,10,80,128]{3,2,1,0:T(8,128)S(1)}) custom-call(bf16[4,64,704]{2,1,0:T(8,128)(2,1)S(1)} %copy-done.6, bf16[3,64,704]{2,1,0:T(8,128)(2,1)S(1)} %collective-permute-done.2.before, bf16[3,64,704]{2,1,0:T(8,128)(2,1)S(1)} %collective-permute-done.3.after, f32[6,4,80,128]{3,2,1,0:T(8,128)S(1)} %get-tuple-element.66.band.cots, ...), custom_call_target="tpu_custom_call" | custom-call | flops 1000000 | bytes 100000 | tf_op jit(solution)/shard_map/grads/pallas_call | solution.py:482
  42.4 2.5 %image.1 = (bf16[8,352,128]{2,1,0:T(8,128)(2,1)}, bf16[56,704]{1,0:T(8,128)(2,1)S(1)}) custom-call(bf16[256,512]{1,0:T(8,128)(2,1)S(1)} %get-tuple-element.77.order.pre_b, bf16[256,192]{1,0:T(8,128)(2,1)S(1)} %get-tuple-element.78.order.pre_a, bf16[704,1408]{1,0:T(8,128)(2,1)S(1)} %bitcast.6, bf16[1408,256]{1,0:T(8,128)(2,1)S(1)} %copy-done.5, ...), custom_call_target="tpu_custom_call" | custom-call | flops 1000000 | bytes 100000 | tf_op jit(solution)/shard_map/image/pallas_call | solution.py:489
  44.8 3.7 %front.1.order = bf16[4,64,704]{2,1,0:T(8,128)(2,1)} custom-call(f32[6,10,80,128]{3,2,1,0:T(8,128)S(1)} %get-tuple-element.79.band, f32[6,49,8,128]{3,2,1,0:T(8,128)S(1)} %get-tuple-element.67.taps, f32[704]{0:T(1024)S(1)} %copy-done.11, f32[64,128]{1,0:T(8,128)S(1)} %copy-done.2, bf16[56,704]{1,0:T(8,128)(2,1)S(1)} %get-tuple-element.106.order), custom_call_target="tpu_custom_call" | custom-call | flops 1000000 | bytes 100000 | tf_op jit(solution)/shard_map/front/pallas_call | solution.py:497
  48.6 2.8 %collective-permute-start.12 = (bf16[4,88,192]{2,1,0:T(8,128)(2,1)S(1)}, bf16[4,88,192]{2,1,0:T(8,128)(2,1)S(1)}, u32[]{:S(2)}, u32[]{:S(2)}) collective-permute-start(bf16[4,88,192]{2,1,0:T(8,128)(2,1)S(1)} %get-tuple-element.100), channel_id=1, source_target_pairs={{0,3},{1,0},{2,1},{3,2},{4,7},{5,4},{6,5},{7,6},{8,11},{9,8},{10,9... | collective-permute-start | bytes 405512 | tf_op jit(solution)/shard_map/ppermute | solution.py:375
  51.3 1.1 %collective-permute-done.5.c2 = bf16[4,88,512]{2,1,0:T(8,128)(2,1)S(1)} collective-permute-done((bf16[4,88,512]{2,1,0:T(8,128)(2,1)}, bf16[4,88,512]{2,1,0:T(8,128)(2,1)S(1)}, u32[]{:S(2)}, u32[]{:S(2)}) %collective-permute-start.5) | collective-permute-done | bytes 360480 | tf_op jit(solution)/shard_map/ppermute | solution.py:375
  52.4 1.0 %copy-done.4 = bf16[4,64,704]{2,1,0:T(8,128)(2,1)S(1)} copy-done((bf16[4,64,704]{2,1,0:T(8,128)(2,1)S(1)}, bf16[4,64,704]{2,1,0:T(8,128)(2,1)}, u32[]{:S(2)}) %copy-start.4) | copy-done | bytes 360472
  53.6 2.0 %collective-permute-start.7 = (bf16[88,512]{1,0:T(8,128)(2,1)S(1)}, bf16[88,512]{1,0:T(8,128)(2,1)S(1)}, u32[]{:S(2)}, u32[]{:S(2)}) collective-permute-start(bf16[88,512]{1,0:T(8,128)(2,1)S(1)} %get-tuple-element.93), channel_id=1, source_target_pairs={{0,4},{1,5},{2,6},{3,7},{4,8},{5,9},{6,10},{7,11},{8,12},{9,13},{1... | collective-permute-start | bytes 270344 | tf_op jit(solution)/shard_map/ppermute | solution.py:375
  55.6 1.8 %collective-permute-start.18 = (bf16[56,704]{1,0:T(8,128)(2,1)S(1)}, bf16[56,704]{1,0:T(8,128)(2,1)S(1)}, u32[]{:S(2)}, u32[]{:S(2)}) collective-permute-start(bf16[56,704]{1,0:T(8,128)(2,1)S(1)} %get-tuple-element.106.order), channel_id=1, source_target_pairs={{0,3},{1,0},{2,1},{3,2},{4,7},{5,4},{6,5},{7,6},{8,11},{9,8},{10,9... | collective-permute-start | bytes 236552 | tf_op jit(solution)/shard_map/ppermute | solution.py:375
  57.4 0.9 %collective-permute-start.16 = (bf16[56,704]{1,0:T(8,128)(2,1)S(1)}, bf16[56,704]{1,0:T(8,128)(2,1)S(1)}, u32[]{:S(2)}, u32[]{:S(2)}) collective-permute-start(bf16[56,704]{1,0:T(8,128)(2,1)S(1)} %get-tuple-element.106.order), channel_id=1, source_target_pairs={{0,1},{1,2},{2,3},{3,0},{4,5},{5,6},{6,7},{7,4},{8,9},{9,10},{10,1... | collective-permute-start | bytes 236552 | tf_op jit(solution)/shard_map/ppermute | solution.py:375
  58.3 6.9 %collective-permute-start.8 = (bf16[88,512]{1,0:T(8,128)(2,1)S(1)}, bf16[88,512]{1,0:T(8,128)(2,1)S(1)}, u32[]{:S(2)}, u32[]{:S(2)}) collective-permute-start(bf16[88,512]{1,0:T(8,128)(2,1)S(1)} %get-tuple-element.94), channel_id=1, source_target_pairs={{0,8},{1,9},{2,10},{3,11},{4,12},{5,13},{6,14},{7,15},{8,0},{9,1},... | collective-permute-start | bytes 270344 | tf_op jit(solution)/shard_map/ppermute | solution.py:375
  65.6 1.8 %collective-permute-start.13 = (bf16[88,192]{1,0:T(8,128)(2,1)S(1)}, bf16[88,192]{1,0:T(8,128)(2,1)S(1)}, u32[]{:S(2)}, u32[]{:S(2)}) collective-permute-start(bf16[88,192]{1,0:T(8,128)(2,1)S(1)} %get-tuple-element.102), channel_id=1, source_target_pairs={{0,4},{1,5},{2,6},{3,7},{4,8},{5,9},{6,10},{7,11},{8,12},{9,13},{1... | collective-permute-start | bytes 101384 | tf_op jit(solution)/shard_map/ppermute | solution.py:375
  67.4 3.4 %collective-permute-start.14 = (bf16[88,192]{1,0:T(8,128)(2,1)S(1)}, bf16[88,192]{1,0:T(8,128)(2,1)S(1)}, u32[]{:S(2)}, u32[]{:S(2)}) collective-permute-start(bf16[88,192]{1,0:T(8,128)(2,1)S(1)} %get-tuple-element.103), channel_id=1, source_target_pairs={{0,8},{1,9},{2,10},{3,11},{4,12},{5,13},{6,14},{7,15},{8,0},{9,1},... | collective-permute-start | bytes 101384 | tf_op jit(solution)/shard_map/ppermute | solution.py:375
  71.6 0.8 collective-permute-start.21
  72.4 3.4 %collective-permute-done.14.a2 = bf16[88,192]{1,0:T(8,128)(2,1)S(1)} collective-permute-done((bf16[88,192]{1,0:T(8,128)(2,1)S(1)}, bf16[88,192]{1,0:T(8,128)(2,1)S(1)}, u32[]{:S(2)}, u32[]{:S(2)}) %collective-permute-start.14) | collective-permute-done | bytes 33824 | tf_op jit(solution)/shard_map/ppermute | solution.py:375
  76.6 2.9 %collective-permute-start.19 = (bf16[56,704]{1,0:T(8,128)(2,1)S(1)}, bf16[56,704]{1,0:T(8,128)(2,1)S(1)}, u32[]{:S(2)}, u32[]{:S(2)}) collective-permute-start(bf16[56,704]{1,0:T(8,128)(2,1)S(1)} %add_convert_fusion.t0), channel_id=1, source_target_pairs={{0,4},{1,5},{2,6},{3,7},{4,8},{5,9},{6,10},{7,11},{8,12},{9,13},{1... | collective-permute-start | bytes 236552 | tf_op jit(solution)/shard_map/ppermute | solution.py:375
  79.5 3.5 %collective-permute-done.20.t2 = bf16[56,704]{1,0:T(8,128)(2,1)S(1)} collective-permute-done((bf16[56,704]{1,0:T(8,128)(2,1)S(1)}, bf16[56,704]{1,0:T(8,128)(2,1)S(1)}, u32[]{:S(2)}, u32[]{:S(2)}) %collective-permute-start.20) | collective-permute-done | bytes 78880 | tf_op jit(solution)/shard_map/ppermute | solution.py:375
  83.0 0.8 last.1
  (48 shorter events, 2.2 us)
Async XLA Ops:
  0.6 17.3 %copy-start.3 = (bf16[4,64,704]{2,1,0:T(8,128)(2,1)S(1)}, bf16[4,64,704]{2,1,0:T(8,128)(2,1)}, u32[]{:S(2)}) copy-start(bf16[4,64,704]{2,1,0:T(8,128)(2,1)} %cot_in.3) | copy-start | bytes 1081348
  0.6 17.3 %copy-start.8 = (f32[49,704]{1,0:T(8,128)S(1)}, f32[49,704]{1,0:T(8,128)}, u32[]{:S(2)}) copy-start(f32[49,704]{1,0:T(8,128)} %kernel_in.1) | copy-start | bytes 413956
  2.6 15.3 %copy-start.2 = (f32[64,128]{1,0:T(8,128)S(1)}, f32[64,128]{1,0:T(8,128)}, u32[]{:S(2)}) copy-start(f32[64,128]{1,0:T(8,128)} %get-tuple-element.61.mask.order.order_too) | copy-start | bytes 98308
  2.6 18.9 %collective-permute-start = (bf16[3,64,704]{2,1,0:T(8,128)(2,1)}, bf16[3,64,704]{2,1,0:T(8,128)(2,1)S(1)}, u32[]{:S(2)}, u32[]{:S(2)}) collective-permute-start(bf16[3,64,704]{2,1,0:T(8,128)(2,1)} %get-tuple-element.64), channel_id=1, source_target_pairs={{0,1},{1,2},{2,3},{3,4},{4,5},{5,6},{6,7},{7,8},{8,9},{9,10},{10,1... | collective-permute-start | bytes 811016 | tf_op jit(solution)/shard_map/ppermute | solution.py:412
  6.1 15.5 %collective-permute-start.1 = (bf16[3,64,704]{2,1,0:T(8,128)(2,1)}, bf16[3,64,704]{2,1,0:T(8,128)(2,1)S(1)}, u32[]{:S(2)}, u32[]{:S(2)}) collective-permute-start(bf16[3,64,704]{2,1,0:T(8,128)(2,1)} %get-tuple-element.62.order), channel_id=1, source_target_pairs={{1,0},{2,1},{3,2},{4,3},{5,4},{6,5},{7,6},{8,7},{9,8},{10,9},{11,1... | collective-permute-start | bytes 811016 | tf_op jit(solution)/shard_map/ppermute | solution.py:413
  12.0 13.5 %collective-permute-start.2 = (bf16[3,64,704]{2,1,0:T(8,128)(2,1)}, bf16[3,64,704]{2,1,0:T(8,128)(2,1)S(1)}, u32[]{:S(2)}, u32[]{:S(2)}) collective-permute-start(bf16[3,64,704]{2,1,0:T(8,128)(2,1)} %get-tuple-element.74), channel_id=1, source_target_pairs={{0,1},{1,2},{2,3},{3,4},{4,5},{5,6},{6,7},{7,8},{8,9},{9,10},{10,1... | collective-permute-start | bytes 811016 | tf_op jit(solution)/shard_map/ppermute | solution.py:441
  16.6 10.0 %collective-permute-start.3 = (bf16[3,64,704]{2,1,0:T(8,128)(2,1)}, bf16[3,64,704]{2,1,0:T(8,128)(2,1)S(1)}, u32[]{:S(2)}, u32[]{:S(2)}) collective-permute-start(bf16[3,64,704]{2,1,0:T(8,128)(2,1)} %get-tuple-element.65.order), channel_id=1, source_target_pairs={{1,0},{2,1},{3,2},{4,3},{5,4},{6,5},{7,6},{8,7},{9,8},{10,9},{11,1... | collective-permute-start | bytes 811016 | tf_op jit(solution)/shard_map/ppermute | solution.py:442
  21.6 1.1 %copy-start.1 = (bf16[1408,256]{1,0:T(8,128)(2,1)S(1)}, bf16[1408,256]{1,0:T(8,128)(2,1)}, u32[]{:S(2)}) copy-start(bf16[1408,256]{1,0:T(8,128)(2,1)} %get-tuple-element.69.patches) | copy-start | bytes 2162692
  26.6 22.0 %collective-permute-start.4 = (bf16[4,88,512]{2,1,0:T(8,128)(2,1)S(1)}, bf16[4,88,512]{2,1,0:T(8,128)(2,1)S(1)}, u32[]{:S(2)}, u32[]{:S(2)}) collective-permute-start(bf16[4,88,512]{2,1,0:T(8,128)(2,1)S(1)} %get-tuple-element.86), channel_id=1, source_target_pairs={{0,1},{1,2},{2,3},{3,0},{4,5},{5,6},{6,7},{7,4},{8,9},{9,10},{10,1... | collective-permute-start | bytes 1081352 | tf_op jit(solution)/shard_map/ppermute | solution.py:375
  28.2 24.2 %collective-permute-start.5 = (bf16[4,88,512]{2,1,0:T(8,128)(2,1)}, bf16[4,88,512]{2,1,0:T(8,128)(2,1)S(1)}, u32[]{:S(2)}, u32[]{:S(2)}) collective-permute-start(bf16[4,88,512]{2,1,0:T(8,128)(2,1)} %get-tuple-element.87), channel_id=1, source_target_pairs={{0,2},{1,3},{2,0},{3,1},{4,6},{5,7},{6,4},{7,5},{8,10},{9,11},{10,... | collective-permute-start | bytes 1081352 | tf_op jit(solution)/shard_map/ppermute | solution.py:375
  35.3 17.1 %collective-permute-start.6 = (bf16[4,88,512]{2,1,0:T(8,128)(2,1)}, bf16[4,88,512]{2,1,0:T(8,128)(2,1)S(1)}, u32[]{:S(2)}, u32[]{:S(2)}) collective-permute-start(bf16[4,88,512]{2,1,0:T(8,128)(2,1)} %get-tuple-element.88), channel_id=1, source_target_pairs={{0,3},{1,0},{2,1},{3,2},{4,7},{5,4},{6,5},{7,6},{8,11},{9,8},{10,9... | collective-permute-start | bytes 1081352 | tf_op jit(solution)/shard_map/ppermute | solution.py:375
  35.3 3.9 %copy-start.6 = (bf16[4,64,704]{2,1,0:T(8,128)(2,1)S(1)}, bf16[4,64,704]{2,1,0:T(8,128)(2,1)}, u32[]{:S(2)}) copy-start(bf16[4,64,704]{2,1,0:T(8,128)(2,1)} %get-tuple-element.63.down) | copy-start | bytes 1081348
  35.3 7.0 %copy-start.5 = (bf16[1408,256]{1,0:T(8,128)(2,1)S(1)}, bf16[1408,256]{1,0:T(8,128)(2,1)}, u32[]{:S(2)}) copy-start(bf16[1408,256]{1,0:T(8,128)(2,1)} %get-tuple-element.80.normed) | copy-start | bytes 2162692
  37.1 5.3 %copy-start = (bf16[1408,704]{0,1:T(8,128)(2,1)S(1)}, bf16[1408,704]{0,1:T(8,128)(2,1)}, u32[]{:S(2)}) copy-start(bf16[1408,704]{0,1:T(8,128)(2,1)} %param.11) | copy-start | bytes 5947396
  37.1 5.3 %copy-start.9 = (f32[8,256]{1,0:T(8,128)S(1)}, f32[8,256]{1,0:T(8,128)}, u32[]{:S(2)}) copy-start(f32[8,256]{1,0:T(8,128)} %get-tuple-element.81.rstd) | copy-start | bytes 24580
  37.1 5.3 %copy-start.10 = (f32[352]{0:T(512)S(1)}, f32[352]{0:T(512)}, u32[]{:S(2)}) copy-start(f32[352]{0:T(512)} %gain.1) | copy-start | bytes 4228
  37.1 20.3 %collective-permute-start.10 = (bf16[4,88,192]{2,1,0:T(8,128)(2,1)}, bf16[4,88,192]{2,1,0:T(8,128)(2,1)S(1)}, u32[]{:S(2)}, u32[]{:S(2)}) collective-permute-start(bf16[4,88,192]{2,1,0:T(8,128)(2,1)} %get-tuple-element.97), channel_id=1, source_target_pairs={{0,1},{1,2},{2,3},{3,0},{4,5},{5,6},{6,7},{7,4},{8,9},{9,10},{10,1... | collective-permute-start | bytes 405512 | tf_op jit(solution)/shard_map/ppermute | solution.py:375
  39.1 18.3 %collective-permute-start.11 = (bf16[4,88,192]{2,1,0:T(8,128)(2,1)}, bf16[4,88,192]{2,1,0:T(8,128)(2,1)S(1)}, u32[]{:S(2)}, u32[]{:S(2)}) collective-permute-start(bf16[4,88,192]{2,1,0:T(8,128)(2,1)} %get-tuple-element.98), channel_id=1, source_target_pairs={{0,2},{1,3},{2,0},{3,1},{4,6},{5,7},{6,4},{7,5},{8,10},{9,11},{10,... | collective-permute-start | bytes 405512 | tf_op jit(solution)/shard_map/ppermute | solution.py:375
  42.3 2.5 %copy-start.11 = (f32[704]{0:T(1024)S(1)}, f32[704]{0:T(1024)}, u32[]{:S(2)}) copy-start(f32[704]{0:T(1024)} %bias.1) | copy-start | bytes 8452
  48.6 9.7 %collective-permute-start.12 = (bf16[4,88,192]{2,1,0:T(8,128)(2,1)S(1)}, bf16[4,88,192]{2,1,0:T(8,128)(2,1)S(1)}, u32[]{:S(2)}, u32[]{:S(2)}) collective-permute-start(bf16[4,88,192]{2,1,0:T(8,128)(2,1)S(1)} %get-tuple-element.100), channel_id=1, source_target_pairs={{0,3},{1,0},{2,1},{3,2},{4,7},{5,4},{6,5},{7,6},{8,11},{9,8},{10,9... | collective-permute-start | bytes 405512 | tf_op jit(solution)/shard_map/ppermute | solution.py:375
  53.6 17.2 %collective-permute-start.7 = (bf16[88,512]{1,0:T(8,128)(2,1)S(1)}, bf16[88,512]{1,0:T(8,128)(2,1)S(1)}, u32[]{:S(2)}, u32[]{:S(2)}) collective-permute-start(bf16[88,512]{1,0:T(8,128)(2,1)S(1)} %get-tuple-element.93), channel_id=1, source_target_pairs={{0,4},{1,5},{2,6},{3,7},{4,8},{5,9},{6,10},{7,11},{8,12},{9,13},{1... | collective-permute-start | bytes 270344 | tf_op jit(solution)/shard_map/ppermute | solution.py:375
  55.6 9.7 %collective-permute-start.18 = (bf16[56,704]{1,0:T(8,128)(2,1)S(1)}, bf16[56,704]{1,0:T(8,128)(2,1)S(1)}, u32[]{:S(2)}, u32[]{:S(2)}) collective-permute-start(bf16[56,704]{1,0:T(8,128)(2,1)S(1)} %get-tuple-element.106.order), channel_id=1, source_target_pairs={{0,3},{1,0},{2,1},{3,2},{4,7},{5,4},{6,5},{7,6},{8,11},{9,8},{10,9... | collective-permute-start | bytes 236552 | tf_op jit(solution)/shard_map/ppermute | solution.py:375
  57.4 8.2 %collective-permute-start.17 = (bf16[56,704]{1,0:T(8,128)(2,1)S(1)}, bf16[56,704]{1,0:T(8,128)(2,1)S(1)}, u32[]{:S(2)}, u32[]{:S(2)}) collective-permute-start(bf16[56,704]{1,0:T(8,128)(2,1)S(1)} %get-tuple-element.106.order), channel_id=1, source_target_pairs={{0,2},{1,3},{2,0},{3,1},{4,6},{5,7},{6,4},{7,5},{8,10},{9,11},{10,... | collective-permute-start | bytes 236552 | tf_op jit(solution)/shard_map/ppermute | solution.py:375
  57.4 10.0 %collective-permute-start.16 = (bf16[56,704]{1,0:T(8,128)(2,1)S(1)}, bf16[56,704]{1,0:T(8,128)(2,1)S(1)}, u32[]{:S(2)}, u32[]{:S(2)}) collective-permute-start(bf16[56,704]{1,0:T(8,128)(2,1)S(1)} %get-tuple-element.106.order), channel_id=1, source_target_pairs={{0,1},{1,2},{2,3},{3,0},{4,5},{5,6},{6,7},{7,4},{8,9},{9,10},{10,1... | collective-permute-start | bytes 236552 | tf_op jit(solution)/shard_map/ppermute | solution.py:375
  58.3 21.2 %collective-permute-start.8 = (bf16[88,512]{1,0:T(8,128)(2,1)S(1)}, bf16[88,512]{1,0:T(8,128)(2,1)S(1)}, u32[]{:S(2)}, u32[]{:S(2)}) collective-permute-start(bf16[88,512]{1,0:T(8,128)(2,1)S(1)} %get-tuple-element.94), channel_id=1, source_target_pairs={{0,8},{1,9},{2,10},{3,11},{4,12},{5,13},{6,14},{7,15},{8,0},{9,1},... | collective-permute-start | bytes 270344 | tf_op jit(solution)/shard_map/ppermute | solution.py:375
  65.3 14.1 %collective-permute-start.9 = (bf16[88,512]{1,0:T(8,128)(2,1)S(1)}, bf16[88,512]{1,0:T(8,128)(2,1)S(1)}, u32[]{:S(2)}, u32[]{:S(2)}) collective-permute-start(bf16[88,512]{1,0:T(8,128)(2,1)S(1)} %get-tuple-element.95), channel_id=1, source_target_pairs={{0,12},{1,13},{2,14},{3,15},{4,0},{5,1},{6,2},{7,3},{8,4},{9,5},{1... | collective-permute-start | bytes 270344 | tf_op jit(solution)/shard_map/ppermute | solution.py:375
  65.6 6.0 %collective-permute-start.13 = (bf16[88,192]{1,0:T(8,128)(2,1)S(1)}, bf16[88,192]{1,0:T(8,128)(2,1)S(1)}, u32[]{:S(2)}, u32[]{:S(2)}) collective-permute-start(bf16[88,192]{1,0:T(8,128)(2,1)S(1)} %get-tuple-element.102), channel_id=1, source_target_pairs={{0,4},{1,5},{2,6},{3,7},{4,8},{5,9},{6,10},{7,11},{8,12},{9,13},{1... | collective-permute-start | bytes 101384 | tf_op jit(solution)/shard_map/ppermute | solution.py:375
  67.4 8.4 %collective-permute-start.14 = (bf16[88,192]{1,0:T(8,128)(2,1)S(1)}, bf16[88,192]{1,0:T(8,128)(2,1)S(1)}, u32[]{:S(2)}, u32[]{:S(2)}) collective-permute-start(bf16[88,192]{1,0:T(8,128)(2,1)S(1)} %get-tuple-element.103), channel_id=1, source_target_pairs={{0,8},{1,9},{2,10},{3,11},{4,12},{5,13},{6,14},{7,15},{8,0},{9,1},... | collective-permute-start | bytes 101384 | tf_op jit(solution)/shard_map/ppermute | solution.py:375
  70.8 5.8 %collective-permute-start.15 = (bf16[88,192]{1,0:T(8,128)(2,1)S(1)}, bf16[88,192]{1,0:T(8,128)(2,1)S(1)}, u32[]{:S(2)}, u32[]{:S(2)}) collective-permute-start(bf16[88,192]{1,0:T(8,128)(2,1)S(1)} %get-tuple-element.104), channel_id=1, source_target_pairs={{0,12},{1,13},{2,14},{3,15},{4,0},{5,1},{6,2},{7,3},{8,4},{9,5},{1... | collective-permute-start | bytes 101384 | tf_op jit(solution)/shard_map/ppermute | solution.py:375
  71.6 7.9 %collective-permute-start.21 = (bf16[56,704]{1,0:T(8,128)(2,1)S(1)}, bf16[56,704]{1,0:T(8,128)(2,1)S(1)}, u32[]{:S(2)}, u32[]{:S(2)}) collective-permute-start(bf16[56,704]{1,0:T(8,128)(2,1)S(1)} %add_convert_fusion.t0), channel_id=1, source_target_pairs={{0,12},{1,13},{2,14},{3,15},{4,0},{5,1},{6,2},{7,3},{8,4},{9,5},{1... | collective-permute-start | bytes 236552 | tf_op jit(solution)/shard_map/ppermute | solution.py:375
  75.8 7.2 %collective-permute-start.20 = (bf16[56,704]{1,0:T(8,128)(2,1)S(1)}, bf16[56,704]{1,0:T(8,128)(2,1)S(1)}, u32[]{:S(2)}, u32[]{:S(2)}) collective-permute-start(bf16[56,704]{1,0:T(8,128)(2,1)S(1)} %add_convert_fusion.t0), channel_id=1, source_target_pairs={{0,8},{1,9},{2,10},{3,11},{4,12},{5,13},{6,14},{7,15},{8,0},{9,1},... | collective-permute-start | bytes 236552 | tf_op jit(solution)/shard_map/ppermute | solution.py:375
  76.6 6.4 %collective-permute-start.19 = (bf16[56,704]{1,0:T(8,128)(2,1)S(1)}, bf16[56,704]{1,0:T(8,128)(2,1)S(1)}, u32[]{:S(2)}, u32[]{:S(2)}) collective-permute-start(bf16[56,704]{1,0:T(8,128)(2,1)S(1)} %add_convert_fusion.t0), channel_id=1, source_target_pairs={{0,4},{1,5},{2,6},{3,7},{4,8},{5,9},{6,10},{7,11},{8,12},{9,13},{1... | collective-permute-start | bytes 236552 | tf_op jit(solution)/shard_map/ppermute | solution.py:375
  (2 other events, 2.0 us)

commit v4 on v3

--- a/solution.py
+++ b/solution.py
@@ -1,4 +1,3 @@
-import functools
 import math
 
 import jax
@@ -17,7 +16,6 @@
 SM = pl.BlockSpec(memory_space=pltpu.SMEM)
 ANY = pl.BlockSpec(memory_space=pl.ANY)
 HBM = pl.BlockSpec(memory_space=pltpu.HBM)
-FIRST = 4
 
 
 def tiles_of(chans):
@@ -59,23 +57,6 @@
     )
 
 
-def edge_kernel(vis_in, cot_in, first, last, mask_out, vis, cot, sems):
-    copies = fetch((vis_in, cot_in), (vis, cot), sems)
-    height, width, chans = cot.shape
-    copies[0].wait()
-    mask = column_mask(vis, width)
-    mask_out[...] = mask
-    copies[1].wait()
-    for t, wd in tiles_of(chans):
-        lanes = lanes_of(t, wd)
-        for p in range(height):
-            row = (cot[p, :, lanes].astype(F32) * mask[:, :wd]).astype(BF16)
-            if p < 3:
-                first[p, :, lanes] = row
-            if p >= height - 3:
-                last[p - (height - 3), :, lanes] = row
-
-
 def sorter(width, back):
     size = 4 * width
     row = lax.broadcasted_iota(jnp.int32, (size, size), 1 if back else 0)
@@ -90,15 +71,28 @@
 
 
 def reduce_kernel(
-    image_in, gain_in, weight_in, bias_in, mask, order,
-    patches, normed, rstd, down, first, last,
-    column, sort, image, gain, weight, bias, sems,
+    vis_in, cot_in, image_in, gain_in, weight_in, bias_in,
+    cot_first, cot_last, mask, patches, normed, rstd, down, first, last,
+    column, sort, vis, cot, image, gain, weight, bias, sems,
 ):
     copies = fetch(
-        (image_in, gain_in, weight_in, bias_in), (image, gain, weight, bias), sems
+        (image_in, gain_in, weight_in, bias_in, vis_in, cot_in),
+        (image, gain, weight, bias, vis, cot),
+        sems,
     )
     rows, chans, cols = image.shape
     height, width = rows // 2, cols // 2
+    copies[4].wait()
+    mask[...] = column_mask(vis, width)
+    copies[5].wait()
+    for t, wd in tiles_of(cot.shape[2]):
+        lanes = lanes_of(t, wd)
+        for p in range(height):
+            row = (cot[p, :, lanes].astype(F32) * mask[:, :wd]).astype(BF16)
+            if p < 3:
+                cot_first[p, :, lanes] = row
+            if p >= height - 3:
+                cot_last[p - (height - 3), :, lanes] = row
     sort[...] = sorter(width, False)
     copies[1].wait()
     gain_column(gain, column)
@@ -136,14 +130,13 @@
                 last[p - (height - 3), :, lanes] = row
 
 
-def fill_band(dst, at, ref, tiles, first=0):
+def fill_band(dst, at, ref, tiles):
     count, width = ref.shape[:2]
     for t, wd in tiles:
-        d = t - first
         for k in range(count):
             if wd < LANES:
-                dst[d, at + k, 8 : 8 + width, wd:LANES] = jnp.zeros((width, LANES - wd), F32)
-            dst[d, at + k, 8 : 8 + width, 0:wd] = ref[k, :, lanes_of(t, wd)].astype(F32)
+                dst[t, at + k, 8 : 8 + width, wd:LANES] = jnp.zeros((width, LANES - wd), F32)
+            dst[t, at + k, 8 : 8 + width, 0:wd] = ref[k, :, lanes_of(t, wd)].astype(F32)
 
 
 def clear_edges(dst):
@@ -153,7 +146,7 @@
     dst[:, :, span - 8 : span, :] = edge
 
 
-def own_kernel(cot_in, kernel_in, mask, order, band, taps, part, cot, kernel, sems):
+def own_kernel(cot_in, kernel_in, mask, band, taps, part, cot, kernel, sems):
     copies = fetch((cot_in, kernel_in), (cot, kernel), sems)
     height, width, chans = cot.shape
     tiles = tiles_of(chans)
@@ -190,33 +183,32 @@
 
 
 def back_kernel(
-    base, place, before, after, band, taps, part, mask, patches, order, order_too,
+    place, before, after, band, taps, part, mask, patches,
     pre, c0, c1, c2, c3, halo, total, prod,
 ):
     chunks = (c0, c1, c2, c3)
     height, width = part.shape[1:3]
     chans = pre.shape[1]
-    tiles = tiles_of(before.shape[2])[base : base + -(-chans // LANES)]
+    tiles = tiles_of(chans)
     clear_edges(halo)
-    fill_band(halo, 0, before, tiles, base)
-    fill_band(halo, 3, after, tiles, base)
+    fill_band(halo, 0, before, tiles)
+    fill_band(halo, 3, after, tiles)
     half = width // 2
 
     def step(u, carry):
-        d, h = u // 2, (u % 2) * half
-        t = d + base
+        t, h = u // 2, (u % 2) * half
         here = pl.ds(pl.multiple_of(h, 8), half)
         acc = [part[t, p, here, :].reshape(half // 8, 8, LANES) for p in range(height)]
         for m in range(6):
             s = m if m < 3 else m + height
             for j in range(KS):
-                value = halo[d, m, pl.ds(h + 5 + j, half), :].reshape(half // 8, 8, LANES)
+                value = halo[t, m, pl.ds(h + 5 + j, half), :].reshape(half // 8, 8, LANES)
                 for p in range(height):
                     i = s - p
                     if 0 <= i < KS:
                         acc[p] = acc[p] + value * taps[t, 48 - (KS * i + j)][None]
         keep = mask[here, :]
-        lanes = pl.ds(pl.multiple_of(d * LANES, LANES), LANES)
+        lanes = pl.ds(pl.multiple_of(t * LANES, LANES), LANES)
         for p in range(height):
             own = band[t, p, pl.ds(pl.multiple_of(h + 8, 8), half), :]
             value = own + keep * acc[p].reshape(half, LANES)
@@ -238,42 +230,45 @@
             chunks[d][k] = prod[at, :].astype(BF16)
 
 
-def grad_kernel(down, before, after, cots, order, grads, band, kg):
+def grad_kernel(down, cots, halo, grads, band, kg):
     height, width, chans = down.shape
+    tiles = tiles_of(chans)
+    clear_edges(band)
+    fill_band(band, 0, down, tiles)
+    half = width // 2
+
+    def step(u, carry):
+        t, h = u // 2, (u % 2) * half
+        here = pl.ds(pl.multiple_of(h + 8, 8), half)
+        mine = [halo[t, m, here, :] for m in range(3)]
+        mine += [cots[t, p, here, :] for p in range(height)]
+        mine += [halo[t, m, here, :] for m in range(3, 6)]
+        mine = [m.reshape(half // 8, 8, LANES) for m in mine]
+        for j in range(KS):
+            part = [jnp.zeros((8, LANES), F32) for _ in range(KS)]
+            for r in range(height):
+                value = band[t, r, pl.ds(h + 5 + j, half), :].reshape(half // 8, 8, LANES)
+                for i in range(KS):
+                    part[i] = part[i] + jnp.sum(value * mine[r + 6 - i], axis=0)
+            for i in range(KS):
+                kg[u, KS * i + j] = part[i]
+        kg[u, KS * KS] = sum(jnp.sum(m, axis=0) for m in mine[3 : 3 + height])
+        return carry
+
+    lax.fori_loop(0, 2 * len(tiles), step, 0)
+    scale = 1.0 / math.sqrt(height * 16 * width)
+    for t, wd in tiles:
+        term = jnp.sum(kg[2 * t] + kg[2 * t + 1], axis=1) * scale
+        grads[0 : KS * KS + 1, lanes_of(t, wd)] = term[:, :wd]
+
+
+def front_kernel(down, before, after, taps, bias, mask, features, outs, band):
+    height, width, chans = features.shape
     tiles = tiles_of(chans)
     clear_edges(band)
     fill_band(band, 0, before, tiles)
     fill_band(band, 3, down, tiles)
     fill_band(band, 3 + height, after, tiles)
-    half = width // 2
-
-    def step(u, carry):
-        t, h = u // 2, (u % 2) * half
-        here = pl.ds(pl.multiple_of(h + 8, 8), half)
-        mine = [cots[t, p, here, :].reshape(half // 8, 8, LANES) for p in range(height)]
-        for j in range(KS):
-            part = [jnp.zeros((half // 8, 8, LANES), F32) for _ in range(KS)]
-            for s in range(height + 6):
-                value = band[t, s, pl.ds(h + 5 + j, half), :].reshape(half // 8, 8, LANES)
-                for p in range(height):
-                    i = s - p
-                    if 0 <= i < KS:
-                        part[i] = part[i] + value * mine[p]
-            for i in range(KS):
-                kg[u, KS * i + j] = jnp.sum(part[i], axis=0)
-        kg[u, KS * KS] = sum(jnp.sum(m, axis=0) for m in mine)
-        return carry
-
-    lax.fori_loop(0, 2 * len(tiles), step, 0)
-    scale = 1.0 / math.sqrt(height * 16 * width)
-    for t, wd in tiles:
-        term = jnp.sum(kg[2 * t] + kg[2 * t + 1], axis=1) * scale
-        grads[0 : KS * KS + 1, lanes_of(t, wd)] = term[:, :wd]
-
-
-def front_kernel(band, taps, bias, mask, order, features, outs):
-    height, width, chans = features.shape
-    tiles = tiles_of(chans)
     half = width // 2
 
     def step(u, carry):
@@ -300,16 +295,14 @@
 
 
 def image_kernel(
-    pre_b, pre_a, weight, normed, rstd, gain, grads, image_grad, small, column, sort, flat, sums
+    pre, weight, normed, rstd, gain, grads, image_grad, small, column, sort, flat, sums
 ):
     rows, chans, cols = image_grad.shape
     height, width = rows // 2, cols // 2
     scale = 1.0 / math.sqrt(height * 16 * width)
-    cut = pre_b.shape[1]
     gain_column(gain, column)
     sort[...] = sorter(width, True)
-    value = jnp.dot(pre_b[...], weight[:cut, :], preferred_element_type=F32)
-    value = value + jnp.dot(pre_a[...], weight[cut:, :], preferred_element_type=F32)
+    value = jnp.dot(pre[...], weight[...], preferred_element_type=F32)
     flat[...] = jnp.transpose(value)
     gain_sum = jnp.zeros((chans, LANES), F32)
     for a in range(2):
@@ -331,30 +324,28 @@
             out = jnp.dot(jnp.concatenate(two, axis=1), sort[...], preferred_element_type=F32)
             image_grad[top] = out[:, :cols].astype(BF16)
             image_grad[top + 2] = out[:, cols:].astype(BF16)
-    ones = jnp.ones((8, pre_b.shape[0]), BF16)
+    ones = jnp.ones((8, pre.shape[0]), BF16)
     gain_row = jnp.sum(jnp.transpose(gain_sum), axis=0, keepdims=True)
     taps = KS * KS + 1
     sums[...] = jnp.zeros(sums.shape, F32)
     sums[0:taps, :] = grads[0:taps, :]
-    for pre, lanes in ((pre_b, slice(0, cut)), (pre_a, slice(cut, weight.shape[0]))):
-        bias_sum = jnp.dot(ones, pre[...], preferred_element_type=F32)[0:1]
-        sums[taps : taps + 1, lanes] = bias_sum * scale
+    bias_sum = jnp.dot(ones, pre[...], preferred_element_type=F32)[0:1]
+    sums[taps : taps + 1, :] = bias_sum * scale
     sums[taps + 1 : taps + 2, 0:chans] = gain_row * scale
     small[...] = sums[...].astype(BF16)
 
 
-def middle_kernel(place, c0, c1, c2, c3, order, *outs):
+def middle_kernel(place, c0, c1, c2, c3, *outs):
     for k in range(4):
         to = lax.rem(place[0] + k, 4)
         outs[k][...] = sum_four(c0[to], c1[to], c2[to], c3[to]).astype(BF16)
 
 
 def last_kernel(
-    b0, b1, b2, b3, a0, a1, a2, a3, t0, t1, t2, t3, weight, gain, bias, kernel, depth_bias
+    w0, w1, w2, w3, t0, t1, t2, t3,
+    weight, gain, bias, kernel, depth_bias,
 ):
-    cut = b0.shape[1]
-    weight[:, :cut] = sum_four(b0[...], b1[...], b2[...], b3[...])
-    weight[:, cut:] = sum_four(a0[...], a1[...], a2[...], a3[...])
+    weight[...] = sum_four(w0[...], w1[...], w2[...], w3[...])
     total = sum_four(t0[...], t1[...], t2[...], t3[...])
     taps = KS * KS
     kernel[...] = total[:taps]
@@ -391,32 +382,18 @@
     along_y = [[(4 * z + y, 4 * z + (y + k) % 4) for z, y in ring] for k in (1, 2, 3)]
     along_z = [[(4 * z + y, 4 * ((z + k) % 4) + y) for z, y in ring] for k in (1, 2, 3)]
     tiles = len(tiles_of(chans))
-    cut = FIRST * LANES
     share = in_chans // 4
     halo = sd((3, width, chans), BF16)
     span = width + 16
 
-    cot_first, cot_last, mask = call(
-        edge_kernel,
-        (halo, halo, sd((width, LANES), F32)),
-        [HBM, HBM],
-        [
-            pltpu.SMEM((1, width // PATCH), jnp.int32),
-            pltpu.VMEM((height, width, chans), BF16),
-            pltpu.SemaphoreType.DMA((2,)),
-        ],
-        "edge",
-        60,
-        2 * 10**7,
-    )(visible, cotangent)
-    cot_before = lax.ppermute(cot_last, "rows", up)
-    cot_after = lax.ppermute(cot_first, "rows", low)
-
     column = pltpu.VMEM((in_chans, LANES), F32)
     sort = pltpu.VMEM((4 * width, 4 * width), BF16)
-    patches, normed, rstd, down, down_first, down_last = call(
+    cot_first, cot_last, mask, patches, normed, rstd, down, down_first, down_last = call(
         reduce_kernel,
         (
+            halo,
+            halo,
+            sd((width, LANES), F32),
             sd((4 * in_chans, pixels), BF16),
             sd((4 * in_chans, pixels), BF16),
             sd((8, pixels), F32),
@@ -424,20 +401,24 @@
             halo,
             halo,
         ),
-        [HBM, HBM, HBM, HBM, VM, ANY],
+        [HBM] * 6,
         [
             column,
             sort,
+            pltpu.SMEM((1, width // PATCH), jnp.int32),
+            pltpu.VMEM((height, width, chans), BF16),
             pltpu.VMEM(image.shape, BF16),
             pltpu.VMEM((in_chans,), F32),
             pltpu.VMEM(weight.shape, BF16),
             pltpu.VMEM((chans,), F32),
-            pltpu.SemaphoreType.DMA((4,)),
+            pltpu.SemaphoreType.DMA((6,)),
         ],
         "reduce",
         60,
         2 * 10**7,
-    )(image, layer_norm_gain, weight, reducer_bias, mask, cot_first)
+    )(visible, cotangent, image, layer_norm_gain, weight, reducer_bias)
+    cot_before = lax.ppermute(cot_last, "rows", up)
+    cot_after = lax.ppermute(cot_first, "rows", low)
     down_before = lax.ppermute(down_last, "rows", up)
     down_after = lax.ppermute(down_first, "rows", low)
 
@@ -448,80 +429,72 @@
             sd((tiles, KS * KS, 8, LANES), F32),
             sd((tiles, height, width, LANES), F32),
         ),
-        [HBM, HBM, VM, ANY],
+        [HBM, HBM, VM],
         [
             pltpu.VMEM((height, width, chans), BF16),
             pltpu.VMEM((KS * KS, chans), F32),
             pltpu.SemaphoreType.DMA((2,)),
         ],
         "own",
-    )(cotangent, depth_kernel, mask, down_first)
-
-    def back(here, *order):
-        size = here[1] - here[0]
-        count = -(-size // LANES)
-        return call(
-            functools.partial(back_kernel, here[0] // LANES),
-            (sd((pixels, size), BF16),) + (sd((4, share, size), BF16),) * 4,
-            [SM] + [VM] * 7 + [ANY] * 2,
-            [
-                pltpu.VMEM((count, 6, span, LANES), F32),
-                pltpu.VMEM((pixels, count * LANES), F32),
-                pltpu.VMEM((in_chans, size), F32),
-            ],
-            "back",
-        )(place_y, cot_before, cot_after, band, taps, part, mask, patches, *order)
-
-    pre_b, *chunks_b = back((0, cut), mask, mask)
-    chunks_b, down_before, down_after = lax.optimization_barrier(
-        (chunks_b, down_before, down_after)
-    )
-    got_b = send(chunks_b[1:], along_y)
-    pre_a, *chunks_a = back((cut, chans), pre_b, mask)
-
-    grads, down_band = call(
+        16,
+        10**7,
+    )(cotangent, depth_kernel, mask)
+    pre, *chunks, halo_rows = call(
+        back_kernel,
+        (sd((pixels, chans), BF16),)
+        + (sd((4, share, chans), BF16),) * 4
+        + (sd((tiles, 6, span, LANES), F32),),
+        [SM] + [VM] * 7,
+        [pltpu.VMEM((pixels, tiles * LANES), F32), pltpu.VMEM((in_chans, chans), F32)],
+        "back",
+    )(place_y, cot_before, cot_after, band, taps, part, mask, patches)
+    chunks, down_before, down_after = lax.optimization_barrier((chunks, down_before, down_after))
+    got = send(chunks[1:], along_y)
+
+    grads = call(
         grad_kernel,
-        (sd((56, chans), F32), sd((tiles, height + 6, span, LANES), F32)),
-        [VM] * 4 + [ANY],
-        [pltpu.VMEM((2 * tiles, KS * KS + 1, 8, LANES), F32)],
+        sd((56, chans), F32),
+        [VM] * 3,
+        [
+            pltpu.VMEM((tiles, height, span, LANES), F32),
+            pltpu.VMEM((2 * tiles, KS * KS + 1, 8, LANES), F32),
+        ],
         "grads",
-    )(down, down_before, down_after, band, pre_a)
+    )(down, band, halo_rows)
     image_grad, small = call(
         image_kernel,
         (sd((rows, in_chans, cols), BF16), sd((56, chans), BF16)),
-        [VM] * 7,
+        [VM] * 6,
         [column, sort, pltpu.VMEM((4 * in_chans, pixels), F32), pltpu.VMEM((56, chans), F32)],
         "image",
-    )(pre_b, pre_a, weight, normed, rstd, layer_norm_gain, grads)
+    )(pre, weight, normed, rstd, layer_norm_gain, grads)
     image_grad = jnp.transpose(image_grad, (0, 2, 1))
+    got_t = send([small] * 3, along_z)
+    parts = call(
+        middle_kernel,
+        (sd((share, chans), BF16),) * 4,
+        [SM] + [VM] * 4,
+        [],
+        "middle",
+        16,
+        4 * 10**7,
+    )(place_z, chunks[0], *got)
+    got_w = send(parts[1:], along_z)
+    front_mask, _ = lax.optimization_barrier((mask, parts[0]))
     features = call(
         front_kernel,
         sd((height, width, chans), BF16),
-        [VM] * 4 + [ANY],
-        [pltpu.VMEM((tiles, height, width, LANES), F32)],
+        [VM] * 6,
+        [
+            pltpu.VMEM((tiles, height, width, LANES), F32),
+            pltpu.VMEM((tiles, height + 6, span, LANES), F32),
+        ],
         "front",
-    )(down_band, taps, depth_bias, mask, small)
-
-    def middle(own, got, size, order):
-        return call(
-            middle_kernel,
-            (sd((share, size), BF16),) * 4,
-            [SM] + [VM] * 4 + [ANY],
-            [],
-            "middle",
-        )(place_z, own, *got, order)
-
-    chunks_a[3], _ = lax.optimization_barrier((chunks_a[3], features))
-    got_a = send(chunks_a[1:], along_y)
-    small, *got_b = lax.optimization_barrier((small, *got_b))
+        16,
+        10**7,
+    )(down, down_before, down_after, taps, depth_bias, front_mask)
+    small = sum_four(small, *got_t).astype(BF16)
     got_t = send([small] * 3, along_y)
-    parts_b = middle(chunks_b[0], got_b, cut, features)
-    last_b = send(parts_b[1:], along_z)
-    small, *got_t = lax.optimization_barrier((small, *got_t, last_b[0]))[:4]
-    small = sum_four(small, *got_t).astype(BF16)
-    got_t = send([small] * 3, along_z)
-    parts_a = middle(chunks_a[0], got_a, chans - cut, parts_b[0])
-    last_a = send(parts_a[1:], along_z)
     down_weight_grad, gain_grad, bias_grad, kernel_grad, depth_bias_grad = call(
         last_kernel,
         (
@@ -531,10 +504,10 @@
             sd((KS * KS, chans), F32),
             sd((chans,), F32),
         ),
-        [VM] * 12,
+        [VM] * 8,
         [],
         "last",
-    )(parts_b[0], *last_b, parts_a[0], *last_a, small, *got_t)
+    )(parts[0], *got_w, small, *got_t)
     return (
         features,
         image_grad,

time: 84.6 us -> 76.5 us (0.904)
  starting transfers between devices: 45.1 us -> 36 us
  Pallas kernels: 24.2 us -> 23.1 us
  local copies, waits for them, and re-layouts: 3.1 us -> 4.08 us
    ppermute x18 -> x12, starting transfers between devices: 34.5 us -> 25.4 us  [send(): lax.ppermute(value, 'rows', pair)]
    pallas_call x8 -> x5, Pallas kernels: 18.3 us -> 17.2 us  [the longest x1 4.8 us: body(): call(reduce_kernel, (halo, halo, sd((width, LANES), F32), sd((4 * in_chan...]
    ppermute x1, waiting for transfers between devices: 1.08 us -> 0.01 us  [body(): down_after = lax.ppermute(down_first, 'rows', low)]
    ppermute x18 -> x12, waiting for transfers between devices: 9.38 us -> 10.4 us  [send(): lax.ppermute(value, 'rows', pair)]
    unnamed x24 -> x32, local copies, waits for them, and re-layouts: 3.1 us -> 4.08 us
  transfers between devices with their start and end apart: 22 -> 16, of which waited for: 6 -> 7; matrix products, arithmetic and copies ran while one was open for 0% -> 0% of each run, Pallas kernels for 26% -> 23%
where the time goes in v4:
time: 76.5 us; the launch traced here: 75.3 us
  starting transfers between devices  36 us (47%)
  Pallas kernels  23.1 us (30%)
  waiting for transfers between devices  11.2 us (15%)
  local copies, waits for them, and re-layouts  4.08 us (5%)
  between operations  0.83 us (1%)
    ppermute x12, starting transfers between devices, send(): lax.ppermute(value, 'rows', pair)  25.4 us
    ppermute x12, waiting for transfers between devices, send(): lax.ppermute(value, 'rows', pair)  10.4 us
    pallas_call x1, Pallas kernels, body(): call(reduce_kernel, (halo, halo, sd((width, LANES), F32), sd((4 * in_chan...  4.8 us
    ppermute x1, starting transfers between devices, body(): down_before = lax.ppermute(down_last, 'rows', up)  4.56 us
    pallas_call x1, Pallas kernels, body(): call(back_kernel, (sd((pixels, chans), BF16),) + (sd((4, share, chans), B...  4.16 us
    unnamed x32, local copies, waits for them, and re-layouts  4.08 us
    pallas_call x1, Pallas kernels, body(): call(front_kernel, sd((height, width, chans), BF16), [VM] * 6, [pltpu.VME...  3.8 us
    ppermute x1, starting transfers between devices, body(): cot_before = lax.ppermute(cot_last, 'rows', up)  3.5 us
  transfers between devices with their start and end apart: 16, of which 7 were waited for; matrix products, arithmetic and copies ran while one was open for 0% of the time, Pallas kernels for 23%

profile of v4, /device:TPU:2, one launch (start us, length us, event | category | flops | bytes accessed | tf_op | source)
XLA Modules:
  0.0 75.3 jit_solution(8969277252767418740)
XLA Ops:
  0.7 4.8 %reduce.1 = (bf16[3,64,704]{2,1,0:T(8,128)(2,1)}, bf16[3,64,704]{2,1,0:T(8,128)(2,1)}, f32[64,128]{1,0:T(8,128)}, bf16[1408,256]{1,0:T(8,128)(2,1)}, bf16[1408,2...) custom-call(s32[1,16]{1,0:T(1,128)} %vis_in.1, ...), custom_call_target="tpu_custom_call" | custom-call | flops 1000000 | bytes 20000000 | tf_op jit(solution)/shard_map/reduce/pallas_call | solution.py:391
  5.5 3.5 %collective-permute-start = (bf16[3,64,704]{2,1,0:T(8,128)(2,1)}, bf16[3,64,704]{2,1,0:T(8,128)(2,1)S(1)}, u32[]{:S(2)}, u32[]{:S(2)}) collective-permute-start(bf16[3,64,704]{2,1,0:T(8,128)(2,1)} %get-tuple-element.44), channel_id=1, source_target_pairs={{0,1},{1,2},{2,3},{3,4},{4,5},{5,6},{6,7},{7,8},{8,9},{9,10},{10,1... | collective-permute-start | bytes 811016 | tf_op jit(solution)/shard_map/ppermute | solution.py:420
  9.0 1.3 %collective-permute-start.1 = (bf16[3,64,704]{2,1,0:T(8,128)(2,1)}, bf16[3,64,704]{2,1,0:T(8,128)(2,1)S(1)}, u32[]{:S(2)}, u32[]{:S(2)}) collective-permute-start(bf16[3,64,704]{2,1,0:T(8,128)(2,1)} %get-tuple-element.45), channel_id=1, source_target_pairs={{1,0},{2,1},{3,2},{4,3},{5,4},{6,5},{7,6},{8,7},{9,8},{10,9},{11,1... | collective-permute-start | bytes 811016 | tf_op jit(solution)/shard_map/ppermute | solution.py:421
  10.3 4.6 %collective-permute-start.2 = (bf16[3,64,704]{2,1,0:T(8,128)(2,1)}, bf16[3,64,704]{2,1,0:T(8,128)(2,1)S(1)}, u32[]{:S(2)}, u32[]{:S(2)}) collective-permute-start(bf16[3,64,704]{2,1,0:T(8,128)(2,1)} %get-tuple-element.55), channel_id=1, source_target_pairs={{0,1},{1,2},{2,3},{3,4},{4,5},{5,6},{6,7},{7,8},{8,9},{9,10},{10,1... | collective-permute-start | bytes 811016 | tf_op jit(solution)/shard_map/ppermute | solution.py:422
  14.8 1.3 %collective-permute-start.3 = (bf16[3,64,704]{2,1,0:T(8,128)(2,1)}, bf16[3,64,704]{2,1,0:T(8,128)(2,1)S(1)}, u32[]{:S(2)}, u32[]{:S(2)}) collective-permute-start(bf16[3,64,704]{2,1,0:T(8,128)(2,1)} %get-tuple-element.56), channel_id=1, source_target_pairs={{1,0},{2,1},{3,2},{4,3},{5,4},{6,5},{7,6},{8,7},{9,8},{10,9},{11,1... | collective-permute-start | bytes 811016 | tf_op jit(solution)/shard_map/ppermute | solution.py:423
  16.2 0.7 copy-done.5
  16.9 2.7 %own.1 = (f32[6,4,80,128]{3,2,1,0:T(8,128)S(1)}, f32[6,49,8,128]{3,2,1,0:T(8,128)S(1)}, f32[6,4,64,128]{3,2,1,0:T(8,128)S(1)}) custom-call(bf16[4,64,704]{2,1,0:T(8,128)(2,1)S(1)} %copy-done.2, f32[49,704]{1,0:T(8,128)S(1)} %copy-done.12, f32[64,128]{1,0:T(8,128)S(1)} %copy-done.5), custom_call_target="tpu_custom_call" | custom-call | flops 1000000 | bytes 10000000 | tf_op jit(solution)/shard_map/own/pallas_call | solution.py:425
  19.7 0.8 %collective-permute-done.1.after = bf16[3,64,704]{2,1,0:T(8,128)(2,1)S(1)} collective-permute-done((bf16[3,64,704]{2,1,0:T(8,128)(2,1)}, bf16[3,64,704]{2,1,0:T(8,128)(2,1)S(1)}, u32[]{:S(2)}, u32[]{:S(2)}) %collective-permute-start.1) | collective-permute-done | bytes 270368 | tf_op jit(solution)/shard_map/ppermute | solution.py:421
  20.5 1.1 %copy-done.3 = bf16[1408,256]{1,0:T(8,128)(2,1)S(1)} copy-done((bf16[1408,256]{1,0:T(8,128)(2,1)S(1)}, bf16[1408,256]{1,0:T(8,128)(2,1)}, u32[]{:S(2)}) %copy-start.3) | copy-done | bytes 720920
  21.6 0.8 %copy-done.6 = f32[64,128]{1,0:T(8,128)S(1)} copy-done((f32[64,128]{1,0:T(8,128)S(1)}, f32[64,128]{1,0:T(8,128)}, u32[]{:S(2)}) %copy-start.6) | copy-done | bytes 32792
  22.3 4.2 %back.1 = (bf16[256,704]{1,0:T(8,128)(2,1)S(1)}, bf16[4,88,704]{2,1,0:T(8,128)(2,1)S(1)}, bf16[4,88,704]{2,1,0:T(8,128)(2,1)}, bf16[4,88,704]{2,1,0:T(8,128)(2,1...) custom-call(s32[1]{0:T(128)} %bitcast.2.place, bf16[3,64,704]{2,1,0:T(8,128)(2,1)S(1)} %collective-permute-done.before, ...), custom_call_target="tpu_custom_call" | custom-call | flops 1000000 | bytes 100000 | tf_op jit(solution)/shard_map/back/pallas_call | solution.py:442
  26.5 0.7 copy-done.8
  27.2 0.7 copy-done.10
  27.9 1.9 %collective-permute-start.4 = (bf16[4,88,704]{2,1,0:T(8,128)(2,1)}, bf16[4,88,704]{2,1,0:T(8,128)(2,1)S(1)}, u32[]{:S(2)}, u32[]{:S(2)}) collective-permute-start(bf16[4,88,704]{2,1,0:T(8,128)(2,1)} %get-tuple-element.60), channel_id=1, source_target_pairs={{0,1},{1,2},{2,3},{3,0},{4,5},{5,6},{6,7},{7,4},{8,9},{9,10},{10,1... | collective-permute-start | bytes 1486856 | tf_op jit(solution)/shard_map/ppermute | solution.py:366
  29.8 4.5 %collective-permute-start.5 = (bf16[4,88,704]{2,1,0:T(8,128)(2,1)}, bf16[4,88,704]{2,1,0:T(8,128)(2,1)S(1)}, u32[]{:S(2)}, u32[]{:S(2)}) collective-permute-start(bf16[4,88,704]{2,1,0:T(8,128)(2,1)} %get-tuple-element.61), channel_id=1, source_target_pairs={{0,2},{1,3},{2,0},{3,1},{4,6},{5,7},{6,4},{7,5},{8,10},{9,11},{10,... | collective-permute-start | bytes 1486856 | tf_op jit(solution)/shard_map/ppermute | solution.py:366
  34.4 3.1 %grads.1 = f32[56,704]{1,0:T(8,128)S(1)} custom-call(bf16[4,64,704]{2,1,0:T(8,128)(2,1)S(1)} %copy-done.1, f32[6,4,80,128]{3,2,1,0:T(8,128)S(1)} %get-tuple-element.47.band.cots, f32[6,6,80,128]{3,2,1,0:T(8,128)S(1)} %get-tuple-element.68.halo), custom_call_target="tpu_custom_call" | custom-call | flops 1000000 | bytes 100000 | tf_op jit(solution)/shard_map/grads/pallas_call | solution.py:454
  37.5 2.4 %image.1 = (bf16[8,352,128]{2,1,0:T(8,128)(2,1)}, bf16[56,704]{1,0:T(8,128)(2,1)S(1)}) custom-call(bf16[256,704]{1,0:T(8,128)(2,1)S(1)} %get-tuple-element.65.pre, bf16[704,1408]{1,0:T(8,128)(2,1)S(1)} %bitcast.6, bf16[1408,256]{1,0:T(8,128)(2,1)S(1)} %copy-done.4, f32[8,256]{1,0:T(8,128)S(1)} %copy-done.13, f32[352]{0:T(512)S(1)} %copy-done.14, ...), custom_call_target="tpu_custom_call" | custom-call | flops 1000000 | bytes 100000 | tf_op jit(solution)/shard_map/image/pallas_call | solution.py:464
  39.9 5.9 %collective-permute-start.12 = (bf16[56,704]{1,0:T(8,128)(2,1)S(1)}, bf16[56,704]{1,0:T(8,128)(2,1)S(1)}, u32[]{:S(2)}, u32[]{:S(2)}) collective-permute-start(bf16[56,704]{1,0:T(8,128)(2,1)S(1)} %get-tuple-element.73), channel_id=1, source_target_pairs={{0,12},{1,13},{2,14},{3,15},{4,0},{5,1},{6,2},{7,3},{8,4},{9,5},{1... | collective-permute-start | bytes 236552 | tf_op jit(solution)/shard_map/ppermute | solution.py:366
  45.8 2.6 %collective-permute-done.12 = bf16[56,704]{1,0:T(8,128)(2,1)S(1)} collective-permute-done((bf16[56,704]{1,0:T(8,128)(2,1)S(1)}, bf16[56,704]{1,0:T(8,128)(2,1)S(1)}, u32[]{:S(2)}, u32[]{:S(2)}) %collective-permute-start.12) | collective-permute-done | bytes 78880 | tf_op jit(solution)/shard_map/ppermute | solution.py:366
  48.4 0.9 %collective-permute-start.10 = (bf16[56,704]{1,0:T(8,128)(2,1)S(1)}, bf16[56,704]{1,0:T(8,128)(2,1)S(1)}, u32[]{:S(2)}, u32[]{:S(2)}) collective-permute-start(bf16[56,704]{1,0:T(8,128)(2,1)S(1)} %get-tuple-element.73), channel_id=1, source_target_pairs={{0,8},{1,9},{2,10},{3,11},{4,12},{5,13},{6,14},{7,15},{8,0},{9,1},... | collective-permute-start | bytes 236552 | tf_op jit(solution)/shard_map/ppermute | solution.py:366
  49.3 2.8 %collective-permute-done.11 = bf16[56,704]{1,0:T(8,128)(2,1)S(1)} collective-permute-done((bf16[56,704]{1,0:T(8,128)(2,1)S(1)}, bf16[56,704]{1,0:T(8,128)(2,1)S(1)}, u32[]{:S(2)}, u32[]{:S(2)}) %collective-permute-start.11) | collective-permute-done | bytes 78880 | tf_op jit(solution)/shard_map/ppermute | solution.py:366
  52.1 1.7 %collective-permute-done.10 = bf16[56,704]{1,0:T(8,128)(2,1)S(1)} collective-permute-done((bf16[56,704]{1,0:T(8,128)(2,1)S(1)}, bf16[56,704]{1,0:T(8,128)(2,1)S(1)}, u32[]{:S(2)}, u32[]{:S(2)}) %collective-permute-start.10) | collective-permute-done | bytes 78880 | tf_op jit(solution)/shard_map/ppermute | solution.py:366
  53.8 0.9 %collective-permute-start.15 = (bf16[56,704]{1,0:T(8,128)(2,1)S(1)}, bf16[56,704]{1,0:T(8,128)(2,1)S(1)}, u32[]{:S(2)}, u32[]{:S(2)}) collective-permute-start(bf16[56,704]{1,0:T(8,128)(2,1)S(1)} %add_convert_fusion.t0), channel_id=1, source_target_pairs={{0,3},{1,0},{2,1},{3,2},{4,7},{5,4},{6,5},{7,6},{8,11},{9,8},{10,9... | collective-permute-start | bytes 236552 | tf_op jit(solution)/shard_map/ppermute | solution.py:366
  54.8 2.5 %collective-permute-done.5.c2 = bf16[4,88,704]{2,1,0:T(8,128)(2,1)S(1)} collective-permute-done((bf16[4,88,704]{2,1,0:T(8,128)(2,1)}, bf16[4,88,704]{2,1,0:T(8,128)(2,1)S(1)}, u32[]{:S(2)}, u32[]{:S(2)}) %collective-permute-start.5) | collective-permute-done | bytes 495648 | tf_op jit(solution)/shard_map/ppermute | solution.py:366
  57.7 1.3 %middle.1 = (bf16[88,704]{1,0:T(8,128)(2,1)S(1)}, bf16[88,704]{1,0:T(8,128)(2,1)S(1)}, bf16[88,704]{1,0:T(8,128)(2,1)S(1)}, bf16[88,704]{1,0:T(8,128)(2,1)S(1)}) custom-call(s32[1]{0:T(128)} %bitcast.3.place, bf16[4,88,704]{2,1,0:T(8,128)(2,1)S(1)} %get-tuple-element.59.c0, bf16[4,88,704]{2,1,0:T(8,128)(2,1)S(1)} %collective-permute-done.4.c1, ...), custom_call_target="tpu_custom_call" | custom-call | flops 1000000 | bytes 40000000 | tf_op jit(solution)/shard_map/middle/pallas_call | solution.py:473
  59.1 4.2 %collective-permute-start.7 = (bf16[88,704]{1,0:T(8,128)(2,1)S(1)}, bf16[88,704]{1,0:T(8,128)(2,1)S(1)}, u32[]{:S(2)}, u32[]{:S(2)}) collective-permute-start(bf16[88,704]{1,0:T(8,128)(2,1)S(1)} %get-tuple-element.70), channel_id=1, source_target_pairs={{0,4},{1,5},{2,6},{3,7},{4,8},{5,9},{6,10},{7,11},{8,12},{9,13},{1... | collective-permute-start | bytes 371720 | tf_op jit(solution)/shard_map/ppermute | solution.py:366
  63.3 3.3 %collective-permute-start.8 = (bf16[88,704]{1,0:T(8,128)(2,1)S(1)}, bf16[88,704]{1,0:T(8,128)(2,1)S(1)}, u32[]{:S(2)}, u32[]{:S(2)}) collective-permute-start(bf16[88,704]{1,0:T(8,128)(2,1)S(1)} %get-tuple-element.71), channel_id=1, source_target_pairs={{0,8},{1,9},{2,10},{3,11},{4,12},{5,13},{6,14},{7,15},{8,0},{9,1},... | collective-permute-start | bytes 371720 | tf_op jit(solution)/shard_map/ppermute | solution.py:366
  66.5 1.0 %collective-permute-start.9 = (bf16[88,704]{1,0:T(8,128)(2,1)S(1)}, bf16[88,704]{1,0:T(8,128)(2,1)S(1)}, u32[]{:S(2)}, u32[]{:S(2)}) collective-permute-start(bf16[88,704]{1,0:T(8,128)(2,1)S(1)} %get-tuple-element.72), channel_id=1, source_target_pairs={{0,12},{1,13},{2,14},{3,15},{4,0},{5,1},{6,2},{7,3},{8,4},{9,5},{1... | collective-permute-start | bytes 371720 | tf_op jit(solution)/shard_map/ppermute | solution.py:366
  67.5 0.9 %collective-permute-start.14 = (bf16[56,704]{1,0:T(8,128)(2,1)S(1)}, bf16[56,704]{1,0:T(8,128)(2,1)S(1)}, u32[]{:S(2)}, u32[]{:S(2)}) collective-permute-start(bf16[56,704]{1,0:T(8,128)(2,1)S(1)} %add_convert_fusion.t0), channel_id=1, source_target_pairs={{0,2},{1,3},{2,0},{3,1},{4,6},{5,7},{6,4},{7,5},{8,10},{9,11},{10,... | collective-permute-start | bytes 236552 | tf_op jit(solution)/shard_map/ppermute | solution.py:366
  68.4 1.8 %collective-permute-start.13 = (bf16[56,704]{1,0:T(8,128)(2,1)S(1)}, bf16[56,704]{1,0:T(8,128)(2,1)S(1)}, u32[]{:S(2)}, u32[]{:S(2)}) collective-permute-start(bf16[56,704]{1,0:T(8,128)(2,1)S(1)} %add_convert_fusion.t0), channel_id=1, source_target_pairs={{0,1},{1,2},{2,3},{3,0},{4,5},{5,6},{6,7},{7,4},{8,9},{9,10},{10,1... | collective-permute-start | bytes 236552 | tf_op jit(solution)/shard_map/ppermute | solution.py:366
  70.3 3.8 %front.1 = bf16[4,64,704]{2,1,0:T(8,128)(2,1)} custom-call(bf16[4,64,704]{2,1,0:T(8,128)(2,1)S(1)} %copy-done.1, bf16[3,64,704]{2,1,0:T(8,128)(2,1)S(1)} %copy-done.9, bf16[3,64,704]{2,1,0:T(8,128)(2,1)S(1)} %copy-done.11, f32[6,49,8,128]{3,2,1,0:T(8,128)S(1)} %get-tuple-element.48.taps, f32[704]{0:T(1024)S(1)} %copy-done.15, f32[64,128]{1,0:T(8,128)S(1)} %copy-done.7), custom_call_target="tpu_custom_call" | custom-call | flops 1000000 | bytes 10000000 | tf_op jit(solution)/shard_map/front/pallas_call | solution.py:484
  74.4 0.8 %last.1 = (f32[88,704]{1,0:T(8,128)}, f32[352]{0:T(512)}, f32[704]{0:T(1024)}, f32[49,704]{1,0:T(8,128)}, f32[704]{0:T(1024)}) custom-call(bf16[88,704]{1,0:T(8,128)(2,1)S(1)} %get-tuple-element.63.w0, bf16[88,704]{1,0:T(8,128)(2,1)S(1)} %collective-permute-done.7.w1, bf16[88,704]{1,0:T(8,128)(2,1)S(1)} %collective-permute-done.8.w2, ...), custom_call_target="tpu_custom_call" | custom-call | flops 1000000 | bytes 100000 | tf_op jit(solution)/shard_map/last/pallas_call | solution.py:498
  (41 shorter events, 1.0 us)
Async XLA Ops:
  0.6 15.5 %copy-start.2 = (bf16[4,64,704]{2,1,0:T(8,128)(2,1)S(1)}, bf16[4,64,704]{2,1,0:T(8,128)(2,1)}, u32[]{:S(2)}) copy-start(bf16[4,64,704]{2,1,0:T(8,128)(2,1)} %cot_in.3) | copy-start | bytes 1081348
  0.6 15.5 %copy-start.12 = (f32[49,704]{1,0:T(8,128)S(1)}, f32[49,704]{1,0:T(8,128)}, u32[]{:S(2)}) copy-start(f32[49,704]{1,0:T(8,128)} %kernel_in.1) | copy-start | bytes 413956
  5.5 14.2 %collective-permute-start = (bf16[3,64,704]{2,1,0:T(8,128)(2,1)}, bf16[3,64,704]{2,1,0:T(8,128)(2,1)S(1)}, u32[]{:S(2)}, u32[]{:S(2)}) collective-permute-start(bf16[3,64,704]{2,1,0:T(8,128)(2,1)} %get-tuple-element.44), channel_id=1, source_target_pairs={{0,1},{1,2},{2,3},{3,4},{4,5},{5,6},{6,7},{7,8},{8,9},{9,10},{10,1... | collective-permute-start | bytes 811016 | tf_op jit(solution)/shard_map/ppermute | solution.py:420
  9.0 11.5 %collective-permute-start.1 = (bf16[3,64,704]{2,1,0:T(8,128)(2,1)}, bf16[3,64,704]{2,1,0:T(8,128)(2,1)S(1)}, u32[]{:S(2)}, u32[]{:S(2)}) collective-permute-start(bf16[3,64,704]{2,1,0:T(8,128)(2,1)} %get-tuple-element.45), channel_id=1, source_target_pairs={{1,0},{2,1},{3,2},{4,3},{5,4},{6,5},{7,6},{8,7},{9,8},{10,9},{11,1... | collective-permute-start | bytes 811016 | tf_op jit(solution)/shard_map/ppermute | solution.py:421
  10.3 16.2 %collective-permute-start.2 = (bf16[3,64,704]{2,1,0:T(8,128)(2,1)}, bf16[3,64,704]{2,1,0:T(8,128)(2,1)S(1)}, u32[]{:S(2)}, u32[]{:S(2)}) collective-permute-start(bf16[3,64,704]{2,1,0:T(8,128)(2,1)} %get-tuple-element.55), channel_id=1, source_target_pairs={{0,1},{1,2},{2,3},{3,4},{4,5},{5,6},{6,7},{7,8},{8,9},{9,10},{10,1... | collective-permute-start | bytes 811016 | tf_op jit(solution)/shard_map/ppermute | solution.py:422
  14.8 12.4 %collective-permute-start.3 = (bf16[3,64,704]{2,1,0:T(8,128)(2,1)}, bf16[3,64,704]{2,1,0:T(8,128)(2,1)S(1)}, u32[]{:S(2)}, u32[]{:S(2)}) collective-permute-start(bf16[3,64,704]{2,1,0:T(8,128)(2,1)} %get-tuple-element.56), channel_id=1, source_target_pairs={{1,0},{2,1},{3,2},{4,3},{5,4},{6,5},{7,6},{8,7},{9,8},{10,9},{11,1... | collective-permute-start | bytes 811016 | tf_op jit(solution)/shard_map/ppermute | solution.py:423
  16.2 0.8 %copy-start.5 = (f32[64,128]{1,0:T(8,128)S(1)}, f32[64,128]{1,0:T(8,128)}, u32[]{:S(2)}) copy-start(f32[64,128]{1,0:T(8,128)} %get-tuple-element.64.mask) | copy-start | bytes 98308
  20.5 1.1 %copy-start.3 = (bf16[1408,256]{1,0:T(8,128)(2,1)S(1)}, bf16[1408,256]{1,0:T(8,128)(2,1)}, u32[]{:S(2)}) copy-start(bf16[1408,256]{1,0:T(8,128)(2,1)} %get-tuple-element.50.patches) | copy-start | bytes 2162692
  21.6 0.8 %copy-start.6 = (f32[64,128]{1,0:T(8,128)S(1)}, f32[64,128]{1,0:T(8,128)}, u32[]{:S(2)}) copy-start(f32[64,128]{1,0:T(8,128)} %get-tuple-element.64.mask) | copy-start | bytes 98308
  22.3 12.0 %copy-start.1 = (bf16[4,64,704]{2,1,0:T(8,128)(2,1)S(1)}, bf16[4,64,704]{2,1,0:T(8,128)(2,1)}, u32[]{:S(2)}) copy-start(bf16[4,64,704]{2,1,0:T(8,128)(2,1)} %get-tuple-element.43.down) | copy-start | bytes 1081348
  26.5 0.7 copy-start.8
  27.2 0.7 copy-start.10
  27.9 26.8 %collective-permute-start.4 = (bf16[4,88,704]{2,1,0:T(8,128)(2,1)}, bf16[4,88,704]{2,1,0:T(8,128)(2,1)S(1)}, u32[]{:S(2)}, u32[]{:S(2)}) collective-permute-start(bf16[4,88,704]{2,1,0:T(8,128)(2,1)} %get-tuple-element.60), channel_id=1, source_target_pairs={{0,1},{1,2},{2,3},{3,0},{4,5},{5,6},{6,7},{7,4},{8,9},{9,10},{10,1... | collective-permute-start | bytes 1486856 | tf_op jit(solution)/shard_map/ppermute | solution.py:366
  29.8 27.5 %collective-permute-start.5 = (bf16[4,88,704]{2,1,0:T(8,128)(2,1)}, bf16[4,88,704]{2,1,0:T(8,128)(2,1)S(1)}, u32[]{:S(2)}, u32[]{:S(2)}) collective-permute-start(bf16[4,88,704]{2,1,0:T(8,128)(2,1)} %get-tuple-element.61), channel_id=1, source_target_pairs={{0,2},{1,3},{2,0},{3,1},{4,6},{5,7},{6,4},{7,5},{8,10},{9,11},{10,... | collective-permute-start | bytes 1486856 | tf_op jit(solution)/shard_map/ppermute | solution.py:366
  34.3 23.4 %collective-permute-start.6 = (bf16[4,88,704]{2,1,0:T(8,128)(2,1)}, bf16[4,88,704]{2,1,0:T(8,128)(2,1)}, u32[]{:S(2)}, u32[]{:S(2)}) collective-permute-start(bf16[4,88,704]{2,1,0:T(8,128)(2,1)} %get-tuple-element.62), channel_id=1, source_target_pairs={{0,3},{1,0},{2,1},{3,2},{4,7},{5,4},{6,5},{7,6},{8,11},{9,8},{10,9... | collective-permute-start | bytes 1486856 | tf_op jit(solution)/shard_map/ppermute | solution.py:366
  34.3 3.1 %copy-start = (bf16[1408,704]{0,1:T(8,128)(2,1)S(1)}, bf16[1408,704]{0,1:T(8,128)(2,1)}, u32[]{:S(2)}) copy-start(bf16[1408,704]{0,1:T(8,128)(2,1)} %param.11) | copy-start | bytes 5947396
  34.3 3.1 %copy-start.4 = (bf16[1408,256]{1,0:T(8,128)(2,1)S(1)}, bf16[1408,256]{1,0:T(8,128)(2,1)}, u32[]{:S(2)}) copy-start(bf16[1408,256]{1,0:T(8,128)(2,1)} %get-tuple-element.66.normed) | copy-start | bytes 2162692
  34.3 3.2 %copy-start.13 = (f32[8,256]{1,0:T(8,128)S(1)}, f32[8,256]{1,0:T(8,128)}, u32[]{:S(2)}) copy-start(f32[8,256]{1,0:T(8,128)} %get-tuple-element.67.rstd) | copy-start | bytes 24580
  34.3 3.1 %copy-start.14 = (f32[352]{0:T(512)S(1)}, f32[352]{0:T(512)}, u32[]{:S(2)}) copy-start(f32[352]{0:T(512)} %gain.1) | copy-start | bytes 4228
  39.9 30.4 %copy-start.7 = (f32[64,128]{1,0:T(8,128)S(1)}, f32[64,128]{1,0:T(8,128)}, u32[]{:S(2)}) copy-start(f32[64,128]{1,0:T(8,128)} %get-tuple-element.64.mask) | copy-start | bytes 98308
  39.9 30.4 %copy-start.15 = (f32[704]{0:T(1024)S(1)}, f32[704]{0:T(1024)}, u32[]{:S(2)}) copy-start(f32[704]{0:T(1024)} %bias.1) | copy-start | bytes 8452
  39.9 8.5 %collective-permute-start.12 = (bf16[56,704]{1,0:T(8,128)(2,1)S(1)}, bf16[56,704]{1,0:T(8,128)(2,1)S(1)}, u32[]{:S(2)}, u32[]{:S(2)}) collective-permute-start(bf16[56,704]{1,0:T(8,128)(2,1)S(1)} %get-tuple-element.73), channel_id=1, source_target_pairs={{0,12},{1,13},{2,14},{3,15},{4,0},{5,1},{6,2},{7,3},{8,4},{9,5},{1... | collective-permute-start | bytes 236552 | tf_op jit(solution)/shard_map/ppermute | solution.py:366
  45.8 6.3 %collective-permute-start.11 = (bf16[56,704]{1,0:T(8,128)(2,1)S(1)}, bf16[56,704]{1,0:T(8,128)(2,1)S(1)}, u32[]{:S(2)}, u32[]{:S(2)}) collective-permute-start(bf16[56,704]{1,0:T(8,128)(2,1)S(1)} %get-tuple-element.73), channel_id=1, source_target_pairs={{0,4},{1,5},{2,6},{3,7},{4,8},{5,9},{6,10},{7,11},{8,12},{9,13},{1... | collective-permute-start | bytes 236552 | tf_op jit(solution)/shard_map/ppermute | solution.py:366
  48.4 5.4 %collective-permute-start.10 = (bf16[56,704]{1,0:T(8,128)(2,1)S(1)}, bf16[56,704]{1,0:T(8,128)(2,1)S(1)}, u32[]{:S(2)}, u32[]{:S(2)}) collective-permute-start(bf16[56,704]{1,0:T(8,128)(2,1)S(1)} %get-tuple-element.73), channel_id=1, source_target_pairs={{0,8},{1,9},{2,10},{3,11},{4,12},{5,13},{6,14},{7,15},{8,0},{9,1},... | collective-permute-start | bytes 236552 | tf_op jit(solution)/shard_map/ppermute | solution.py:366
  53.8 14.6 %collective-permute-start.15 = (bf16[56,704]{1,0:T(8,128)(2,1)S(1)}, bf16[56,704]{1,0:T(8,128)(2,1)S(1)}, u32[]{:S(2)}, u32[]{:S(2)}) collective-permute-start(bf16[56,704]{1,0:T(8,128)(2,1)S(1)} %add_convert_fusion.t0), channel_id=1, source_target_pairs={{0,3},{1,0},{2,1},{3,2},{4,7},{5,4},{6,5},{7,6},{8,11},{9,8},{10,9... | collective-permute-start | bytes 236552 | tf_op jit(solution)/shard_map/ppermute | solution.py:366
  54.7 15.5 %copy-start.9 = (bf16[3,64,704]{2,1,0:T(8,128)(2,1)S(1)}, bf16[3,64,704]{2,1,0:T(8,128)(2,1)}, u32[]{:S(2)}) copy-start(bf16[3,64,704]{2,1,0:T(8,128)(2,1)} %copy-done.8) | copy-start | bytes 811012
  54.8 15.5 %copy-start.11 = (bf16[3,64,704]{2,1,0:T(8,128)(2,1)S(1)}, bf16[3,64,704]{2,1,0:T(8,128)(2,1)}, u32[]{:S(2)}) copy-start(bf16[3,64,704]{2,1,0:T(8,128)(2,1)} %copy-done.10) | copy-start | bytes 811012
  59.1 15.4 %collective-permute-start.7 = (bf16[88,704]{1,0:T(8,128)(2,1)S(1)}, bf16[88,704]{1,0:T(8,128)(2,1)S(1)}, u32[]{:S(2)}, u32[]{:S(2)}) collective-permute-start(bf16[88,704]{1,0:T(8,128)(2,1)S(1)} %get-tuple-element.70), channel_id=1, source_target_pairs={{0,4},{1,5},{2,6},{3,7},{4,8},{5,9},{6,10},{7,11},{8,12},{9,13},{1... | collective-permute-start | bytes 371720 | tf_op jit(solution)/shard_map/ppermute | solution.py:366
  63.3 11.2 %collective-permute-start.8 = (bf16[88,704]{1,0:T(8,128)(2,1)S(1)}, bf16[88,704]{1,0:T(8,128)(2,1)S(1)}, u32[]{:S(2)}, u32[]{:S(2)}) collective-permute-start(bf16[88,704]{1,0:T(8,128)(2,1)S(1)} %get-tuple-element.71), channel_id=1, source_target_pairs={{0,8},{1,9},{2,10},{3,11},{4,12},{5,13},{6,14},{7,15},{8,0},{9,1},... | collective-permute-start | bytes 371720 | tf_op jit(solution)/shard_map/ppermute | solution.py:366
  66.5 7.9 %collective-permute-start.9 = (bf16[88,704]{1,0:T(8,128)(2,1)S(1)}, bf16[88,704]{1,0:T(8,128)(2,1)S(1)}, u32[]{:S(2)}, u32[]{:S(2)}) collective-permute-start(bf16[88,704]{1,0:T(8,128)(2,1)S(1)} %get-tuple-element.72), channel_id=1, source_target_pairs={{0,12},{1,13},{2,14},{3,15},{4,0},{5,1},{6,2},{7,3},{8,4},{9,5},{1... | collective-permute-start | bytes 371720 | tf_op jit(solution)/shard_map/ppermute | solution.py:366
  67.5 6.5 %collective-permute-start.14 = (bf16[56,704]{1,0:T(8,128)(2,1)S(1)}, bf16[56,704]{1,0:T(8,128)(2,1)S(1)}, u32[]{:S(2)}, u32[]{:S(2)}) collective-permute-start(bf16[56,704]{1,0:T(8,128)(2,1)S(1)} %add_convert_fusion.t0), channel_id=1, source_target_pairs={{0,2},{1,3},{2,0},{3,1},{4,6},{5,7},{6,4},{7,5},{8,10},{9,11},{10,... | collective-permute-start | bytes 236552 | tf_op jit(solution)/shard_map/ppermute | solution.py:366
  68.4 6.0 %collective-permute-start.13 = (bf16[56,704]{1,0:T(8,128)(2,1)S(1)}, bf16[56,704]{1,0:T(8,128)(2,1)S(1)}, u32[]{:S(2)}, u32[]{:S(2)}) collective-permute-start(bf16[56,704]{1,0:T(8,128)(2,1)S(1)} %add_convert_fusion.t0), channel_id=1, source_target_pairs={{0,1},{1,2},{2,3},{3,0},{4,5},{5,6},{6,7},{7,4},{8,9},{9,10},{10,1... | collective-permute-start | bytes 236552 | tf_op jit(solution)/shard_map/ppermute | solution.py:366

commit v5 on v4

--- a/solution.py
+++ b/solution.py
@@ -14,7 +14,6 @@
 BF16 = jnp.bfloat16
 VM = pl.BlockSpec(memory_space=pltpu.VMEM)
 SM = pl.BlockSpec(memory_space=pltpu.SMEM)
-ANY = pl.BlockSpec(memory_space=pl.ANY)
 HBM = pl.BlockSpec(memory_space=pltpu.HBM)
 
 
@@ -72,7 +71,7 @@
 
 def reduce_kernel(
     vis_in, cot_in, image_in, gain_in, weight_in, bias_in,
-    cot_first, cot_last, mask, patches, normed, rstd, down, first, last,
+    cot_first, cot_last, patches, normed, rstd, down, first, last,
     column, sort, vis, cot, image, gain, weight, bias, sems,
 ):
     copies = fetch(
@@ -83,7 +82,7 @@
     rows, chans, cols = image.shape
     height, width = rows // 2, cols // 2
     copies[4].wait()
-    mask[...] = column_mask(vis, width)
+    mask = column_mask(vis, width)
     copies[5].wait()
     for t, wd in tiles_of(cot.shape[2]):
         lanes = lanes_of(t, wd)
@@ -146,9 +145,14 @@
     dst[:, :, span - 8 : span, :] = edge
 
 
-def own_kernel(cot_in, kernel_in, mask, band, taps, part, cot, kernel, sems):
-    copies = fetch((cot_in, kernel_in), (cot, kernel), sems)
+def own_kernel(
+    vis_in, cot_in, kernel_in, band, taps, part, mask_out, vis, cot, kernel, sems
+):
+    copies = fetch((cot_in, kernel_in, vis_in), (cot, kernel, vis), sems)
     height, width, chans = cot.shape
+    copies[2].wait()
+    mask = column_mask(vis, width)
+    mask_out[...] = mask
     tiles = tiles_of(chans)
     clear_edges(band)
     copies[1].wait()
@@ -388,12 +392,11 @@
 
     column = pltpu.VMEM((in_chans, LANES), F32)
     sort = pltpu.VMEM((4 * width, 4 * width), BF16)
-    cot_first, cot_last, mask, patches, normed, rstd, down, down_first, down_last = call(
+    cot_first, cot_last, patches, normed, rstd, down, down_first, down_last = call(
         reduce_kernel,
         (
             halo,
             halo,
-            sd((width, LANES), F32),
             sd((4 * in_chans, pixels), BF16),
             sd((4 * in_chans, pixels), BF16),
             sd((8, pixels), F32),
@@ -422,23 +425,27 @@
     down_before = lax.ppermute(down_last, "rows", up)
     down_after = lax.ppermute(down_first, "rows", low)
 
-    band, taps, part = call(
+    vis_own, _ = lax.optimization_barrier((visible, rstd))
+    band, taps, part, mask = call(
         own_kernel,
         (
             sd((tiles, height, span, LANES), F32),
             sd((tiles, KS * KS, 8, LANES), F32),
             sd((tiles, height, width, LANES), F32),
+            sd((width, LANES), F32),
         ),
-        [HBM, HBM, VM],
+        [HBM] * 3,
         [
+            pltpu.SMEM((1, width // PATCH), jnp.int32),
             pltpu.VMEM((height, width, chans), BF16),
             pltpu.VMEM((KS * KS, chans), F32),
-            pltpu.SemaphoreType.DMA((2,)),
+            pltpu.SemaphoreType.DMA((3,)),
         ],
         "own",
         16,
-        10**7,
-    )(cotangent, depth_kernel, mask)
+        5 * 10**7,
+    )(vis_own, cotangent, depth_kernel)
+
     pre, *chunks, halo_rows = call(
         back_kernel,
         (sd((pixels, chans), BF16),)
@@ -447,9 +454,11 @@
         [SM] + [VM] * 7,
         [pltpu.VMEM((pixels, tiles * LANES), F32), pltpu.VMEM((in_chans, chans), F32)],
         "back",
+        16,
+        10**9,
     )(place_y, cot_before, cot_after, band, taps, part, mask, patches)
-    chunks, down_before, down_after = lax.optimization_barrier((chunks, down_before, down_after))
     got = send(chunks[1:], along_y)
+    down, down_before, down_after = lax.optimization_barrier((down, down_before, down_after))
 
     grads = call(
         grad_kernel,

time: 76.5 us -> 74 us (0.967)
  local copies, waits for them, and re-layouts: 4.08 us -> 1.16 us
  Pallas kernels: 23.1 us -> 24.6 us
    unnamed x32 -> x24, local copies, waits for them, and re-layouts: 4.08 us -> 1.16 us
    pallas_call x1, Pallas kernels: 3.8 us -> 4.76 us  [body(): call(front_kernel, sd((height, width, chans), BF16), [VM] * 6, [pltpu.VME...]
  transfers between devices with their start and end apart: 16 -> 16, of which waited for: 7 -> 6; matrix products, arithmetic and copies ran while one was open for 0% -> 0% of each run, Pallas kernels for 23% -> 26%
where the time goes in v5:
time: 74 us; the launch traced here: 73.5 us
  starting transfers between devices  35.8 us (48%)
  Pallas kernels  24.6 us (33%)
  waiting for transfers between devices  11 us (15%)
  local copies, waits for them, and re-layouts  1.16 us (2%)
  between operations  0.88 us (1%)
    ppermute x12, starting transfers between devices, send(): lax.ppermute(value, 'rows', pair)  25.2 us
    ppermute x12, waiting for transfers between devices, send(): lax.ppermute(value, 'rows', pair)  9.96 us
    pallas_call x1, Pallas kernels, body(): call(reduce_kernel, (halo, halo, sd((4 * in_chans, pixels), BF16), sd((4...  4.78 us
    pallas_call x1, Pallas kernels, body(): call(front_kernel, sd((height, width, chans), BF16), [VM] * 6, [pltpu.VME...  4.76 us
    ppermute x1, starting transfers between devices, body(): down_before = lax.ppermute(down_last, 'rows', up)  4.56 us
    pallas_call x1, Pallas kernels, body(): call(back_kernel, (sd((pixels, chans), BF16),) + (sd((4, share, chans), B...  4.15 us
    ppermute x1, starting transfers between devices, body(): cot_before = lax.ppermute(cot_last, 'rows', up)  3.5 us
    pallas_call x1, Pallas kernels, body(): call(own_kernel, (sd((tiles, height, span, LANES), F32), sd((tiles, KS *...  3.27 us
  transfers between devices with their start and end apart: 16, of which 6 were waited for; matrix products, arithmetic and copies ran while one was open for 0% of the time, Pallas kernels for 26%

profile of v5, /device:TPU:2, one launch (start us, length us, event | category | flops | bytes accessed | tf_op | source)
XLA Modules:
  0.0 73.5 jit_solution(4442551707112115435)
XLA Ops:
  0.7 4.8 %reduce.1 = (bf16[3,64,704]{2,1,0:T(8,128)(2,1)}, bf16[3,64,704]{2,1,0:T(8,128)(2,1)}, bf16[1408,256]{1,0:T(8,128)(2,1)}, bf16[1408,256]{1,0:T(8,128)(2,1)}, f32...) custom-call(s32[1,16]{1,0:T(1,128)} %vis_in.2, ...), custom_call_target="tpu_custom_call" | custom-call | flops 1000000 | bytes 20000000 | tf_op jit(solution)/shard_map/reduce/pallas_call | solution.py:395
  5.5 3.5 %collective-permute-start.2 = (bf16[3,64,704]{2,1,0:T(8,128)(2,1)}, bf16[3,64,704]{2,1,0:T(8,128)(2,1)S(1)}, u32[]{:S(2)}, u32[]{:S(2)}) collective-permute-start(bf16[3,64,704]{2,1,0:T(8,128)(2,1)} %get-tuple-element.51), channel_id=1, source_target_pairs={{0,1},{1,2},{2,3},{3,4},{4,5},{5,6},{6,7},{7,8},{8,9},{9,10},{10,1... | collective-permute-start | bytes 811016 | tf_op jit(solution)/shard_map/ppermute | solution.py:423
  9.0 1.3 %collective-permute-start.3 = (bf16[3,64,704]{2,1,0:T(8,128)(2,1)}, bf16[3,64,704]{2,1,0:T(8,128)(2,1)S(1)}, u32[]{:S(2)}, u32[]{:S(2)}) collective-permute-start(bf16[3,64,704]{2,1,0:T(8,128)(2,1)} %get-tuple-element.52), channel_id=1, source_target_pairs={{1,0},{2,1},{3,2},{4,3},{5,4},{6,5},{7,6},{8,7},{9,8},{10,9},{11,1... | collective-permute-start | bytes 811016 | tf_op jit(solution)/shard_map/ppermute | solution.py:424
  10.3 4.6 %collective-permute-start = (bf16[3,64,704]{2,1,0:T(8,128)(2,1)}, bf16[3,64,704]{2,1,0:T(8,128)(2,1)S(1)}, u32[]{:S(2)}, u32[]{:S(2)}) collective-permute-start(bf16[3,64,704]{2,1,0:T(8,128)(2,1)} %get-tuple-element.42), channel_id=1, source_target_pairs={{0,1},{1,2},{2,3},{3,4},{4,5},{5,6},{6,7},{7,8},{8,9},{9,10},{10,1... | collective-permute-start | bytes 811016 | tf_op jit(solution)/shard_map/ppermute | solution.py:425
  14.8 1.3 %collective-permute-start.1 = (bf16[3,64,704]{2,1,0:T(8,128)(2,1)}, bf16[3,64,704]{2,1,0:T(8,128)(2,1)}, u32[]{:S(2)}, u32[]{:S(2)}) collective-permute-start(bf16[3,64,704]{2,1,0:T(8,128)(2,1)} %get-tuple-element.43), channel_id=1, source_target_pairs={{1,0},{2,1},{3,2},{4,3},{5,4},{6,5},{7,6},{8,7},{9,8},{10,9},{11,1... | collective-permute-start | bytes 811016 | tf_op jit(solution)/shard_map/ppermute | solution.py:426
  16.2 3.3 %own.1 = (f32[6,4,80,128]{3,2,1,0:T(8,128)S(1)}, f32[6,49,8,128]{3,2,1,0:T(8,128)S(1)}, f32[6,4,64,128]{3,2,1,0:T(8,128)S(1)}, f32[64,128]{1,0:T(8,128)S(1)}) custom-call(s32[1,16]{1,0:T(1,128)S(1)} %copy-done.11, bf16[4,64,704]{2,1,0:T(8,128)(2,1)S(1)} %copy-done.2, f32[49,704]{1,0:T(8,128)S(1)} %copy-done.7), custom_call_target="tpu_custom_call" | custom-call | flops 1000000 | bytes 50000000 | tf_op jit(solution)/shard_map/own/pallas_call | solution.py:429
  19.5 1.0 %collective-permute-done.3.after = bf16[3,64,704]{2,1,0:T(8,128)(2,1)S(1)} collective-permute-done((bf16[3,64,704]{2,1,0:T(8,128)(2,1)}, bf16[3,64,704]{2,1,0:T(8,128)(2,1)S(1)}, u32[]{:S(2)}, u32[]{:S(2)}) %collective-permute-start.3) | collective-permute-done | bytes 270368 | tf_op jit(solution)/shard_map/ppermute | solution.py:424
  20.5 1.1 %copy-done.3 = bf16[1408,256]{1,0:T(8,128)(2,1)S(1)} copy-done((bf16[1408,256]{1,0:T(8,128)(2,1)S(1)}, bf16[1408,256]{1,0:T(8,128)(2,1)}, u32[]{:S(2)}) %copy-start.3) | copy-done | bytes 720920
  21.6 4.1 %back.1 = (bf16[256,704]{1,0:T(8,128)(2,1)S(1)}, bf16[4,88,704]{2,1,0:T(8,128)(2,1)S(1)}, bf16[4,88,704]{2,1,0:T(8,128)(2,1)}, bf16[4,88,704]{2,1,0:T(8,128)(2,1...) custom-call(s32[1]{0:T(128)} %bitcast.3.place, bf16[3,64,704]{2,1,0:T(8,128)(2,1)S(1)} %collective-permute-done.2.before, ...), custom_call_target="tpu_custom_call" | custom-call | flops 1000000 | bytes 1000000000 | tf_op jit(solution)/shard_map/back/pallas_call | solution.py:449
  25.7 1.7 %collective-permute-start.4 = (bf16[4,88,704]{2,1,0:T(8,128)(2,1)}, bf16[4,88,704]{2,1,0:T(8,128)(2,1)S(1)}, u32[]{:S(2)}, u32[]{:S(2)}) collective-permute-start(bf16[4,88,704]{2,1,0:T(8,128)(2,1)} %get-tuple-element.57), channel_id=1, source_target_pairs={{0,1},{1,2},{2,3},{3,0},{4,5},{5,6},{6,7},{7,4},{8,9},{9,10},{10,1... | collective-permute-start | bytes 1486856 | tf_op jit(solution)/shard_map/ppermute | solution.py:370
  27.4 4.5 %collective-permute-start.5 = (bf16[4,88,704]{2,1,0:T(8,128)(2,1)}, bf16[4,88,704]{2,1,0:T(8,128)(2,1)S(1)}, u32[]{:S(2)}, u32[]{:S(2)}) collective-permute-start(bf16[4,88,704]{2,1,0:T(8,128)(2,1)} %get-tuple-element.58), channel_id=1, source_target_pairs={{0,2},{1,3},{2,0},{3,1},{4,6},{5,7},{6,4},{7,5},{8,10},{9,11},{10,... | collective-permute-start | bytes 1486856 | tf_op jit(solution)/shard_map/ppermute | solution.py:370
  32.0 0.0 copy-start
  32.0 0.0 copy-start.8
  32.0 0.0 copy-start.9
  32.0 3.1 %grads.1 = f32[56,704]{1,0:T(8,128)S(1)} custom-call(bf16[4,64,704]{2,1,0:T(8,128)(2,1)S(1)} %copy-done.1, f32[6,4,80,128]{3,2,1,0:T(8,128)S(1)} %get-tuple-element.53.band.cots, f32[6,6,80,128]{3,2,1,0:T(8,128)S(1)} %get-tuple-element.64.halo), custom_call_target="tpu_custom_call" | custom-call | flops 1000000 | bytes 100000 | tf_op jit(solution)/shard_map/grads/pallas_call | solution.py:463
  35.2 2.4 %image.1 = (bf16[8,352,128]{2,1,0:T(8,128)(2,1)}, bf16[56,704]{1,0:T(8,128)(2,1)S(1)}) custom-call(bf16[256,704]{1,0:T(8,128)(2,1)S(1)} %get-tuple-element.62.pre, bf16[704,1408]{1,0:T(8,128)(2,1)S(1)} %bitcast.6, bf16[1408,256]{1,0:T(8,128)(2,1)S(1)} %copy-done.4, f32[8,256]{1,0:T(8,128)S(1)} %copy-done.8, f32[352]{0:T(512)S(1)} %copy-done.9, ...), custom_call_target="tpu_custom_call" | custom-call | flops 1000000 | bytes 100000 | tf_op jit(solution)/shard_map/image/pallas_call | solution.py:473
  37.6 5.9 %collective-permute-start.12 = (bf16[56,704]{1,0:T(8,128)(2,1)S(1)}, bf16[56,704]{1,0:T(8,128)(2,1)S(1)}, u32[]{:S(2)}, u32[]{:S(2)}) collective-permute-start(bf16[56,704]{1,0:T(8,128)(2,1)S(1)} %get-tuple-element.69), channel_id=1, source_target_pairs={{0,12},{1,13},{2,14},{3,15},{4,0},{5,1},{6,2},{7,3},{8,4},{9,5},{1... | collective-permute-start | bytes 236552 | tf_op jit(solution)/shard_map/ppermute | solution.py:370
  43.5 2.6 %collective-permute-done.12 = bf16[56,704]{1,0:T(8,128)(2,1)S(1)} collective-permute-done((bf16[56,704]{1,0:T(8,128)(2,1)S(1)}, bf16[56,704]{1,0:T(8,128)(2,1)S(1)}, u32[]{:S(2)}, u32[]{:S(2)}) %collective-permute-start.12) | collective-permute-done | bytes 78880 | tf_op jit(solution)/shard_map/ppermute | solution.py:370
  46.0 0.9 %collective-permute-start.10 = (bf16[56,704]{1,0:T(8,128)(2,1)S(1)}, bf16[56,704]{1,0:T(8,128)(2,1)S(1)}, u32[]{:S(2)}, u32[]{:S(2)}) collective-permute-start(bf16[56,704]{1,0:T(8,128)(2,1)S(1)} %get-tuple-element.69), channel_id=1, source_target_pairs={{0,8},{1,9},{2,10},{3,11},{4,12},{5,13},{6,14},{7,15},{8,0},{9,1},... | collective-permute-start | bytes 236552 | tf_op jit(solution)/shard_map/ppermute | solution.py:370
  47.0 2.8 %collective-permute-done.11 = bf16[56,704]{1,0:T(8,128)(2,1)S(1)} collective-permute-done((bf16[56,704]{1,0:T(8,128)(2,1)S(1)}, bf16[56,704]{1,0:T(8,128)(2,1)S(1)}, u32[]{:S(2)}, u32[]{:S(2)}) %collective-permute-start.11) | collective-permute-done | bytes 78880 | tf_op jit(solution)/shard_map/ppermute | solution.py:370
  49.8 1.7 %collective-permute-done.10 = bf16[56,704]{1,0:T(8,128)(2,1)S(1)} collective-permute-done((bf16[56,704]{1,0:T(8,128)(2,1)S(1)}, bf16[56,704]{1,0:T(8,128)(2,1)S(1)}, u32[]{:S(2)}, u32[]{:S(2)}) %collective-permute-start.10) | collective-permute-done | bytes 78880 | tf_op jit(solution)/shard_map/ppermute | solution.py:370
  51.5 0.9 %collective-permute-start.15 = (bf16[56,704]{1,0:T(8,128)(2,1)S(1)}, bf16[56,704]{1,0:T(8,128)(2,1)S(1)}, u32[]{:S(2)}, u32[]{:S(2)}) collective-permute-start(bf16[56,704]{1,0:T(8,128)(2,1)S(1)} %add_convert_fusion.t0), channel_id=1, source_target_pairs={{0,3},{1,0},{2,1},{3,2},{4,7},{5,4},{6,5},{7,6},{8,11},{9,8},{10,9... | collective-permute-start | bytes 236552 | tf_op jit(solution)/shard_map/ppermute | solution.py:370
  52.4 2.5 %collective-permute-done.5.c2 = bf16[4,88,704]{2,1,0:T(8,128)(2,1)S(1)} collective-permute-done((bf16[4,88,704]{2,1,0:T(8,128)(2,1)}, bf16[4,88,704]{2,1,0:T(8,128)(2,1)S(1)}, u32[]{:S(2)}, u32[]{:S(2)}) %collective-permute-start.5) | collective-permute-done | bytes 495648 | tf_op jit(solution)/shard_map/ppermute | solution.py:370
  54.9 0.5 collective-permute-done.6.c3
  55.4 1.3 %middle.1 = (bf16[88,704]{1,0:T(8,128)(2,1)S(1)}, bf16[88,704]{1,0:T(8,128)(2,1)S(1)}, bf16[88,704]{1,0:T(8,128)(2,1)S(1)}, bf16[88,704]{1,0:T(8,128)(2,1)S(1)}) custom-call(s32[1]{0:T(128)} %bitcast.2.place, bf16[4,88,704]{2,1,0:T(8,128)(2,1)S(1)} %get-tuple-element.56.c0, bf16[4,88,704]{2,1,0:T(8,128)(2,1)S(1)} %collective-permute-done.4.c1, ...), custom_call_target="tpu_custom_call" | custom-call | flops 1000000 | bytes 40000000 | tf_op jit(solution)/shard_map/middle/pallas_call | solution.py:482
  56.7 4.2 %collective-permute-start.7 = (bf16[88,704]{1,0:T(8,128)(2,1)S(1)}, bf16[88,704]{1,0:T(8,128)(2,1)S(1)}, u32[]{:S(2)}, u32[]{:S(2)}) collective-permute-start(bf16[88,704]{1,0:T(8,128)(2,1)S(1)} %get-tuple-element.66), channel_id=1, source_target_pairs={{0,4},{1,5},{2,6},{3,7},{4,8},{5,9},{6,10},{7,11},{8,12},{9,13},{1... | collective-permute-start | bytes 371720 | tf_op jit(solution)/shard_map/ppermute | solution.py:370
  60.9 3.3 %collective-permute-start.8 = (bf16[88,704]{1,0:T(8,128)(2,1)S(1)}, bf16[88,704]{1,0:T(8,128)(2,1)S(1)}, u32[]{:S(2)}, u32[]{:S(2)}) collective-permute-start(bf16[88,704]{1,0:T(8,128)(2,1)S(1)} %get-tuple-element.67), channel_id=1, source_target_pairs={{0,8},{1,9},{2,10},{3,11},{4,12},{5,13},{6,14},{7,15},{8,0},{9,1},... | collective-permute-start | bytes 371720 | tf_op jit(solution)/shard_map/ppermute | solution.py:370
  64.1 1.0 %collective-permute-start.9 = (bf16[88,704]{1,0:T(8,128)(2,1)S(1)}, bf16[88,704]{1,0:T(8,128)(2,1)S(1)}, u32[]{:S(2)}, u32[]{:S(2)}) collective-permute-start(bf16[88,704]{1,0:T(8,128)(2,1)S(1)} %get-tuple-element.68), channel_id=1, source_target_pairs={{0,12},{1,13},{2,14},{3,15},{4,0},{5,1},{6,2},{7,3},{8,4},{9,5},{1... | collective-permute-start | bytes 371720 | tf_op jit(solution)/shard_map/ppermute | solution.py:370
  65.1 0.9 %collective-permute-start.14 = (bf16[56,704]{1,0:T(8,128)(2,1)S(1)}, bf16[56,704]{1,0:T(8,128)(2,1)S(1)}, u32[]{:S(2)}, u32[]{:S(2)}) collective-permute-start(bf16[56,704]{1,0:T(8,128)(2,1)S(1)} %add_convert_fusion.t0), channel_id=1, source_target_pairs={{0,2},{1,3},{2,0},{3,1},{4,6},{5,7},{6,4},{7,5},{8,10},{9,11},{10,... | collective-permute-start | bytes 236552 | tf_op jit(solution)/shard_map/ppermute | solution.py:370
  66.0 1.8 %collective-permute-start.13 = (bf16[56,704]{1,0:T(8,128)(2,1)S(1)}, bf16[56,704]{1,0:T(8,128)(2,1)S(1)}, u32[]{:S(2)}, u32[]{:S(2)}) collective-permute-start(bf16[56,704]{1,0:T(8,128)(2,1)S(1)} %add_convert_fusion.t0), channel_id=1, source_target_pairs={{0,1},{1,2},{2,3},{3,0},{4,5},{5,6},{6,7},{7,4},{8,9},{9,10},{10,1... | collective-permute-start | bytes 236552 | tf_op jit(solution)/shard_map/ppermute | solution.py:370
  67.9 4.8 %front.1 = bf16[4,64,704]{2,1,0:T(8,128)(2,1)} custom-call(bf16[4,64,704]{2,1,0:T(8,128)(2,1)S(1)} %copy-done.1, bf16[3,64,704]{2,1,0:T(8,128)(2,1)S(1)} %copy-done.6, bf16[3,64,704]{2,1,0:T(8,128)(2,1)} %collective-permute-done.1.after, f32[6,49,8,128]{3,2,1,0:T(8,128)S(1)} %get-tuple-element.49.taps, f32[704]{0:T(1024)S(1)} %copy-done.10, ...), custom_call_target="tpu_custom_call" | custom-call | flops 1000000 | bytes 10000000 | tf_op jit(solution)/shard_map/front/pallas_call | solution.py:493
  72.7 0.8 %last.1 = (f32[88,704]{1,0:T(8,128)}, f32[352]{0:T(512)}, f32[704]{0:T(1024)}, f32[49,704]{1,0:T(8,128)}, f32[704]{0:T(1024)}) custom-call(bf16[88,704]{1,0:T(8,128)(2,1)S(1)} %get-tuple-element.60.w0, bf16[88,704]{1,0:T(8,128)(2,1)S(1)} %collective-permute-done.7.w1, bf16[88,704]{1,0:T(8,128)(2,1)S(1)} %collective-permute-done.8.w2, ...), custom_call_target="tpu_custom_call" | custom-call | flops 1000000 | bytes 100000 | tf_op jit(solution)/shard_map/last/pallas_call | solution.py:507
  (33 shorter events, 0.1 us)
Async XLA Ops:
  0.6 15.5 %copy-start.2 = (bf16[4,64,704]{2,1,0:T(8,128)(2,1)S(1)}, bf16[4,64,704]{2,1,0:T(8,128)(2,1)}, u32[]{:S(2)}) copy-start(bf16[4,64,704]{2,1,0:T(8,128)(2,1)} %cot_in.3) | copy-start | bytes 1081348
  0.6 15.5 %copy-start.7 = (f32[49,704]{1,0:T(8,128)S(1)}, f32[49,704]{1,0:T(8,128)}, u32[]{:S(2)}) copy-start(f32[49,704]{1,0:T(8,128)} %kernel_in.1) | copy-start | bytes 413956
  0.7 15.5 %copy-start.11 = (s32[1,16]{1,0:T(1,128)S(1)}, s32[1,16]{1,0:T(1,128)}, u32[]{:S(2)}) copy-start(s32[1,16]{1,0:T(1,128)} %vis_in.2) | copy-start | bytes 196
  5.5 14.0 %collective-permute-start.2 = (bf16[3,64,704]{2,1,0:T(8,128)(2,1)}, bf16[3,64,704]{2,1,0:T(8,128)(2,1)S(1)}, u32[]{:S(2)}, u32[]{:S(2)}) collective-permute-start(bf16[3,64,704]{2,1,0:T(8,128)(2,1)} %get-tuple-element.51), channel_id=1, source_target_pairs={{0,1},{1,2},{2,3},{3,4},{4,5},{5,6},{6,7},{7,8},{8,9},{9,10},{10,1... | collective-permute-start | bytes 811016 | tf_op jit(solution)/shard_map/ppermute | solution.py:423
  9.0 11.5 %collective-permute-start.3 = (bf16[3,64,704]{2,1,0:T(8,128)(2,1)}, bf16[3,64,704]{2,1,0:T(8,128)(2,1)S(1)}, u32[]{:S(2)}, u32[]{:S(2)}) collective-permute-start(bf16[3,64,704]{2,1,0:T(8,128)(2,1)} %get-tuple-element.52), channel_id=1, source_target_pairs={{1,0},{2,1},{3,2},{4,3},{5,4},{6,5},{7,6},{8,7},{9,8},{10,9},{11,1... | collective-permute-start | bytes 811016 | tf_op jit(solution)/shard_map/ppermute | solution.py:424
  10.3 21.7 %collective-permute-start = (bf16[3,64,704]{2,1,0:T(8,128)(2,1)}, bf16[3,64,704]{2,1,0:T(8,128)(2,1)S(1)}, u32[]{:S(2)}, u32[]{:S(2)}) collective-permute-start(bf16[3,64,704]{2,1,0:T(8,128)(2,1)} %get-tuple-element.42), channel_id=1, source_target_pairs={{0,1},{1,2},{2,3},{3,4},{4,5},{5,6},{6,7},{7,8},{8,9},{9,10},{10,1... | collective-permute-start | bytes 811016 | tf_op jit(solution)/shard_map/ppermute | solution.py:425
  14.8 17.1 %collective-permute-start.1 = (bf16[3,64,704]{2,1,0:T(8,128)(2,1)}, bf16[3,64,704]{2,1,0:T(8,128)(2,1)}, u32[]{:S(2)}, u32[]{:S(2)}) collective-permute-start(bf16[3,64,704]{2,1,0:T(8,128)(2,1)} %get-tuple-element.43), channel_id=1, source_target_pairs={{1,0},{2,1},{3,2},{4,3},{5,4},{6,5},{7,6},{8,7},{9,8},{10,9},{11,1... | collective-permute-start | bytes 811016 | tf_op jit(solution)/shard_map/ppermute | solution.py:426
  20.5 1.1 %copy-start.3 = (bf16[1408,256]{1,0:T(8,128)(2,1)S(1)}, bf16[1408,256]{1,0:T(8,128)(2,1)}, u32[]{:S(2)}) copy-start(bf16[1408,256]{1,0:T(8,128)(2,1)} %get-tuple-element.55.patches) | copy-start | bytes 2162692
  21.6 10.4 %copy-start.1 = (bf16[4,64,704]{2,1,0:T(8,128)(2,1)S(1)}, bf16[4,64,704]{2,1,0:T(8,128)(2,1)}, u32[]{:S(2)}) copy-start(bf16[4,64,704]{2,1,0:T(8,128)(2,1)} %get-tuple-element.44.down) | copy-start | bytes 1081348
  25.7 26.7 %collective-permute-start.4 = (bf16[4,88,704]{2,1,0:T(8,128)(2,1)}, bf16[4,88,704]{2,1,0:T(8,128)(2,1)S(1)}, u32[]{:S(2)}, u32[]{:S(2)}) collective-permute-start(bf16[4,88,704]{2,1,0:T(8,128)(2,1)} %get-tuple-element.57), channel_id=1, source_target_pairs={{0,1},{1,2},{2,3},{3,0},{4,5},{5,6},{6,7},{7,4},{8,9},{9,10},{10,1... | collective-permute-start | bytes 1486856 | tf_op jit(solution)/shard_map/ppermute | solution.py:370
  27.4 27.5 %collective-permute-start.5 = (bf16[4,88,704]{2,1,0:T(8,128)(2,1)}, bf16[4,88,704]{2,1,0:T(8,128)(2,1)S(1)}, u32[]{:S(2)}, u32[]{:S(2)}) collective-permute-start(bf16[4,88,704]{2,1,0:T(8,128)(2,1)} %get-tuple-element.58), channel_id=1, source_target_pairs={{0,2},{1,3},{2,0},{3,1},{4,6},{5,7},{6,4},{7,5},{8,10},{9,11},{10,... | collective-permute-start | bytes 1486856 | tf_op jit(solution)/shard_map/ppermute | solution.py:370
  31.9 23.4 %collective-permute-start.6 = (bf16[4,88,704]{2,1,0:T(8,128)(2,1)}, bf16[4,88,704]{2,1,0:T(8,128)(2,1)}, u32[]{:S(2)}, u32[]{:S(2)}) collective-permute-start(bf16[4,88,704]{2,1,0:T(8,128)(2,1)} %get-tuple-element.59), channel_id=1, source_target_pairs={{0,3},{1,0},{2,1},{3,2},{4,7},{5,4},{6,5},{7,6},{8,11},{9,8},{10,9... | collective-permute-start | bytes 1486856 | tf_op jit(solution)/shard_map/ppermute | solution.py:370
  31.9 3.2 %copy-start.5 = (bf16[3,64,704]{2,1,0:T(8,128)(2,1)}, bf16[3,64,704]{2,1,0:T(8,128)(2,1)S(1)}, u32[]{:S(2)}) copy-start(bf16[3,64,704]{2,1,0:T(8,128)(2,1)S(1)} %collective-permute-done.before) | copy-start | bytes 811012
  32.0 3.2 %copy-start = (bf16[1408,704]{0,1:T(8,128)(2,1)S(1)}, bf16[1408,704]{0,1:T(8,128)(2,1)}, u32[]{:S(2)}) copy-start(bf16[1408,704]{0,1:T(8,128)(2,1)} %param.11) | copy-start | bytes 5947396
  32.0 3.2 %copy-start.4 = (bf16[1408,256]{1,0:T(8,128)(2,1)S(1)}, bf16[1408,256]{1,0:T(8,128)(2,1)}, u32[]{:S(2)}) copy-start(bf16[1408,256]{1,0:T(8,128)(2,1)} %get-tuple-element.63.normed) | copy-start | bytes 2162692
  32.0 3.2 %copy-start.8 = (f32[8,256]{1,0:T(8,128)S(1)}, f32[8,256]{1,0:T(8,128)}, u32[]{:S(2)}) copy-start(f32[8,256]{1,0:T(8,128)} %get-tuple-element.47.rstd) | copy-start | bytes 24580
  32.0 3.2 %copy-start.9 = (f32[352]{0:T(512)S(1)}, f32[352]{0:T(512)}, u32[]{:S(2)}) copy-start(f32[352]{0:T(512)} %gain.1) | copy-start | bytes 4228
  37.6 30.3 %copy-start.10 = (f32[704]{0:T(1024)S(1)}, f32[704]{0:T(1024)}, u32[]{:S(2)}) copy-start(f32[704]{0:T(1024)} %bias.1) | copy-start | bytes 8452
  37.6 8.5 %collective-permute-start.12 = (bf16[56,704]{1,0:T(8,128)(2,1)S(1)}, bf16[56,704]{1,0:T(8,128)(2,1)S(1)}, u32[]{:S(2)}, u32[]{:S(2)}) collective-permute-start(bf16[56,704]{1,0:T(8,128)(2,1)S(1)} %get-tuple-element.69), channel_id=1, source_target_pairs={{0,12},{1,13},{2,14},{3,15},{4,0},{5,1},{6,2},{7,3},{8,4},{9,5},{1... | collective-permute-start | bytes 236552 | tf_op jit(solution)/shard_map/ppermute | solution.py:370
  43.5 6.3 %collective-permute-start.11 = (bf16[56,704]{1,0:T(8,128)(2,1)S(1)}, bf16[56,704]{1,0:T(8,128)(2,1)S(1)}, u32[]{:S(2)}, u32[]{:S(2)}) collective-permute-start(bf16[56,704]{1,0:T(8,128)(2,1)S(1)} %get-tuple-element.69), channel_id=1, source_target_pairs={{0,4},{1,5},{2,6},{3,7},{4,8},{5,9},{6,10},{7,11},{8,12},{9,13},{1... | collective-permute-start | bytes 236552 | tf_op jit(solution)/shard_map/ppermute | solution.py:370
  46.0 5.4 %collective-permute-start.10 = (bf16[56,704]{1,0:T(8,128)(2,1)S(1)}, bf16[56,704]{1,0:T(8,128)(2,1)S(1)}, u32[]{:S(2)}, u32[]{:S(2)}) collective-permute-start(bf16[56,704]{1,0:T(8,128)(2,1)S(1)} %get-tuple-element.69), channel_id=1, source_target_pairs={{0,8},{1,9},{2,10},{3,11},{4,12},{5,13},{6,14},{7,15},{8,0},{9,1},... | collective-permute-start | bytes 236552 | tf_op jit(solution)/shard_map/ppermute | solution.py:370
  51.5 14.6 %collective-permute-start.15 = (bf16[56,704]{1,0:T(8,128)(2,1)S(1)}, bf16[56,704]{1,0:T(8,128)(2,1)S(1)}, u32[]{:S(2)}, u32[]{:S(2)}) collective-permute-start(bf16[56,704]{1,0:T(8,128)(2,1)S(1)} %add_convert_fusion.t0), channel_id=1, source_target_pairs={{0,3},{1,0},{2,1},{3,2},{4,7},{5,4},{6,5},{7,6},{8,11},{9,8},{10,9... | collective-permute-start | bytes 236552 | tf_op jit(solution)/shard_map/ppermute | solution.py:370
  52.4 15.5 %copy-start.6 = (bf16[3,64,704]{2,1,0:T(8,128)(2,1)S(1)}, bf16[3,64,704]{2,1,0:T(8,128)(2,1)}, u32[]{:S(2)}) copy-start(bf16[3,64,704]{2,1,0:T(8,128)(2,1)} %copy-done.5) | copy-start | bytes 811012
  56.7 16.0 %collective-permute-start.7 = (bf16[88,704]{1,0:T(8,128)(2,1)S(1)}, bf16[88,704]{1,0:T(8,128)(2,1)S(1)}, u32[]{:S(2)}, u32[]{:S(2)}) collective-permute-start(bf16[88,704]{1,0:T(8,128)(2,1)S(1)} %get-tuple-element.66), channel_id=1, source_target_pairs={{0,4},{1,5},{2,6},{3,7},{4,8},{5,9},{6,10},{7,11},{8,12},{9,13},{1... | collective-permute-start | bytes 371720 | tf_op jit(solution)/shard_map/ppermute | solution.py:370
  60.9 11.8 %collective-permute-start.8 = (bf16[88,704]{1,0:T(8,128)(2,1)S(1)}, bf16[88,704]{1,0:T(8,128)(2,1)S(1)}, u32[]{:S(2)}, u32[]{:S(2)}) collective-permute-start(bf16[88,704]{1,0:T(8,128)(2,1)S(1)} %get-tuple-element.67), channel_id=1, source_target_pairs={{0,8},{1,9},{2,10},{3,11},{4,12},{5,13},{6,14},{7,15},{8,0},{9,1},... | collective-permute-start | bytes 371720 | tf_op jit(solution)/shard_map/ppermute | solution.py:370
  64.1 8.5 %collective-permute-start.9 = (bf16[88,704]{1,0:T(8,128)(2,1)S(1)}, bf16[88,704]{1,0:T(8,128)(2,1)S(1)}, u32[]{:S(2)}, u32[]{:S(2)}) collective-permute-start(bf16[88,704]{1,0:T(8,128)(2,1)S(1)} %get-tuple-element.68), channel_id=1, source_target_pairs={{0,12},{1,13},{2,14},{3,15},{4,0},{5,1},{6,2},{7,3},{8,4},{9,5},{1... | collective-permute-start | bytes 371720 | tf_op jit(solution)/shard_map/ppermute | solution.py:370
  65.1 7.5 %collective-permute-start.14 = (bf16[56,704]{1,0:T(8,128)(2,1)S(1)}, bf16[56,704]{1,0:T(8,128)(2,1)S(1)}, u32[]{:S(2)}, u32[]{:S(2)}) collective-permute-start(bf16[56,704]{1,0:T(8,128)(2,1)S(1)} %add_convert_fusion.t0), channel_id=1, source_target_pairs={{0,2},{1,3},{2,0},{3,1},{4,6},{5,7},{6,4},{7,5},{8,10},{9,11},{10,... | collective-permute-start | bytes 236552 | tf_op jit(solution)/shard_map/ppermute | solution.py:370
  66.0 6.6 %collective-permute-start.13 = (bf16[56,704]{1,0:T(8,128)(2,1)S(1)}, bf16[56,704]{1,0:T(8,128)(2,1)S(1)}, u32[]{:S(2)}, u32[]{:S(2)}) collective-permute-start(bf16[56,704]{1,0:T(8,128)(2,1)S(1)} %add_convert_fusion.t0), channel_id=1, source_target_pairs={{0,1},{1,2},{2,3},{3,0},{4,5},{5,6},{6,7},{7,4},{8,9},{9,10},{10,1... | collective-permute-start | bytes 236552 | tf_op jit(solution)/shard_map/ppermute | solution.py:370

commit v6 on v5

--- a/solution.py
+++ b/solution.py
@@ -186,11 +186,7 @@
     lax.fori_loop(0, 2 * len(tiles), step, 0)
 
 
-def back_kernel(
-    place, before, after, band, taps, part, mask, patches,
-    pre, c0, c1, c2, c3, halo, total, prod,
-):
-    chunks = (c0, c1, c2, c3)
+def back_kernel(before, after, band, taps, part, mask, pre, halo, total):
     height, width = part.shape[1:3]
     chans = pre.shape[1]
     tiles = tiles_of(chans)
@@ -221,7 +217,10 @@
 
     lax.fori_loop(0, 2 * len(tiles), step, 0)
     pre[...] = total[:, :chans].astype(BF16)
-    scale = 1.0 / math.sqrt(height * 16 * width)
+
+def product_kernel(place, patches, pre, c0, c1, c2, c3, prod):
+    chunks = (c0, c1, c2, c3)
+    scale = 1.0 / math.sqrt(pre.shape[0] * 16)
     depth = patches.shape[0] // 4
     share = depth // 4
     for k in range(4):
@@ -340,16 +339,18 @@
 
 
 def middle_kernel(place, c0, c1, c2, c3, *outs):
-    for k in range(4):
-        to = lax.rem(place[0] + k, 4)
-        outs[k][...] = sum_four(c0[to], c1[to], c2[to], c3[to]).astype(BF16)
+    for k in (1, 2, 3):
+        to = jnp.bitwise_xor(place[0], k)
+        outs[k - 1][...] = sum_four(c0[to], c1[to], c2[to], c3[to]).astype(BF16)
 
 
 def last_kernel(
-    w0, w1, w2, w3, t0, t1, t2, t3,
+    place, c0, c1, c2, c3, w1, w2, w3, t0, t1, t2, t3,
     weight, gain, bias, kernel, depth_bias,
 ):
-    weight[...] = sum_four(w0[...], w1[...], w2[...], w3[...])
+    z = place[0]
+    own = sum_four(c0[z], c1[z], c2[z], c3[z])
+    weight[...] = sum_four(own, w1[...], w2[...], w3[...])
     total = sum_four(t0[...], t1[...], t2[...], t3[...])
     taps = KS * KS
     kernel[...] = total[:taps]
@@ -384,7 +385,7 @@
     low = [(j, i) for i, j in up]
     ring = [(z, y) for z in range(4) for y in range(4)]
     along_y = [[(4 * z + y, 4 * z + (y + k) % 4) for z, y in ring] for k in (1, 2, 3)]
-    along_z = [[(4 * z + y, 4 * ((z + k) % 4) + y) for z, y in ring] for k in (1, 2, 3)]
+    along_z = [[(4 * z + y, 4 * (z ^ k) + y) for z, y in ring] for k in (1, 2, 3)]
     tiles = len(tiles_of(chans))
     share = in_chans // 4
     halo = sd((3, width, chans), BF16)
@@ -446,17 +447,22 @@
         5 * 10**7,
     )(vis_own, cotangent, depth_kernel)
 
-    pre, *chunks, halo_rows = call(
+    pre, halo_rows = call(
         back_kernel,
-        (sd((pixels, chans), BF16),)
-        + (sd((4, share, chans), BF16),) * 4
-        + (sd((tiles, 6, span, LANES), F32),),
-        [SM] + [VM] * 7,
-        [pltpu.VMEM((pixels, tiles * LANES), F32), pltpu.VMEM((in_chans, chans), F32)],
+        (sd((pixels, chans), BF16), sd((tiles, 6, span, LANES), F32)),
+        [VM] * 6,
+        [pltpu.VMEM((pixels, tiles * LANES), F32)],
         "back",
         16,
         10**9,
-    )(place_y, cot_before, cot_after, band, taps, part, mask, patches)
+    )(cot_before, cot_after, band, taps, part, mask)
+    chunks = call(
+        product_kernel,
+        [sd((4, share, chans), BF16)] * 4,
+        [SM] + [VM] * 2,
+        [pltpu.VMEM((in_chans, chans), F32)],
+        "product",
+    )(place_y, patches, pre)
     got = send(chunks[1:], along_y)
     down, down_before, down_after = lax.optimization_barrier((down, down_before, down_after))
 
@@ -481,14 +487,14 @@
     got_t = send([small] * 3, along_z)
     parts = call(
         middle_kernel,
-        (sd((share, chans), BF16),) * 4,
+        (sd((share, chans), BF16),) * 3,
         [SM] + [VM] * 4,
         [],
         "middle",
         16,
         4 * 10**7,
     )(place_z, chunks[0], *got)
-    got_w = send(parts[1:], along_z)
+    got_w = send(parts, along_z)
     front_mask, _ = lax.optimization_barrier((mask, parts[0]))
     features = call(
         front_kernel,
@@ -513,10 +519,10 @@
             sd((KS * KS, chans), F32),
             sd((chans,), F32),
         ),
-        [VM] * 8,
+        [SM] + [VM] * 11,
         [],
         "last",
-    )(parts[0], *got_w, small, *got_t)
+    )(place_z, chunks[0], *got, *got_w, small, *got_t)
     return (
         features,
         image_grad,

time: 74 us -> 72.8 us (0.984)
  waiting for transfers between devices: 11 us -> 6.62 us
  starting transfers between devices: 35.8 us -> 39.8 us
  local copies, waits for them, and re-layouts: 1.16 us -> 0.06 us
    ppermute x12, waiting for transfers between devices: 9.96 us -> 6.61 us  [send(): lax.ppermute(value, 'rows', pair)]
    ppermute x12, starting transfers between devices: 25.2 us -> 28.4 us  [send(): lax.ppermute(value, 'rows', pair)]
    pallas_call x2 -> x3, Pallas kernels: 5.46 us -> 4.32 us  [the longest x1 2.38 us: body(): call(product_kernel, [sd((4, share, chans), BF16)] * 4, [SM] + [VM] * 2,...]
    unnamed x24 -> x22, local copies, waits for them, and re-layouts: 1.16 us -> 0.06 us
    ppermute x1, waiting for transfers between devices: 1 us -> 0.01 us  [body(): cot_after = lax.ppermute(cot_first, 'rows', low)]
    pallas_call x1, Pallas kernels: 0.82 us -> 1.78 us  [body(): call(last_kernel, (sd((share, chans), F32), sd((in_chans,), F32), sd((cha...]
  transfers between devices with their start and end apart: 16 -> 16, of which waited for: 6 -> 4; matrix products, arithmetic and copies ran while one was open for 0% -> 0% of each run, Pallas kernels for 26% -> 25%
where the time goes in v6:
time: 72.8 us; the launch traced here: 71.9 us
  starting transfers between devices  39.8 us (55%)
  Pallas kernels  24.5 us (34%)
  waiting for transfers between devices  6.62 us (9%)
  between operations  0.88 us (1%)
    ppermute x12, starting transfers between devices, send(): lax.ppermute(value, 'rows', pair)  28.4 us
    ppermute x12, waiting for transfers between devices, send(): lax.ppermute(value, 'rows', pair)  6.61 us
    ppermute x1, starting transfers between devices, body(): down_before = lax.ppermute(down_last, 'rows', up)  5.28 us
    pallas_call x1, Pallas kernels, body(): call(front_kernel, sd((height, width, chans), BF16), [VM] * 6, [pltpu.VME...  4.85 us
    pallas_call x1, Pallas kernels, body(): call(reduce_kernel, (halo, halo, sd((4 * in_chans, pixels), BF16), sd((4...  4.78 us
    ppermute x1, starting transfers between devices, body(): cot_before = lax.ppermute(cot_last, 'rows', up)  3.5 us
    pallas_call x1, Pallas kernels, body(): call(own_kernel, (sd((tiles, height, span, LANES), F32), sd((tiles, KS *...  3.33 us
    pallas_call x1, Pallas kernels, body(): call(grad_kernel, sd((56, chans), F32), [VM] * 3, [pltpu.VMEM((tiles, hei...  3.1 us
  transfers between devices with their start and end apart: 16, of which 4 were waited for; matrix products, arithmetic and copies ran while one was open for 0% of the time, Pallas kernels for 25%

profile of v6, /device:TPU:2, one launch (start us, length us, event | category | flops | bytes accessed | tf_op | source)
XLA Modules:
  0.0 71.9 jit_solution(1669048656982531853)
XLA Ops:
  0.7 4.8 %reduce.1 = (bf16[3,64,704]{2,1,0:T(8,128)(2,1)}, bf16[3,64,704]{2,1,0:T(8,128)(2,1)}, bf16[1408,256]{1,0:T(8,128)(2,1)}, bf16[1408,256]{1,0:T(8,128)(2,1)}, f32...) custom-call(s32[1,16]{1,0:T(1,128)} %vis_in.2, ...), custom_call_target="tpu_custom_call" | custom-call | flops 1000000 | bytes 20000000 | tf_op jit(solution)/shard_map/reduce/pallas_call | solution.py:396
  5.5 3.5 %collective-permute-start.2 = (bf16[3,64,704]{2,1,0:T(8,128)(2,1)}, bf16[3,64,704]{2,1,0:T(8,128)(2,1)S(1)}, u32[]{:S(2)}, u32[]{:S(2)}) collective-permute-start(bf16[3,64,704]{2,1,0:T(8,128)(2,1)} %get-tuple-element.51), channel_id=1, source_target_pairs={{0,1},{1,2},{2,3},{3,4},{4,5},{5,6},{6,7},{7,8},{8,9},{9,10},{10,1... | collective-permute-start | bytes 811016 | tf_op jit(solution)/shard_map/ppermute | solution.py:424
  9.0 1.3 %collective-permute-start.3 = (bf16[3,64,704]{2,1,0:T(8,128)(2,1)}, bf16[3,64,704]{2,1,0:T(8,128)(2,1)S(1)}, u32[]{:S(2)}, u32[]{:S(2)}) collective-permute-start(bf16[3,64,704]{2,1,0:T(8,128)(2,1)} %get-tuple-element.52), channel_id=1, source_target_pairs={{1,0},{2,1},{3,2},{4,3},{5,4},{6,5},{7,6},{8,7},{9,8},{10,9},{11,1... | collective-permute-start | bytes 811016 | tf_op jit(solution)/shard_map/ppermute | solution.py:425
  10.3 5.3 %collective-permute-start = (bf16[3,64,704]{2,1,0:T(8,128)(2,1)}, bf16[3,64,704]{2,1,0:T(8,128)(2,1)}, u32[]{:S(2)}, u32[]{:S(2)}) collective-permute-start(bf16[3,64,704]{2,1,0:T(8,128)(2,1)} %get-tuple-element.41), channel_id=1, source_target_pairs={{0,1},{1,2},{2,3},{3,4},{4,5},{5,6},{6,7},{7,8},{8,9},{9,10},{10,1... | collective-permute-start | bytes 811016 | tf_op jit(solution)/shard_map/ppermute | solution.py:426
  15.5 1.3 %collective-permute-start.1 = (bf16[3,64,704]{2,1,0:T(8,128)(2,1)}, bf16[3,64,704]{2,1,0:T(8,128)(2,1)}, u32[]{:S(2)}, u32[]{:S(2)}) collective-permute-start(bf16[3,64,704]{2,1,0:T(8,128)(2,1)} %get-tuple-element.42), channel_id=1, source_target_pairs={{1,0},{2,1},{3,2},{4,3},{5,4},{6,5},{7,6},{8,7},{9,8},{10,9},{11,1... | collective-permute-start | bytes 811016 | tf_op jit(solution)/shard_map/ppermute | solution.py:427
  16.9 3.3 %own.1 = (f32[6,4,80,128]{3,2,1,0:T(8,128)S(1)}, f32[6,49,8,128]{3,2,1,0:T(8,128)S(1)}, f32[6,4,64,128]{3,2,1,0:T(8,128)S(1)}, f32[64,128]{1,0:T(8,128)S(1)}) custom-call(s32[1,16]{1,0:T(1,128)S(1)} %copy-done.10, bf16[4,64,704]{2,1,0:T(8,128)(2,1)S(1)} %copy-done.3, f32[49,704]{1,0:T(8,128)S(1)} %copy-done.6), custom_call_target="tpu_custom_call" | custom-call | flops 1000000 | bytes 50000000 | tf_op jit(solution)/shard_map/own/pallas_call | solution.py:430
  20.2 0.0 copy-start.4
  20.2 0.0 copy-start.1
  20.3 1.7 %back.1 = (bf16[256,704]{1,0:T(8,128)(2,1)S(1)}, f32[6,6,80,128]{3,2,1,0:T(8,128)S(1)}) custom-call(bf16[3,64,704]{2,1,0:T(8,128)(2,1)S(1)} %collective-permute-done.2.before, bf16[3,64,704]{2,1,0:T(8,128)(2,1)S(1)} %collective-permute-done.3.after, f32[6,4,80,128]{3,2,1,0:T(8,128)S(1)} %get-tuple-element.53.band.cots, ...), custom_call_target="tpu_custom_call" | custom-call | flops 1000000 | bytes 1000000000 | tf_op jit(solution)/shard_map/back/pallas_call | solution.py:450
  22.0 2.4 %product.1 = (bf16[4,88,704]{2,1,0:T(8,128)(2,1)S(1)}, bf16[4,88,704]{2,1,0:T(8,128)(2,1)}, bf16[4,88,704]{2,1,0:T(8,128)(2,1)}, bf16[4,88,704]{2,1,0:T(8,128)(2,1)}) custom-call(s32[1]{0:T(128)} %bitcast.3.place, bf16[1408,256]{1,0:T(8,128)(2,1)S(1)} %copy-done.4, bf16[256,704]{1,0:T(8,128)(2,1)S(1)} %get-tuple-element.55.pre), custom_call_target="tpu_custom_call" | custom-call | flops 1000000 | bytes 100000 | tf_op jit(solution)/shard_map/product/pallas_call | solution.py:459
  24.4 2.6 %collective-permute-start.4 = (bf16[4,88,704]{2,1,0:T(8,128)(2,1)}, bf16[4,88,704]{2,1,0:T(8,128)(2,1)S(1)}, u32[]{:S(2)}, u32[]{:S(2)}) collective-permute-start(bf16[4,88,704]{2,1,0:T(8,128)(2,1)} %get-tuple-element.57), channel_id=1, source_target_pairs={{0,1},{1,2},{2,3},{3,0},{4,5},{5,6},{6,7},{7,4},{8,9},{9,10},{10,1... | collective-permute-start | bytes 1486856 | tf_op jit(solution)/shard_map/ppermute | solution.py:371
  27.0 3.8 %collective-permute-start.5 = (bf16[4,88,704]{2,1,0:T(8,128)(2,1)}, bf16[4,88,704]{2,1,0:T(8,128)(2,1)S(1)}, u32[]{:S(2)}, u32[]{:S(2)}) collective-permute-start(bf16[4,88,704]{2,1,0:T(8,128)(2,1)} %get-tuple-element.58), channel_id=1, source_target_pairs={{0,2},{1,3},{2,0},{3,1},{4,6},{5,7},{6,4},{7,5},{8,10},{9,11},{10,... | collective-permute-start | bytes 1486856 | tf_op jit(solution)/shard_map/ppermute | solution.py:371
  30.9 0.0 copy-start
  30.9 0.0 copy-start.7
  30.9 0.0 copy-start.8
  30.9 3.1 %grads.1 = f32[56,704]{1,0:T(8,128)S(1)} custom-call(bf16[4,64,704]{2,1,0:T(8,128)(2,1)S(1)} %copy-done.1, f32[6,4,80,128]{3,2,1,0:T(8,128)S(1)} %get-tuple-element.53.band.cots, f32[6,6,80,128]{3,2,1,0:T(8,128)S(1)} %get-tuple-element.63.halo), custom_call_target="tpu_custom_call" | custom-call | flops 1000000 | bytes 100000 | tf_op jit(solution)/shard_map/grads/pallas_call | solution.py:469
  34.1 2.3 %image.1 = (bf16[8,352,128]{2,1,0:T(8,128)(2,1)}, bf16[56,704]{1,0:T(8,128)(2,1)S(1)}) custom-call(bf16[256,704]{1,0:T(8,128)(2,1)S(1)} %get-tuple-element.55.pre, bf16[704,1408]{1,0:T(8,128)(2,1)S(1)} %bitcast.6, bf16[1408,256]{1,0:T(8,128)(2,1)S(1)} %copy-done.5, f32[8,256]{1,0:T(8,128)S(1)} %copy-done.7, f32[352]{0:T(512)S(1)} %copy-done.8, ...), custom_call_target="tpu_custom_call" | custom-call | flops 1000000 | bytes 100000 | tf_op jit(solution)/shard_map/image/pallas_call | solution.py:479
  36.4 4.6 %collective-permute-start.10 = (bf16[56,704]{1,0:T(8,128)(2,1)S(1)}, bf16[56,704]{1,0:T(8,128)(2,1)S(1)}, u32[]{:S(2)}, u32[]{:S(2)}) collective-permute-start(bf16[56,704]{1,0:T(8,128)(2,1)S(1)} %get-tuple-element.67), channel_id=1, source_target_pairs={{0,8},{1,9},{2,10},{3,11},{4,12},{5,13},{6,14},{7,15},{8,0},{9,1},... | collective-permute-start | bytes 236552 | tf_op jit(solution)/shard_map/ppermute | solution.py:371
  41.0 1.9 %collective-permute-start.11 = (bf16[56,704]{1,0:T(8,128)(2,1)S(1)}, bf16[56,704]{1,0:T(8,128)(2,1)S(1)}, u32[]{:S(2)}, u32[]{:S(2)}) collective-permute-start(bf16[56,704]{1,0:T(8,128)(2,1)S(1)} %get-tuple-element.67), channel_id=1, source_target_pairs={{0,4},{1,5},{2,6},{3,7},{4,0},{5,1},{6,2},{7,3},{8,12},{9,13},{10,... | collective-permute-start | bytes 236552 | tf_op jit(solution)/shard_map/ppermute | solution.py:371
  42.9 0.6 collective-permute-done.10
  43.5 5.6 %collective-permute-start.12 = (bf16[56,704]{1,0:T(8,128)(2,1)S(1)}, bf16[56,704]{1,0:T(8,128)(2,1)S(1)}, u32[]{:S(2)}, u32[]{:S(2)}) collective-permute-start(bf16[56,704]{1,0:T(8,128)(2,1)S(1)} %get-tuple-element.67), channel_id=1, source_target_pairs={{0,12},{1,13},{2,14},{3,15},{4,8},{5,9},{6,10},{7,11},{8,4},{9,5},... | collective-permute-start | bytes 236552 | tf_op jit(solution)/shard_map/ppermute | solution.py:371
  49.1 2.5 %collective-permute-done.12 = bf16[56,704]{1,0:T(8,128)(2,1)S(1)} collective-permute-done((bf16[56,704]{1,0:T(8,128)(2,1)S(1)}, bf16[56,704]{1,0:T(8,128)(2,1)S(1)}, u32[]{:S(2)}, u32[]{:S(2)}) %collective-permute-start.12) | collective-permute-done | bytes 78880 | tf_op jit(solution)/shard_map/ppermute | solution.py:371
  51.6 0.9 %collective-permute-start.13 = (bf16[56,704]{1,0:T(8,128)(2,1)S(1)}, bf16[56,704]{1,0:T(8,128)(2,1)}, u32[]{:S(2)}, u32[]{:S(2)}) collective-permute-start(bf16[56,704]{1,0:T(8,128)(2,1)S(1)} %add_convert_fusion.t0), channel_id=1, source_target_pairs={{0,1},{1,2},{2,3},{3,0},{4,5},{5,6},{6,7},{7,4},{8,9},{9,10},{10,1... | collective-permute-start | bytes 236552 | tf_op jit(solution)/shard_map/ppermute | solution.py:371
  52.6 2.2 %collective-permute-done.5.c2 = bf16[4,88,704]{2,1,0:T(8,128)(2,1)S(1)} collective-permute-done((bf16[4,88,704]{2,1,0:T(8,128)(2,1)}, bf16[4,88,704]{2,1,0:T(8,128)(2,1)S(1)}, u32[]{:S(2)}, u32[]{:S(2)}) %collective-permute-start.5) | collective-permute-done | bytes 495648 | tf_op jit(solution)/shard_map/ppermute | solution.py:371
  54.7 0.2 middle.1
  54.9 3.0 %collective-permute-start.7 = (bf16[88,704]{1,0:T(8,128)(2,1)S(1)}, bf16[88,704]{1,0:T(8,128)(2,1)S(1)}, u32[]{:S(2)}, u32[]{:S(2)}) collective-permute-start(bf16[88,704]{1,0:T(8,128)(2,1)S(1)} %get-tuple-element.60), channel_id=1, source_target_pairs={{0,4},{1,5},{2,6},{3,7},{4,0},{5,1},{6,2},{7,3},{8,12},{9,13},{10,... | collective-permute-start | bytes 371720 | tf_op jit(solution)/shard_map/ppermute | solution.py:371
  57.9 3.3 %collective-permute-start.8 = (bf16[88,704]{1,0:T(8,128)(2,1)S(1)}, bf16[88,704]{1,0:T(8,128)(2,1)S(1)}, u32[]{:S(2)}, u32[]{:S(2)}) collective-permute-start(bf16[88,704]{1,0:T(8,128)(2,1)S(1)} %get-tuple-element.65), channel_id=1, source_target_pairs={{0,8},{1,9},{2,10},{3,11},{4,12},{5,13},{6,14},{7,15},{8,0},{9,1},... | collective-permute-start | bytes 371720 | tf_op jit(solution)/shard_map/ppermute | solution.py:371
  61.3 0.6 collective-permute-start.14
  61.9 2.0 %collective-permute-start.15 = (bf16[56,704]{1,0:T(8,128)(2,1)S(1)}, bf16[56,704]{1,0:T(8,128)(2,1)S(1)}, u32[]{:S(2)}, u32[]{:S(2)}) collective-permute-start(bf16[56,704]{1,0:T(8,128)(2,1)S(1)} %add_convert_fusion.t0), channel_id=1, source_target_pairs={{0,3},{1,0},{2,1},{3,2},{4,7},{5,4},{6,5},{7,6},{8,11},{9,8},{10,9... | collective-permute-start | bytes 236552 | tf_op jit(solution)/shard_map/ppermute | solution.py:371
  63.9 4.8 %front.1 = bf16[4,64,704]{2,1,0:T(8,128)(2,1)} custom-call(bf16[4,64,704]{2,1,0:T(8,128)(2,1)S(1)} %copy-done.2, bf16[3,64,704]{2,1,0:T(8,128)(2,1)} %collective-permute-done.before, bf16[3,64,704]{2,1,0:T(8,128)(2,1)} %collective-permute-done.1.after, f32[6,49,8,128]{3,2,1,0:T(8,128)S(1)} %get-tuple-element.48.taps, f32[704]{0:T(1024)S(1)} %copy-done.9, ...), custom_call_target="tpu_custom_call" | custom-call | flops 1000000 | bytes 10000000 | tf_op jit(solution)/shard_map/front/pallas_call | solution.py:499
  68.7 1.4 %collective-permute-done.8.w2 = bf16[88,704]{1,0:T(8,128)(2,1)S(1)} collective-permute-done((bf16[88,704]{1,0:T(8,128)(2,1)S(1)}, bf16[88,704]{1,0:T(8,128)(2,1)S(1)}, u32[]{:S(2)}, u32[]{:S(2)}) %collective-permute-start.8) | collective-permute-done | bytes 123936 | tf_op jit(solution)/shard_map/ppermute | solution.py:371
  70.1 1.8 %last.1 = (f32[88,704]{1,0:T(8,128)}, f32[352]{0:T(512)}, f32[704]{0:T(1024)}, f32[49,704]{1,0:T(8,128)}, f32[704]{0:T(1024)}) custom-call(s32[1]{0:T(128)} %bitcast.2.place, bf16[4,88,704]{2,1,0:T(8,128)(2,1)S(1)} %get-tuple-element.56.c0, bf16[4,88,704]{2,1,0:T(8,128)(2,1)S(1)} %collective-permute-done.4.c1, ...), custom_call_target="tpu_custom_call" | custom-call | flops 1000000 | bytes 100000 | tf_op jit(solution)/shard_map/last/pallas_call | solution.py:513
  (32 shorter events, 0.1 us)
Async XLA Ops:
  0.6 16.2 %copy-start.3 = (bf16[4,64,704]{2,1,0:T(8,128)(2,1)S(1)}, bf16[4,64,704]{2,1,0:T(8,128)(2,1)}, u32[]{:S(2)}) copy-start(bf16[4,64,704]{2,1,0:T(8,128)(2,1)} %cot_in.3) | copy-start | bytes 1081348
  0.6 16.2 %copy-start.6 = (f32[49,704]{1,0:T(8,128)S(1)}, f32[49,704]{1,0:T(8,128)}, u32[]{:S(2)}) copy-start(f32[49,704]{1,0:T(8,128)} %kernel_in.1) | copy-start | bytes 413956
  0.7 16.2 %copy-start.10 = (s32[1,16]{1,0:T(1,128)S(1)}, s32[1,16]{1,0:T(1,128)}, u32[]{:S(2)}) copy-start(s32[1,16]{1,0:T(1,128)} %vis_in.2) | copy-start | bytes 196
  5.5 14.8 %collective-permute-start.2 = (bf16[3,64,704]{2,1,0:T(8,128)(2,1)}, bf16[3,64,704]{2,1,0:T(8,128)(2,1)S(1)}, u32[]{:S(2)}, u32[]{:S(2)}) collective-permute-start(bf16[3,64,704]{2,1,0:T(8,128)(2,1)} %get-tuple-element.51), channel_id=1, source_target_pairs={{0,1},{1,2},{2,3},{3,4},{4,5},{5,6},{6,7},{7,8},{8,9},{9,10},{10,1... | collective-permute-start | bytes 811016 | tf_op jit(solution)/shard_map/ppermute | solution.py:424
  9.0 11.3 %collective-permute-start.3 = (bf16[3,64,704]{2,1,0:T(8,128)(2,1)}, bf16[3,64,704]{2,1,0:T(8,128)(2,1)S(1)}, u32[]{:S(2)}, u32[]{:S(2)}) collective-permute-start(bf16[3,64,704]{2,1,0:T(8,128)(2,1)} %get-tuple-element.52), channel_id=1, source_target_pairs={{1,0},{2,1},{3,2},{4,3},{5,4},{6,5},{7,6},{8,7},{9,8},{10,9},{11,1... | collective-permute-start | bytes 811016 | tf_op jit(solution)/shard_map/ppermute | solution.py:425
  10.3 20.6 %collective-permute-start = (bf16[3,64,704]{2,1,0:T(8,128)(2,1)}, bf16[3,64,704]{2,1,0:T(8,128)(2,1)}, u32[]{:S(2)}, u32[]{:S(2)}) collective-permute-start(bf16[3,64,704]{2,1,0:T(8,128)(2,1)} %get-tuple-element.41), channel_id=1, source_target_pairs={{0,1},{1,2},{2,3},{3,4},{4,5},{5,6},{6,7},{7,8},{8,9},{9,10},{10,1... | collective-permute-start | bytes 811016 | tf_op jit(solution)/shard_map/ppermute | solution.py:426
  15.5 15.3 %collective-permute-start.1 = (bf16[3,64,704]{2,1,0:T(8,128)(2,1)}, bf16[3,64,704]{2,1,0:T(8,128)(2,1)}, u32[]{:S(2)}, u32[]{:S(2)}) collective-permute-start(bf16[3,64,704]{2,1,0:T(8,128)(2,1)} %get-tuple-element.42), channel_id=1, source_target_pairs={{1,0},{2,1},{3,2},{4,3},{5,4},{6,5},{7,6},{8,7},{9,8},{10,9},{11,1... | collective-permute-start | bytes 811016 | tf_op jit(solution)/shard_map/ppermute | solution.py:427
  20.2 1.8 %copy-start.4 = (bf16[1408,256]{1,0:T(8,128)(2,1)S(1)}, bf16[1408,256]{1,0:T(8,128)(2,1)}, u32[]{:S(2)}) copy-start(bf16[1408,256]{1,0:T(8,128)(2,1)} %get-tuple-element.50.patches) | copy-start | bytes 2162692
  20.2 10.6 %copy-start.1 = (bf16[4,64,704]{2,1,0:T(8,128)(2,1)S(1)}, bf16[4,64,704]{2,1,0:T(8,128)(2,1)}, u32[]{:S(2)}) copy-start(bf16[4,64,704]{2,1,0:T(8,128)(2,1)} %get-tuple-element.43.down) | copy-start | bytes 1081348
  24.4 28.2 %collective-permute-start.4 = (bf16[4,88,704]{2,1,0:T(8,128)(2,1)}, bf16[4,88,704]{2,1,0:T(8,128)(2,1)S(1)}, u32[]{:S(2)}, u32[]{:S(2)}) collective-permute-start(bf16[4,88,704]{2,1,0:T(8,128)(2,1)} %get-tuple-element.57), channel_id=1, source_target_pairs={{0,1},{1,2},{2,3},{3,0},{4,5},{5,6},{6,7},{7,4},{8,9},{9,10},{10,1... | collective-permute-start | bytes 1486856 | tf_op jit(solution)/shard_map/ppermute | solution.py:371
  27.0 27.7 %collective-permute-start.5 = (bf16[4,88,704]{2,1,0:T(8,128)(2,1)}, bf16[4,88,704]{2,1,0:T(8,128)(2,1)S(1)}, u32[]{:S(2)}, u32[]{:S(2)}) collective-permute-start(bf16[4,88,704]{2,1,0:T(8,128)(2,1)} %get-tuple-element.58), channel_id=1, source_target_pairs={{0,2},{1,3},{2,0},{3,1},{4,6},{5,7},{6,4},{7,5},{8,10},{9,11},{10,... | collective-permute-start | bytes 1486856 | tf_op jit(solution)/shard_map/ppermute | solution.py:371
  30.9 23.9 %collective-permute-start.6 = (bf16[4,88,704]{2,1,0:T(8,128)(2,1)}, bf16[4,88,704]{2,1,0:T(8,128)(2,1)S(1)}, u32[]{:S(2)}, u32[]{:S(2)}) collective-permute-start(bf16[4,88,704]{2,1,0:T(8,128)(2,1)} %get-tuple-element.59), channel_id=1, source_target_pairs={{0,3},{1,0},{2,1},{3,2},{4,7},{5,4},{6,5},{7,6},{8,11},{9,8},{10,9... | collective-permute-start | bytes 1486856 | tf_op jit(solution)/shard_map/ppermute | solution.py:371
  30.9 3.2 %copy-start = (bf16[1408,704]{0,1:T(8,128)(2,1)S(1)}, bf16[1408,704]{0,1:T(8,128)(2,1)}, u32[]{:S(2)}) copy-start(bf16[1408,704]{0,1:T(8,128)(2,1)} %param.11) | copy-start | bytes 5947396
  30.9 3.2 %copy-start.5 = (bf16[1408,256]{1,0:T(8,128)(2,1)S(1)}, bf16[1408,256]{1,0:T(8,128)(2,1)}, u32[]{:S(2)}) copy-start(bf16[1408,256]{1,0:T(8,128)(2,1)} %get-tuple-element.62.normed) | copy-start | bytes 2162692
  30.9 3.2 %copy-start.7 = (f32[8,256]{1,0:T(8,128)S(1)}, f32[8,256]{1,0:T(8,128)}, u32[]{:S(2)}) copy-start(f32[8,256]{1,0:T(8,128)} %get-tuple-element.46.rstd) | copy-start | bytes 24580
  30.9 3.1 %copy-start.8 = (f32[352]{0:T(512)S(1)}, f32[352]{0:T(512)}, u32[]{:S(2)}) copy-start(f32[352]{0:T(512)} %gain.1) | copy-start | bytes 4228
  36.4 27.4 %copy-start.9 = (f32[704]{0:T(1024)S(1)}, f32[704]{0:T(1024)}, u32[]{:S(2)}) copy-start(f32[704]{0:T(1024)} %bias.1) | copy-start | bytes 8452
  36.4 7.1 %collective-permute-start.10 = (bf16[56,704]{1,0:T(8,128)(2,1)S(1)}, bf16[56,704]{1,0:T(8,128)(2,1)S(1)}, u32[]{:S(2)}, u32[]{:S(2)}) collective-permute-start(bf16[56,704]{1,0:T(8,128)(2,1)S(1)} %get-tuple-element.67), channel_id=1, source_target_pairs={{0,8},{1,9},{2,10},{3,11},{4,12},{5,13},{6,14},{7,15},{8,0},{9,1},... | collective-permute-start | bytes 236552 | tf_op jit(solution)/shard_map/ppermute | solution.py:371
  41.0 8.1 %collective-permute-start.11 = (bf16[56,704]{1,0:T(8,128)(2,1)S(1)}, bf16[56,704]{1,0:T(8,128)(2,1)S(1)}, u32[]{:S(2)}, u32[]{:S(2)}) collective-permute-start(bf16[56,704]{1,0:T(8,128)(2,1)S(1)} %get-tuple-element.67), channel_id=1, source_target_pairs={{0,4},{1,5},{2,6},{3,7},{4,0},{5,1},{6,2},{7,3},{8,12},{9,13},{10,... | collective-permute-start | bytes 236552 | tf_op jit(solution)/shard_map/ppermute | solution.py:371
  43.5 8.1 %collective-permute-start.12 = (bf16[56,704]{1,0:T(8,128)(2,1)S(1)}, bf16[56,704]{1,0:T(8,128)(2,1)S(1)}, u32[]{:S(2)}, u32[]{:S(2)}) collective-permute-start(bf16[56,704]{1,0:T(8,128)(2,1)S(1)} %get-tuple-element.67), channel_id=1, source_target_pairs={{0,12},{1,13},{2,14},{3,15},{4,8},{5,9},{6,10},{7,11},{8,4},{9,5},... | collective-permute-start | bytes 236552 | tf_op jit(solution)/shard_map/ppermute | solution.py:371
  51.6 10.3 %collective-permute-start.13 = (bf16[56,704]{1,0:T(8,128)(2,1)S(1)}, bf16[56,704]{1,0:T(8,128)(2,1)}, u32[]{:S(2)}, u32[]{:S(2)}) collective-permute-start(bf16[56,704]{1,0:T(8,128)(2,1)S(1)} %add_convert_fusion.t0), channel_id=1, source_target_pairs={{0,1},{1,2},{2,3},{3,0},{4,5},{5,6},{6,7},{7,4},{8,9},{9,10},{10,1... | collective-permute-start | bytes 236552 | tf_op jit(solution)/shard_map/ppermute | solution.py:371
  52.5 11.3 %copy-start.2 = (bf16[4,64,704]{2,1,0:T(8,128)(2,1)S(1)}, bf16[4,64,704]{2,1,0:T(8,128)(2,1)}, u32[]{:S(2)}) copy-start(bf16[4,64,704]{2,1,0:T(8,128)(2,1)} %get-tuple-element.43.down) | copy-start | bytes 1081348
  54.9 13.8 %collective-permute-start.7 = (bf16[88,704]{1,0:T(8,128)(2,1)S(1)}, bf16[88,704]{1,0:T(8,128)(2,1)S(1)}, u32[]{:S(2)}, u32[]{:S(2)}) collective-permute-start(bf16[88,704]{1,0:T(8,128)(2,1)S(1)} %get-tuple-element.60), channel_id=1, source_target_pairs={{0,4},{1,5},{2,6},{3,7},{4,0},{5,1},{6,2},{7,3},{8,12},{9,13},{10,... | collective-permute-start | bytes 371720 | tf_op jit(solution)/shard_map/ppermute | solution.py:371
  57.9 12.2 %collective-permute-start.8 = (bf16[88,704]{1,0:T(8,128)(2,1)S(1)}, bf16[88,704]{1,0:T(8,128)(2,1)S(1)}, u32[]{:S(2)}, u32[]{:S(2)}) collective-permute-start(bf16[88,704]{1,0:T(8,128)(2,1)S(1)} %get-tuple-element.65), channel_id=1, source_target_pairs={{0,8},{1,9},{2,10},{3,11},{4,12},{5,13},{6,14},{7,15},{8,0},{9,1},... | collective-permute-start | bytes 371720 | tf_op jit(solution)/shard_map/ppermute | solution.py:371
  61.3 8.9 %collective-permute-start.9 = (bf16[88,704]{1,0:T(8,128)(2,1)S(1)}, bf16[88,704]{1,0:T(8,128)(2,1)S(1)}, u32[]{:S(2)}, u32[]{:S(2)}) collective-permute-start(bf16[88,704]{1,0:T(8,128)(2,1)S(1)} %get-tuple-element.66), channel_id=1, source_target_pairs={{0,12},{1,13},{2,14},{3,15},{4,8},{5,9},{6,10},{7,11},{8,4},{9,5},... | collective-permute-start | bytes 371720 | tf_op jit(solution)/shard_map/ppermute | solution.py:371
  61.3 7.5 %collective-permute-start.14 = (bf16[56,704]{1,0:T(8,128)(2,1)S(1)}, bf16[56,704]{1,0:T(8,128)(2,1)S(1)}, u32[]{:S(2)}, u32[]{:S(2)}) collective-permute-start(bf16[56,704]{1,0:T(8,128)(2,1)S(1)} %add_convert_fusion.t0), channel_id=1, source_target_pairs={{0,2},{1,3},{2,0},{3,1},{4,6},{5,7},{6,4},{7,5},{8,10},{9,11},{10,... | collective-permute-start | bytes 236552 | tf_op jit(solution)/shard_map/ppermute | solution.py:371
  61.9 6.8 %collective-permute-start.15 = (bf16[56,704]{1,0:T(8,128)(2,1)S(1)}, bf16[56,704]{1,0:T(8,128)(2,1)S(1)}, u32[]{:S(2)}, u32[]{:S(2)}) collective-permute-start(bf16[56,704]{1,0:T(8,128)(2,1)S(1)} %add_convert_fusion.t0), channel_id=1, source_target_pairs={{0,3},{1,0},{2,1},{3,2},{4,7},{5,4},{6,5},{7,6},{8,11},{9,8},{10,9... | collective-permute-start | bytes 236552 | tf_op jit(solution)/shard_map/ppermute | solution.py:371

commit v7 on v6

--- a/solution.py
+++ b/solution.py
@@ -345,7 +345,7 @@
 
 
 def last_kernel(
-    place, c0, c1, c2, c3, w1, w2, w3, t0, t1, t2, t3,
+    place, c0, c1, c2, c3, w2, w3, w1, t0, t1, t2, t3,
     weight, gain, bias, kernel, depth_bias,
 ):
     z = place[0]
@@ -494,7 +494,7 @@
         16,
         4 * 10**7,
     )(place_z, chunks[0], *got)
-    got_w = send(parts, along_z)
+    got_w = send([parts[k] for k in (1, 2, 0)], [along_z[k] for k in (1, 2, 0)])
     front_mask, _ = lax.optimization_barrier((mask, parts[0]))
     features = call(
         front_kernel,

time: 72.8 us -> 72.1 us (level)
  the two profiles are of different devices: /device:TPU:2 before, /device:TPU:95 now
where the time goes in v7:
time: 72.1 us; the launch traced here: 71.8 us
  Pallas kernels  24.5 us (34%)
  starting transfers between devices  24 us (33%)
  waiting for transfers between devices  22.4 us (31%)
  between operations  0.9 us (1%)
    ppermute x12, waiting for transfers between devices, send(): lax.ppermute(value, 'rows', pair)  22.4 us
    ppermute x12, starting transfers between devices, send(): lax.ppermute(value, 'rows', pair)  11.4 us
    ppermute x1, starting transfers between devices, body(): down_before = lax.ppermute(down_last, 'rows', up)  5.32 us
    pallas_call x1, Pallas kernels, body(): call(front_kernel, sd((height, width, chans), BF16), [VM] * 6, [pltpu.VME...  4.85 us
    pallas_call x1, Pallas kernels, body(): call(reduce_kernel, (halo, halo, sd((4 * in_chans, pixels), BF16), sd((4...  4.78 us
    pallas_call x1, Pallas kernels, body(): call(own_kernel, (sd((tiles, height, span, LANES), F32), sd((tiles, KS *...  3.33 us
    ppermute x1, starting transfers between devices, body(): cot_before = lax.ppermute(cot_last, 'rows', up)  3.21 us
    pallas_call x1, Pallas kernels, body(): call(grad_kernel, sd((56, chans), F32), [VM] * 3, [pltpu.VMEM((tiles, hei...  3.1 us
  transfers between devices with their start and end apart: 16, of which 5 were waited for; matrix products, arithmetic and copies ran while one was open for 0% of the time, Pallas kernels for 25%

profile of v7, /device:TPU:95, one launch (start us, length us, event | category | flops | bytes accessed | tf_op | source)
XLA Modules:
  0.0 71.8 jit_solution(17019734173403928156)
XLA Ops:
  0.7 4.8 %reduce.1 = (bf16[3,64,704]{2,1,0:T(8,128)(2,1)}, bf16[3,64,704]{2,1,0:T(8,128)(2,1)}, bf16[1408,256]{1,0:T(8,128)(2,1)}, bf16[1408,256]{1,0:T(8,128)(2,1)}, f32...) custom-call(s32[1,16]{1,0:T(1,128)} %vis_in.2, ...), custom_call_target="tpu_custom_call" | custom-call | flops 1000000 | bytes 20000000 | tf_op jit(solution)/shard_map/reduce/pallas_call | solution.py:396
  5.5 3.2 %collective-permute-start.2 = (bf16[3,64,704]{2,1,0:T(8,128)(2,1)}, bf16[3,64,704]{2,1,0:T(8,128)(2,1)S(1)}, u32[]{:S(2)}, u32[]{:S(2)}) collective-permute-start(bf16[3,64,704]{2,1,0:T(8,128)(2,1)} %get-tuple-element.51), channel_id=1, source_target_pairs={{0,1},{1,2},{2,3},{3,4},{4,5},{5,6},{6,7},{7,8},{8,9},{9,10},{10,1... | collective-permute-start | bytes 811016 | tf_op jit(solution)/shard_map/ppermute | solution.py:424
  8.7 2.1 %collective-permute-start.3 = (bf16[3,64,704]{2,1,0:T(8,128)(2,1)}, bf16[3,64,704]{2,1,0:T(8,128)(2,1)S(1)}, u32[]{:S(2)}, u32[]{:S(2)}) collective-permute-start(bf16[3,64,704]{2,1,0:T(8,128)(2,1)} %get-tuple-element.52), channel_id=1, source_target_pairs={{1,0},{2,1},{3,2},{4,3},{5,4},{6,5},{7,6},{8,7},{9,8},{10,9},{11,1... | collective-permute-start | bytes 811016 | tf_op jit(solution)/shard_map/ppermute | solution.py:425
  10.7 5.3 %collective-permute-start = (bf16[3,64,704]{2,1,0:T(8,128)(2,1)}, bf16[3,64,704]{2,1,0:T(8,128)(2,1)}, u32[]{:S(2)}, u32[]{:S(2)}) collective-permute-start(bf16[3,64,704]{2,1,0:T(8,128)(2,1)} %get-tuple-element.41), channel_id=1, source_target_pairs={{0,1},{1,2},{2,3},{3,4},{4,5},{5,6},{6,7},{7,8},{8,9},{9,10},{10,1... | collective-permute-start | bytes 811016 | tf_op jit(solution)/shard_map/ppermute | solution.py:426
  16.1 1.9 %collective-permute-start.1 = (bf16[3,64,704]{2,1,0:T(8,128)(2,1)}, bf16[3,64,704]{2,1,0:T(8,128)(2,1)}, u32[]{:S(2)}, u32[]{:S(2)}) collective-permute-start(bf16[3,64,704]{2,1,0:T(8,128)(2,1)} %get-tuple-element.42), channel_id=1, source_target_pairs={{1,0},{2,1},{3,2},{4,3},{5,4},{6,5},{7,6},{8,7},{9,8},{10,9},{11,1... | collective-permute-start | bytes 811016 | tf_op jit(solution)/shard_map/ppermute | solution.py:427
  18.0 3.3 %own.1 = (f32[6,4,80,128]{3,2,1,0:T(8,128)S(1)}, f32[6,49,8,128]{3,2,1,0:T(8,128)S(1)}, f32[6,4,64,128]{3,2,1,0:T(8,128)S(1)}, f32[64,128]{1,0:T(8,128)S(1)}) custom-call(s32[1,16]{1,0:T(1,128)S(1)} %copy-done.10, bf16[4,64,704]{2,1,0:T(8,128)(2,1)S(1)} %copy-done.3, f32[49,704]{1,0:T(8,128)S(1)} %copy-done.6), custom_call_target="tpu_custom_call" | custom-call | flops 1000000 | bytes 50000000 | tf_op jit(solution)/shard_map/own/pallas_call | solution.py:430
  21.4 0.0 copy-start.4
  21.4 0.0 copy-start.1
  21.4 1.7 %back.1 = (bf16[256,704]{1,0:T(8,128)(2,1)S(1)}, f32[6,6,80,128]{3,2,1,0:T(8,128)S(1)}) custom-call(bf16[3,64,704]{2,1,0:T(8,128)(2,1)S(1)} %collective-permute-done.2.before, bf16[3,64,704]{2,1,0:T(8,128)(2,1)S(1)} %collective-permute-done.3.after, f32[6,4,80,128]{3,2,1,0:T(8,128)S(1)} %get-tuple-element.53.band.cots, ...), custom_call_target="tpu_custom_call" | custom-call | flops 1000000 | bytes 1000000000 | tf_op jit(solution)/shard_map/back/pallas_call | solution.py:450
  23.2 2.4 %product.1 = (bf16[4,88,704]{2,1,0:T(8,128)(2,1)S(1)}, bf16[4,88,704]{2,1,0:T(8,128)(2,1)}, bf16[4,88,704]{2,1,0:T(8,128)(2,1)}, bf16[4,88,704]{2,1,0:T(8,128)(2,1)}) custom-call(s32[1]{0:T(128)} %bitcast.3.place, bf16[1408,256]{1,0:T(8,128)(2,1)S(1)} %copy-done.4, bf16[256,704]{1,0:T(8,128)(2,1)S(1)} %get-tuple-element.55.pre), custom_call_target="tpu_custom_call" | custom-call | flops 1000000 | bytes 100000 | tf_op jit(solution)/shard_map/product/pallas_call | solution.py:459
  25.6 2.2 %collective-permute-start.4 = (bf16[4,88,704]{2,1,0:T(8,128)(2,1)}, bf16[4,88,704]{2,1,0:T(8,128)(2,1)S(1)}, u32[]{:S(2)}, u32[]{:S(2)}) collective-permute-start(bf16[4,88,704]{2,1,0:T(8,128)(2,1)} %get-tuple-element.57), channel_id=1, source_target_pairs={{0,1},{1,2},{2,3},{3,0},{4,5},{5,6},{6,7},{7,4},{8,9},{9,10},{10,1... | collective-permute-start | bytes 1486856 | tf_op jit(solution)/shard_map/ppermute | solution.py:371
  27.8 0.6 collective-permute-start.6
  28.4 0.0 copy-start
  28.4 0.0 copy-start.7
  28.4 0.0 copy-start.8
  28.4 3.1 %grads.1 = f32[56,704]{1,0:T(8,128)S(1)} custom-call(bf16[4,64,704]{2,1,0:T(8,128)(2,1)S(1)} %copy-done.1, f32[6,4,80,128]{3,2,1,0:T(8,128)S(1)} %get-tuple-element.53.band.cots, f32[6,6,80,128]{3,2,1,0:T(8,128)S(1)} %get-tuple-element.63.halo), custom_call_target="tpu_custom_call" | custom-call | flops 1000000 | bytes 100000 | tf_op jit(solution)/shard_map/grads/pallas_call | solution.py:469
  31.6 2.3 %image.1 = (bf16[8,352,128]{2,1,0:T(8,128)(2,1)}, bf16[56,704]{1,0:T(8,128)(2,1)S(1)}) custom-call(bf16[256,704]{1,0:T(8,128)(2,1)S(1)} %get-tuple-element.55.pre, bf16[704,1408]{1,0:T(8,128)(2,1)S(1)} %bitcast.6, bf16[1408,256]{1,0:T(8,128)(2,1)S(1)} %copy-done.5, f32[8,256]{1,0:T(8,128)S(1)} %copy-done.7, f32[352]{0:T(512)S(1)} %copy-done.8, ...), custom_call_target="tpu_custom_call" | custom-call | flops 1000000 | bytes 100000 | tf_op jit(solution)/shard_map/image/pallas_call | solution.py:479
  33.9 1.6 %collective-permute-start.11 = (bf16[56,704]{1,0:T(8,128)(2,1)S(1)}, bf16[56,704]{1,0:T(8,128)(2,1)S(1)}, u32[]{:S(2)}, u32[]{:S(2)}) collective-permute-start(bf16[56,704]{1,0:T(8,128)(2,1)S(1)} %get-tuple-element.67), channel_id=1, source_target_pairs={{0,4},{1,5},{2,6},{3,7},{4,0},{5,1},{6,2},{7,3},{8,12},{9,13},{10,... | collective-permute-start | bytes 236552 | tf_op jit(solution)/shard_map/ppermute | solution.py:371
  35.5 2.9 %collective-permute-done.10 = bf16[56,704]{1,0:T(8,128)(2,1)S(1)} collective-permute-done((bf16[56,704]{1,0:T(8,128)(2,1)S(1)}, bf16[56,704]{1,0:T(8,128)(2,1)S(1)}, u32[]{:S(2)}, u32[]{:S(2)}) %collective-permute-start.10) | collective-permute-done | bytes 78880 | tf_op jit(solution)/shard_map/ppermute | solution.py:371
  38.4 0.5 collective-permute-start.12
  38.9 4.2 %collective-permute-done.12 = bf16[56,704]{1,0:T(8,128)(2,1)S(1)} collective-permute-done((bf16[56,704]{1,0:T(8,128)(2,1)S(1)}, bf16[56,704]{1,0:T(8,128)(2,1)S(1)}, u32[]{:S(2)}, u32[]{:S(2)}) %collective-permute-start.12) | collective-permute-done | bytes 78880 | tf_op jit(solution)/shard_map/ppermute | solution.py:371
  43.1 2.2 %collective-permute-start.13 = (bf16[56,704]{1,0:T(8,128)(2,1)S(1)}, bf16[56,704]{1,0:T(8,128)(2,1)}, u32[]{:S(2)}, u32[]{:S(2)}) collective-permute-start(bf16[56,704]{1,0:T(8,128)(2,1)S(1)} %add_convert_fusion.t0), channel_id=1, source_target_pairs={{0,1},{1,2},{2,3},{3,0},{4,5},{5,6},{6,7},{7,4},{8,9},{9,10},{10,1... | collective-permute-start | bytes 236552 | tf_op jit(solution)/shard_map/ppermute | solution.py:371
  45.3 9.3 %collective-permute-done.6.c3 = bf16[4,88,704]{2,1,0:T(8,128)(2,1)S(1)} collective-permute-done((bf16[4,88,704]{2,1,0:T(8,128)(2,1)}, bf16[4,88,704]{2,1,0:T(8,128)(2,1)S(1)}, u32[]{:S(2)}, u32[]{:S(2)}) %collective-permute-start.6) | collective-permute-done | bytes 495648 | tf_op jit(solution)/shard_map/ppermute | solution.py:371
  54.6 0.2 middle.1
  54.8 0.1 collective-permute-start.7
  54.9 2.8 %collective-permute-start.8 = (bf16[88,704]{1,0:T(8,128)(2,1)S(1)}, bf16[88,704]{1,0:T(8,128)(2,1)S(1)}, u32[]{:S(2)}, u32[]{:S(2)}) collective-permute-start(bf16[88,704]{1,0:T(8,128)(2,1)S(1)} %get-tuple-element.66), channel_id=1, source_target_pairs={{0,12},{1,13},{2,14},{3,15},{4,8},{5,9},{6,10},{7,11},{8,4},{9,5},... | collective-permute-start | bytes 371720 | tf_op jit(solution)/shard_map/ppermute | solution.py:371
  57.7 0.7 %collective-permute-start.9 = (bf16[88,704]{1,0:T(8,128)(2,1)S(1)}, bf16[88,704]{1,0:T(8,128)(2,1)S(1)}, u32[]{:S(2)}, u32[]{:S(2)}) collective-permute-start(bf16[88,704]{1,0:T(8,128)(2,1)S(1)} %get-tuple-element.60), channel_id=1, source_target_pairs={{0,4},{1,5},{2,6},{3,7},{4,0},{5,1},{6,2},{7,3},{8,12},{9,13},{10,... | collective-permute-start | bytes 371720 | tf_op jit(solution)/shard_map/ppermute | solution.py:371
  58.5 0.8 %collective-permute-start.14 = (bf16[56,704]{1,0:T(8,128)(2,1)S(1)}, bf16[56,704]{1,0:T(8,128)(2,1)S(1)}, u32[]{:S(2)}, u32[]{:S(2)}) collective-permute-start(bf16[56,704]{1,0:T(8,128)(2,1)S(1)} %add_convert_fusion.t0), channel_id=1, source_target_pairs={{0,2},{1,3},{2,0},{3,1},{4,6},{5,7},{6,4},{7,5},{8,10},{9,11},{10,... | collective-permute-start | bytes 236552 | tf_op jit(solution)/shard_map/ppermute | solution.py:371
  59.2 4.8 %front.1 = bf16[4,64,704]{2,1,0:T(8,128)(2,1)} custom-call(bf16[4,64,704]{2,1,0:T(8,128)(2,1)S(1)} %copy-done.2, bf16[3,64,704]{2,1,0:T(8,128)(2,1)} %collective-permute-done.before, bf16[3,64,704]{2,1,0:T(8,128)(2,1)} %collective-permute-done.1.after, f32[6,49,8,128]{3,2,1,0:T(8,128)S(1)} %get-tuple-element.48.taps, f32[704]{0:T(1024)S(1)} %copy-done.9, ...), custom_call_target="tpu_custom_call" | custom-call | flops 1000000 | bytes 10000000 | tf_op jit(solution)/shard_map/front/pallas_call | solution.py:499
  64.1 0.1 collective-permute-done.15.t3
  64.2 5.8 %collective-permute-done.8.w3 = bf16[88,704]{1,0:T(8,128)(2,1)S(1)} collective-permute-done((bf16[88,704]{1,0:T(8,128)(2,1)S(1)}, bf16[88,704]{1,0:T(8,128)(2,1)S(1)}, u32[]{:S(2)}, u32[]{:S(2)}) %collective-permute-start.8) | collective-permute-done | bytes 123936 | tf_op jit(solution)/shard_map/ppermute | solution.py:371
  70.1 1.8 %last.1 = (f32[88,704]{1,0:T(8,128)}, f32[352]{0:T(512)}, f32[704]{0:T(1024)}, f32[49,704]{1,0:T(8,128)}, f32[704]{0:T(1024)}) custom-call(s32[1]{0:T(128)} %bitcast.2.place, bf16[4,88,704]{2,1,0:T(8,128)(2,1)S(1)} %get-tuple-element.56.c0, bf16[4,88,704]{2,1,0:T(8,128)(2,1)S(1)} %collective-permute-done.4.c1, ...), custom_call_target="tpu_custom_call" | custom-call | flops 1000000 | bytes 100000 | tf_op jit(solution)/shard_map/last/pallas_call | solution.py:513
  (32 shorter events, 0.1 us)
Async XLA Ops:
  0.6 17.4 %copy-start.3 = (bf16[4,64,704]{2,1,0:T(8,128)(2,1)S(1)}, bf16[4,64,704]{2,1,0:T(8,128)(2,1)}, u32[]{:S(2)}) copy-start(bf16[4,64,704]{2,1,0:T(8,128)(2,1)} %cot_in.3) | copy-start | bytes 1081348
  0.6 17.4 %copy-start.6 = (f32[49,704]{1,0:T(8,128)S(1)}, f32[49,704]{1,0:T(8,128)}, u32[]{:S(2)}) copy-start(f32[49,704]{1,0:T(8,128)} %kernel_in.1) | copy-start | bytes 413956
  0.7 17.4 %copy-start.10 = (s32[1,16]{1,0:T(1,128)S(1)}, s32[1,16]{1,0:T(1,128)}, u32[]{:S(2)}) copy-start(s32[1,16]{1,0:T(1,128)} %vis_in.2) | copy-start | bytes 196
  5.5 15.9 %collective-permute-start.2 = (bf16[3,64,704]{2,1,0:T(8,128)(2,1)}, bf16[3,64,704]{2,1,0:T(8,128)(2,1)S(1)}, u32[]{:S(2)}, u32[]{:S(2)}) collective-permute-start(bf16[3,64,704]{2,1,0:T(8,128)(2,1)} %get-tuple-element.51), channel_id=1, source_target_pairs={{0,1},{1,2},{2,3},{3,4},{4,5},{5,6},{6,7},{7,8},{8,9},{9,10},{10,1... | collective-permute-start | bytes 811016 | tf_op jit(solution)/shard_map/ppermute | solution.py:424
  8.7 12.7 %collective-permute-start.3 = (bf16[3,64,704]{2,1,0:T(8,128)(2,1)}, bf16[3,64,704]{2,1,0:T(8,128)(2,1)S(1)}, u32[]{:S(2)}, u32[]{:S(2)}) collective-permute-start(bf16[3,64,704]{2,1,0:T(8,128)(2,1)} %get-tuple-element.52), channel_id=1, source_target_pairs={{1,0},{2,1},{3,2},{4,3},{5,4},{6,5},{7,6},{8,7},{9,8},{10,9},{11,1... | collective-permute-start | bytes 811016 | tf_op jit(solution)/shard_map/ppermute | solution.py:425
  10.7 17.6 %collective-permute-start = (bf16[3,64,704]{2,1,0:T(8,128)(2,1)}, bf16[3,64,704]{2,1,0:T(8,128)(2,1)}, u32[]{:S(2)}, u32[]{:S(2)}) collective-permute-start(bf16[3,64,704]{2,1,0:T(8,128)(2,1)} %get-tuple-element.41), channel_id=1, source_target_pairs={{0,1},{1,2},{2,3},{3,4},{4,5},{5,6},{6,7},{7,8},{8,9},{9,10},{10,1... | collective-permute-start | bytes 811016 | tf_op jit(solution)/shard_map/ppermute | solution.py:426
  16.1 12.3 %collective-permute-start.1 = (bf16[3,64,704]{2,1,0:T(8,128)(2,1)}, bf16[3,64,704]{2,1,0:T(8,128)(2,1)}, u32[]{:S(2)}, u32[]{:S(2)}) collective-permute-start(bf16[3,64,704]{2,1,0:T(8,128)(2,1)} %get-tuple-element.42), channel_id=1, source_target_pairs={{1,0},{2,1},{3,2},{4,3},{5,4},{6,5},{7,6},{8,7},{9,8},{10,9},{11,1... | collective-permute-start | bytes 811016 | tf_op jit(solution)/shard_map/ppermute | solution.py:427
  21.4 1.8 %copy-start.4 = (bf16[1408,256]{1,0:T(8,128)(2,1)S(1)}, bf16[1408,256]{1,0:T(8,128)(2,1)}, u32[]{:S(2)}) copy-start(bf16[1408,256]{1,0:T(8,128)(2,1)} %get-tuple-element.50.patches) | copy-start | bytes 2162692
  21.4 6.9 %copy-start.1 = (bf16[4,64,704]{2,1,0:T(8,128)(2,1)S(1)}, bf16[4,64,704]{2,1,0:T(8,128)(2,1)}, u32[]{:S(2)}) copy-start(bf16[4,64,704]{2,1,0:T(8,128)(2,1)} %get-tuple-element.43.down) | copy-start | bytes 1081348
  25.6 19.8 %collective-permute-start.4 = (bf16[4,88,704]{2,1,0:T(8,128)(2,1)}, bf16[4,88,704]{2,1,0:T(8,128)(2,1)S(1)}, u32[]{:S(2)}, u32[]{:S(2)}) collective-permute-start(bf16[4,88,704]{2,1,0:T(8,128)(2,1)} %get-tuple-element.57), channel_id=1, source_target_pairs={{0,1},{1,2},{2,3},{3,0},{4,5},{5,6},{6,7},{7,4},{8,9},{9,10},{10,1... | collective-permute-start | bytes 1486856 | tf_op jit(solution)/shard_map/ppermute | solution.py:371
  27.8 17.5 %collective-permute-start.5 = (bf16[4,88,704]{2,1,0:T(8,128)(2,1)}, bf16[4,88,704]{2,1,0:T(8,128)(2,1)S(1)}, u32[]{:S(2)}, u32[]{:S(2)}) collective-permute-start(bf16[4,88,704]{2,1,0:T(8,128)(2,1)} %get-tuple-element.58), channel_id=1, source_target_pairs={{0,2},{1,3},{2,0},{3,1},{4,6},{5,7},{6,4},{7,5},{8,10},{9,11},{10,... | collective-permute-start | bytes 1486856 | tf_op jit(solution)/shard_map/ppermute | solution.py:371
  27.8 26.8 %collective-permute-start.6 = (bf16[4,88,704]{2,1,0:T(8,128)(2,1)}, bf16[4,88,704]{2,1,0:T(8,128)(2,1)S(1)}, u32[]{:S(2)}, u32[]{:S(2)}) collective-permute-start(bf16[4,88,704]{2,1,0:T(8,128)(2,1)} %get-tuple-element.59), channel_id=1, source_target_pairs={{0,3},{1,0},{2,1},{3,2},{4,7},{5,4},{6,5},{7,6},{8,11},{9,8},{10,9... | collective-permute-start | bytes 1486856 | tf_op jit(solution)/shard_map/ppermute | solution.py:371
  28.4 3.2 %copy-start = (bf16[1408,704]{0,1:T(8,128)(2,1)S(1)}, bf16[1408,704]{0,1:T(8,128)(2,1)}, u32[]{:S(2)}) copy-start(bf16[1408,704]{0,1:T(8,128)(2,1)} %param.11) | copy-start | bytes 5947396
  28.4 3.2 %copy-start.5 = (bf16[1408,256]{1,0:T(8,128)(2,1)S(1)}, bf16[1408,256]{1,0:T(8,128)(2,1)}, u32[]{:S(2)}) copy-start(bf16[1408,256]{1,0:T(8,128)(2,1)} %get-tuple-element.62.normed) | copy-start | bytes 2162692
  28.4 3.2 %copy-start.7 = (f32[8,256]{1,0:T(8,128)S(1)}, f32[8,256]{1,0:T(8,128)}, u32[]{:S(2)}) copy-start(f32[8,256]{1,0:T(8,128)} %get-tuple-element.46.rstd) | copy-start | bytes 24580
  28.4 3.1 %copy-start.8 = (f32[352]{0:T(512)S(1)}, f32[352]{0:T(512)}, u32[]{:S(2)}) copy-start(f32[352]{0:T(512)} %gain.1) | copy-start | bytes 4228
  33.9 25.3 %copy-start.9 = (f32[704]{0:T(1024)S(1)}, f32[704]{0:T(1024)}, u32[]{:S(2)}) copy-start(f32[704]{0:T(1024)} %bias.1) | copy-start | bytes 8452
  33.9 4.5 %collective-permute-start.10 = (bf16[56,704]{1,0:T(8,128)(2,1)S(1)}, bf16[56,704]{1,0:T(8,128)(2,1)S(1)}, u32[]{:S(2)}, u32[]{:S(2)}) collective-permute-start(bf16[56,704]{1,0:T(8,128)(2,1)S(1)} %get-tuple-element.67), channel_id=1, source_target_pairs={{0,8},{1,9},{2,10},{3,11},{4,12},{5,13},{6,14},{7,15},{8,0},{9,1},... | collective-permute-start | bytes 236552 | tf_op jit(solution)/shard_map/ppermute | solution.py:371
  33.9 5.0 %collective-permute-start.11 = (bf16[56,704]{1,0:T(8,128)(2,1)S(1)}, bf16[56,704]{1,0:T(8,128)(2,1)S(1)}, u32[]{:S(2)}, u32[]{:S(2)}) collective-permute-start(bf16[56,704]{1,0:T(8,128)(2,1)S(1)} %get-tuple-element.67), channel_id=1, source_target_pairs={{0,4},{1,5},{2,6},{3,7},{4,0},{5,1},{6,2},{7,3},{8,12},{9,13},{10,... | collective-permute-start | bytes 236552 | tf_op jit(solution)/shard_map/ppermute | solution.py:371
  38.4 4.7 %collective-permute-start.12 = (bf16[56,704]{1,0:T(8,128)(2,1)S(1)}, bf16[56,704]{1,0:T(8,128)(2,1)S(1)}, u32[]{:S(2)}, u32[]{:S(2)}) collective-permute-start(bf16[56,704]{1,0:T(8,128)(2,1)S(1)} %get-tuple-element.67), channel_id=1, source_target_pairs={{0,12},{1,13},{2,14},{3,15},{4,8},{5,9},{6,10},{7,11},{8,4},{9,5},... | collective-permute-start | bytes 236552 | tf_op jit(solution)/shard_map/ppermute | solution.py:371
  43.1 16.1 %collective-permute-start.13 = (bf16[56,704]{1,0:T(8,128)(2,1)S(1)}, bf16[56,704]{1,0:T(8,128)(2,1)}, u32[]{:S(2)}, u32[]{:S(2)}) collective-permute-start(bf16[56,704]{1,0:T(8,128)(2,1)S(1)} %add_convert_fusion.t0), channel_id=1, source_target_pairs={{0,1},{1,2},{2,3},{3,0},{4,5},{5,6},{6,7},{7,4},{8,9},{9,10},{10,1... | collective-permute-start | bytes 236552 | tf_op jit(solution)/shard_map/ppermute | solution.py:371
  45.3 13.9 %copy-start.2 = (bf16[4,64,704]{2,1,0:T(8,128)(2,1)S(1)}, bf16[4,64,704]{2,1,0:T(8,128)(2,1)}, u32[]{:S(2)}) copy-start(bf16[4,64,704]{2,1,0:T(8,128)(2,1)} %get-tuple-element.43.down) | copy-start | bytes 1081348
  54.8 9.4 %collective-permute-start.7 = (bf16[88,704]{1,0:T(8,128)(2,1)S(1)}, bf16[88,704]{1,0:T(8,128)(2,1)S(1)}, u32[]{:S(2)}, u32[]{:S(2)}) collective-permute-start(bf16[88,704]{1,0:T(8,128)(2,1)S(1)} %get-tuple-element.65), channel_id=1, source_target_pairs={{0,8},{1,9},{2,10},{3,11},{4,12},{5,13},{6,14},{7,15},{8,0},{9,1},... | collective-permute-start | bytes 371720 | tf_op jit(solution)/shard_map/ppermute | solution.py:371
  54.9 15.1 %collective-permute-start.8 = (bf16[88,704]{1,0:T(8,128)(2,1)S(1)}, bf16[88,704]{1,0:T(8,128)(2,1)S(1)}, u32[]{:S(2)}, u32[]{:S(2)}) collective-permute-start(bf16[88,704]{1,0:T(8,128)(2,1)S(1)} %get-tuple-element.66), channel_id=1, source_target_pairs={{0,12},{1,13},{2,14},{3,15},{4,8},{5,9},{6,10},{7,11},{8,4},{9,5},... | collective-permute-start | bytes 371720 | tf_op jit(solution)/shard_map/ppermute | solution.py:371
  57.7 12.3 %collective-permute-start.9 = (bf16[88,704]{1,0:T(8,128)(2,1)S(1)}, bf16[88,704]{1,0:T(8,128)(2,1)S(1)}, u32[]{:S(2)}, u32[]{:S(2)}) collective-permute-start(bf16[88,704]{1,0:T(8,128)(2,1)S(1)} %get-tuple-element.60), channel_id=1, source_target_pairs={{0,4},{1,5},{2,6},{3,7},{4,0},{5,1},{6,2},{7,3},{8,12},{9,13},{10,... | collective-permute-start | bytes 371720 | tf_op jit(solution)/shard_map/ppermute | solution.py:371
  58.5 5.6 %collective-permute-start.14 = (bf16[56,704]{1,0:T(8,128)(2,1)S(1)}, bf16[56,704]{1,0:T(8,128)(2,1)S(1)}, u32[]{:S(2)}, u32[]{:S(2)}) collective-permute-start(bf16[56,704]{1,0:T(8,128)(2,1)S(1)} %add_convert_fusion.t0), channel_id=1, source_target_pairs={{0,2},{1,3},{2,0},{3,1},{4,6},{5,7},{6,4},{7,5},{8,10},{9,11},{10,... | collective-permute-start | bytes 236552 | tf_op jit(solution)/shard_map/ppermute | solution.py:371
  59.2 5.0 %collective-permute-start.15 = (bf16[56,704]{1,0:T(8,128)(2,1)S(1)}, bf16[56,704]{1,0:T(8,128)(2,1)S(1)}, u32[]{:S(2)}, u32[]{:S(2)}) collective-permute-start(bf16[56,704]{1,0:T(8,128)(2,1)S(1)} %add_convert_fusion.t0), channel_id=1, source_target_pairs={{0,3},{1,0},{2,1},{3,2},{4,7},{5,4},{6,5},{7,6},{8,11},{9,8},{10,9... | collective-permute-start | bytes 236552 | tf_op jit(solution)/shard_map/ppermute | solution.py:371

commit v8 on v7

--- a/solution.py
+++ b/solution.py
@@ -338,14 +338,14 @@
     small[...] = sums[...].astype(BF16)
 
 
-def middle_kernel(place, c0, c1, c2, c3, *outs):
+def middle_kernel(place, c0, c2, c1, c3, *outs):
     for k in (1, 2, 3):
         to = jnp.bitwise_xor(place[0], k)
         outs[k - 1][...] = sum_four(c0[to], c1[to], c2[to], c3[to]).astype(BF16)
 
 
 def last_kernel(
-    place, c0, c1, c2, c3, w2, w3, w1, t0, t1, t2, t3,
+    place, c0, c2, c1, c3, w2, w3, w1, t0, t1, t2, t3,
     weight, gain, bias, kernel, depth_bias,
 ):
     z = place[0]
@@ -463,7 +463,7 @@
         [pltpu.VMEM((in_chans, chans), F32)],
         "product",
     )(place_y, patches, pre)
-    got = send(chunks[1:], along_y)
+    got = send([chunks[k] for k in (2, 1, 3)], [along_y[k - 1] for k in (2, 1, 3)])
     down, down_before, down_after = lax.optimization_barrier((down, down_before, down_after))
 
     grads = call(

time: 72.1 us -> 72.1 us (level)
  the two profiles are of different devices: /device:TPU:95 before, /device:TPU:2 now
where the time goes in v8:
time: 72.1 us; the launch traced here: 70.8 us
  starting transfers between devices  39.9 us (55%)
  Pallas kernels  24.5 us (34%)
  waiting for transfers between devices  5.52 us (8%)
  between operations  0.87 us (1%)
    ppermute x12, starting transfers between devices, send(): lax.ppermute(value, 'rows', pair)  28.5 us
    ppermute x12, waiting for transfers between devices, send(): lax.ppermute(value, 'rows', pair)  5.51 us
    ppermute x1, starting transfers between devices, body(): down_before = lax.ppermute(down_last, 'rows', up)  5.28 us
    pallas_call x1, Pallas kernels, body(): call(front_kernel, sd((height, width, chans), BF16), [VM] * 6, [pltpu.VME...  4.85 us
    pallas_call x1, Pallas kernels, body(): call(reduce_kernel, (halo, halo, sd((4 * in_chans, pixels), BF16), sd((4...  4.78 us
    ppermute x1, starting transfers between devices, body(): cot_before = lax.ppermute(cot_last, 'rows', up)  3.5 us
    pallas_call x1, Pallas kernels, body(): call(own_kernel, (sd((tiles, height, span, LANES), F32), sd((tiles, KS *...  3.33 us
    pallas_call x1, Pallas kernels, body(): call(grad_kernel, sd((56, chans), F32), [VM] * 3, [pltpu.VMEM((tiles, hei...  3.1 us
  transfers between devices with their start and end apart: 16, of which 4 were waited for; matrix products, arithmetic and copies ran while one was open for 0% of the time, Pallas kernels for 25%

profile of v8, /device:TPU:2, one launch (start us, length us, event | category | flops | bytes accessed | tf_op | source)
XLA Modules:
  0.0 70.8 jit_solution(8917794007328716701)
XLA Ops:
  0.7 4.8 %reduce.1 = (bf16[3,64,704]{2,1,0:T(8,128)(2,1)}, bf16[3,64,704]{2,1,0:T(8,128)(2,1)}, bf16[1408,256]{1,0:T(8,128)(2,1)}, bf16[1408,256]{1,0:T(8,128)(2,1)}, f32...) custom-call(s32[1,16]{1,0:T(1,128)} %vis_in.2, ...), custom_call_target="tpu_custom_call" | custom-call | flops 1000000 | bytes 20000000 | tf_op jit(solution)/shard_map/reduce/pallas_call | solution.py:396
  5.5 3.5 %collective-permute-start.2 = (bf16[3,64,704]{2,1,0:T(8,128)(2,1)}, bf16[3,64,704]{2,1,0:T(8,128)(2,1)S(1)}, u32[]{:S(2)}, u32[]{:S(2)}) collective-permute-start(bf16[3,64,704]{2,1,0:T(8,128)(2,1)} %get-tuple-element.51), channel_id=1, source_target_pairs={{0,1},{1,2},{2,3},{3,4},{4,5},{5,6},{6,7},{7,8},{8,9},{9,10},{10,1... | collective-permute-start | bytes 811016 | tf_op jit(solution)/shard_map/ppermute | solution.py:424
  9.0 1.3 %collective-permute-start.3 = (bf16[3,64,704]{2,1,0:T(8,128)(2,1)}, bf16[3,64,704]{2,1,0:T(8,128)(2,1)S(1)}, u32[]{:S(2)}, u32[]{:S(2)}) collective-permute-start(bf16[3,64,704]{2,1,0:T(8,128)(2,1)} %get-tuple-element.52), channel_id=1, source_target_pairs={{1,0},{2,1},{3,2},{4,3},{5,4},{6,5},{7,6},{8,7},{9,8},{10,9},{11,1... | collective-permute-start | bytes 811016 | tf_op jit(solution)/shard_map/ppermute | solution.py:425
  10.3 5.3 %collective-permute-start = (bf16[3,64,704]{2,1,0:T(8,128)(2,1)}, bf16[3,64,704]{2,1,0:T(8,128)(2,1)}, u32[]{:S(2)}, u32[]{:S(2)}) collective-permute-start(bf16[3,64,704]{2,1,0:T(8,128)(2,1)} %get-tuple-element.41), channel_id=1, source_target_pairs={{0,1},{1,2},{2,3},{3,4},{4,5},{5,6},{6,7},{7,8},{8,9},{9,10},{10,1... | collective-permute-start | bytes 811016 | tf_op jit(solution)/shard_map/ppermute | solution.py:426
  15.5 1.3 %collective-permute-start.1 = (bf16[3,64,704]{2,1,0:T(8,128)(2,1)}, bf16[3,64,704]{2,1,0:T(8,128)(2,1)}, u32[]{:S(2)}, u32[]{:S(2)}) collective-permute-start(bf16[3,64,704]{2,1,0:T(8,128)(2,1)} %get-tuple-element.42), channel_id=1, source_target_pairs={{1,0},{2,1},{3,2},{4,3},{5,4},{6,5},{7,6},{8,7},{9,8},{10,9},{11,1... | collective-permute-start | bytes 811016 | tf_op jit(solution)/shard_map/ppermute | solution.py:427
  16.9 3.3 %own.1 = (f32[6,4,80,128]{3,2,1,0:T(8,128)S(1)}, f32[6,49,8,128]{3,2,1,0:T(8,128)S(1)}, f32[6,4,64,128]{3,2,1,0:T(8,128)S(1)}, f32[64,128]{1,0:T(8,128)S(1)}) custom-call(s32[1,16]{1,0:T(1,128)S(1)} %copy-done.10, bf16[4,64,704]{2,1,0:T(8,128)(2,1)S(1)} %copy-done.3, f32[49,704]{1,0:T(8,128)S(1)} %copy-done.6), custom_call_target="tpu_custom_call" | custom-call | flops 1000000 | bytes 50000000 | tf_op jit(solution)/shard_map/own/pallas_call | solution.py:430
  20.2 0.0 copy-start.4
  20.2 0.0 copy-start.1
  20.3 1.7 %back.1 = (bf16[256,704]{1,0:T(8,128)(2,1)S(1)}, f32[6,6,80,128]{3,2,1,0:T(8,128)S(1)}) custom-call(bf16[3,64,704]{2,1,0:T(8,128)(2,1)S(1)} %collective-permute-done.2.before, bf16[3,64,704]{2,1,0:T(8,128)(2,1)S(1)} %collective-permute-done.3.after, f32[6,4,80,128]{3,2,1,0:T(8,128)S(1)} %get-tuple-element.53.band.cots, ...), custom_call_target="tpu_custom_call" | custom-call | flops 1000000 | bytes 1000000000 | tf_op jit(solution)/shard_map/back/pallas_call | solution.py:450
  22.0 2.4 %product.1 = (bf16[4,88,704]{2,1,0:T(8,128)(2,1)S(1)}, bf16[4,88,704]{2,1,0:T(8,128)(2,1)}, bf16[4,88,704]{2,1,0:T(8,128)(2,1)}, bf16[4,88,704]{2,1,0:T(8,128)(2,1)}) custom-call(s32[1]{0:T(128)} %bitcast.3.place, bf16[1408,256]{1,0:T(8,128)(2,1)S(1)} %copy-done.4, bf16[256,704]{1,0:T(8,128)(2,1)S(1)} %get-tuple-element.55.pre), custom_call_target="tpu_custom_call" | custom-call | flops 1000000 | bytes 100000 | tf_op jit(solution)/shard_map/product/pallas_call | solution.py:459
  24.4 3.5 %collective-permute-start.4 = (bf16[4,88,704]{2,1,0:T(8,128)(2,1)}, bf16[4,88,704]{2,1,0:T(8,128)(2,1)S(1)}, u32[]{:S(2)}, u32[]{:S(2)}) collective-permute-start(bf16[4,88,704]{2,1,0:T(8,128)(2,1)} %get-tuple-element.57), channel_id=1, source_target_pairs={{0,2},{1,3},{2,0},{3,1},{4,6},{5,7},{6,4},{7,5},{8,10},{9,11},{10,... | collective-permute-start | bytes 1486856 | tf_op jit(solution)/shard_map/ppermute | solution.py:371
  27.9 2.3 %collective-permute-start.5 = (bf16[4,88,704]{2,1,0:T(8,128)(2,1)}, bf16[4,88,704]{2,1,0:T(8,128)(2,1)S(1)}, u32[]{:S(2)}, u32[]{:S(2)}) collective-permute-start(bf16[4,88,704]{2,1,0:T(8,128)(2,1)} %get-tuple-element.58), channel_id=1, source_target_pairs={{0,1},{1,2},{2,3},{3,0},{4,5},{5,6},{6,7},{7,4},{8,9},{9,10},{10,1... | collective-permute-start | bytes 1486856 | tf_op jit(solution)/shard_map/ppermute | solution.py:371
  30.3 0.9 %collective-permute-start.6 = (bf16[4,88,704]{2,1,0:T(8,128)(2,1)}, bf16[4,88,704]{2,1,0:T(8,128)(2,1)S(1)}, u32[]{:S(2)}, u32[]{:S(2)}) collective-permute-start(bf16[4,88,704]{2,1,0:T(8,128)(2,1)} %get-tuple-element.59), channel_id=1, source_target_pairs={{0,3},{1,0},{2,1},{3,2},{4,7},{5,4},{6,5},{7,6},{8,11},{9,8},{10,9... | collective-permute-start | bytes 1486856 | tf_op jit(solution)/shard_map/ppermute | solution.py:371
  31.2 3.1 %grads.1 = f32[56,704]{1,0:T(8,128)S(1)} custom-call(bf16[4,64,704]{2,1,0:T(8,128)(2,1)S(1)} %copy-done.1, f32[6,4,80,128]{3,2,1,0:T(8,128)S(1)} %get-tuple-element.53.band.cots, f32[6,6,80,128]{3,2,1,0:T(8,128)S(1)} %get-tuple-element.63.halo), custom_call_target="tpu_custom_call" | custom-call | flops 1000000 | bytes 100000 | tf_op jit(solution)/shard_map/grads/pallas_call | solution.py:469
  34.4 2.3 %image.1 = (bf16[8,352,128]{2,1,0:T(8,128)(2,1)}, bf16[56,704]{1,0:T(8,128)(2,1)S(1)}) custom-call(bf16[256,704]{1,0:T(8,128)(2,1)S(1)} %get-tuple-element.55.pre, bf16[704,1408]{1,0:T(8,128)(2,1)S(1)} %bitcast.6, bf16[1408,256]{1,0:T(8,128)(2,1)S(1)} %copy-done.5, f32[8,256]{1,0:T(8,128)S(1)} %copy-done.7, f32[352]{0:T(512)S(1)} %copy-done.8, ...), custom_call_target="tpu_custom_call" | custom-call | flops 1000000 | bytes 100000 | tf_op jit(solution)/shard_map/image/pallas_call | solution.py:479
  36.7 4.3 %collective-permute-start.10 = (bf16[56,704]{1,0:T(8,128)(2,1)S(1)}, bf16[56,704]{1,0:T(8,128)(2,1)S(1)}, u32[]{:S(2)}, u32[]{:S(2)}) collective-permute-start(bf16[56,704]{1,0:T(8,128)(2,1)S(1)} %get-tuple-element.67), channel_id=1, source_target_pairs={{0,8},{1,9},{2,10},{3,11},{4,12},{5,13},{6,14},{7,15},{8,0},{9,1},... | collective-permute-start | bytes 236552 | tf_op jit(solution)/shard_map/ppermute | solution.py:371
  41.0 1.9 %collective-permute-start.11 = (bf16[56,704]{1,0:T(8,128)(2,1)S(1)}, bf16[56,704]{1,0:T(8,128)(2,1)S(1)}, u32[]{:S(2)}, u32[]{:S(2)}) collective-permute-start(bf16[56,704]{1,0:T(8,128)(2,1)S(1)} %get-tuple-element.67), channel_id=1, source_target_pairs={{0,4},{1,5},{2,6},{3,7},{4,0},{5,1},{6,2},{7,3},{8,12},{9,13},{10,... | collective-permute-start | bytes 236552 | tf_op jit(solution)/shard_map/ppermute | solution.py:371
  42.9 0.6 collective-permute-done.10
  43.5 5.6 %collective-permute-start.12 = (bf16[56,704]{1,0:T(8,128)(2,1)S(1)}, bf16[56,704]{1,0:T(8,128)(2,1)S(1)}, u32[]{:S(2)}, u32[]{:S(2)}) collective-permute-start(bf16[56,704]{1,0:T(8,128)(2,1)S(1)} %get-tuple-element.67), channel_id=1, source_target_pairs={{0,12},{1,13},{2,14},{3,15},{4,8},{5,9},{6,10},{7,11},{8,4},{9,5},... | collective-permute-start | bytes 236552 | tf_op jit(solution)/shard_map/ppermute | solution.py:371
  49.1 2.5 %collective-permute-done.12 = bf16[56,704]{1,0:T(8,128)(2,1)S(1)} collective-permute-done((bf16[56,704]{1,0:T(8,128)(2,1)S(1)}, bf16[56,704]{1,0:T(8,128)(2,1)S(1)}, u32[]{:S(2)}, u32[]{:S(2)}) %collective-permute-start.12) | collective-permute-done | bytes 78880 | tf_op jit(solution)/shard_map/ppermute | solution.py:371
  51.6 0.3 collective-permute-start.13
  52.0 1.3 %collective-permute-done.6.c3 = bf16[4,88,704]{2,1,0:T(8,128)(2,1)S(1)} collective-permute-done((bf16[4,88,704]{2,1,0:T(8,128)(2,1)}, bf16[4,88,704]{2,1,0:T(8,128)(2,1)S(1)}, u32[]{:S(2)}, u32[]{:S(2)}) %collective-permute-start.6) | collective-permute-done | bytes 495648 | tf_op jit(solution)/shard_map/ppermute | solution.py:371
  53.3 0.2 middle.1
  53.5 5.4 %collective-permute-start.7 = (bf16[88,704]{1,0:T(8,128)(2,1)S(1)}, bf16[88,704]{1,0:T(8,128)(2,1)S(1)}, u32[]{:S(2)}, u32[]{:S(2)}) collective-permute-start(bf16[88,704]{1,0:T(8,128)(2,1)S(1)} %get-tuple-element.65), channel_id=1, source_target_pairs={{0,8},{1,9},{2,10},{3,11},{4,12},{5,13},{6,14},{7,15},{8,0},{9,1},... | collective-permute-start | bytes 371720 | tf_op jit(solution)/shard_map/ppermute | solution.py:371
  58.9 1.5 %collective-permute-start.8 = (bf16[88,704]{1,0:T(8,128)(2,1)S(1)}, bf16[88,704]{1,0:T(8,128)(2,1)S(1)}, u32[]{:S(2)}, u32[]{:S(2)}) collective-permute-start(bf16[88,704]{1,0:T(8,128)(2,1)S(1)} %get-tuple-element.66), channel_id=1, source_target_pairs={{0,12},{1,13},{2,14},{3,15},{4,8},{5,9},{6,10},{7,11},{8,4},{9,5},... | collective-permute-start | bytes 371720 | tf_op jit(solution)/shard_map/ppermute | solution.py:371
  60.3 0.5 collective-permute-start.9
  60.8 0.5 collective-permute-start.14
  61.2 1.8 %collective-permute-start.15 = (bf16[56,704]{1,0:T(8,128)(2,1)S(1)}, bf16[56,704]{1,0:T(8,128)(2,1)S(1)}, u32[]{:S(2)}, u32[]{:S(2)}) collective-permute-start(bf16[56,704]{1,0:T(8,128)(2,1)S(1)} %add_convert_fusion.t0), channel_id=1, source_target_pairs={{0,3},{1,0},{2,1},{3,2},{4,7},{5,4},{6,5},{7,6},{8,11},{9,8},{10,9... | collective-permute-start | bytes 236552 | tf_op jit(solution)/shard_map/ppermute | solution.py:371
  63.1 4.8 %front.1 = bf16[4,64,704]{2,1,0:T(8,128)(2,1)} custom-call(bf16[4,64,704]{2,1,0:T(8,128)(2,1)S(1)} %copy-done.2, bf16[3,64,704]{2,1,0:T(8,128)(2,1)} %collective-permute-done.before, bf16[3,64,704]{2,1,0:T(8,128)(2,1)} %collective-permute-done.1.after, f32[6,49,8,128]{3,2,1,0:T(8,128)S(1)} %get-tuple-element.48.taps, f32[704]{0:T(1024)S(1)} %copy-done.9, ...), custom_call_target="tpu_custom_call" | custom-call | flops 1000000 | bytes 10000000 | tf_op jit(solution)/shard_map/front/pallas_call | solution.py:499
  67.9 1.2 %collective-permute-done.7.w2 = bf16[88,704]{1,0:T(8,128)(2,1)S(1)} collective-permute-done((bf16[88,704]{1,0:T(8,128)(2,1)S(1)}, bf16[88,704]{1,0:T(8,128)(2,1)S(1)}, u32[]{:S(2)}, u32[]{:S(2)}) %collective-permute-start.7) | collective-permute-done | bytes 123936 | tf_op jit(solution)/shard_map/ppermute | solution.py:371
  69.1 0.0 collective-permute-done.9.w1
  69.1 1.8 %last.1 = (f32[88,704]{1,0:T(8,128)}, f32[352]{0:T(512)}, f32[704]{0:T(1024)}, f32[49,704]{1,0:T(8,128)}, f32[704]{0:T(1024)}) custom-call(s32[1]{0:T(128)} %bitcast.2.place, bf16[4,88,704]{2,1,0:T(8,128)(2,1)S(1)} %get-tuple-element.56.c0, bf16[4,88,704]{2,1,0:T(8,128)(2,1)S(1)} %collective-permute-done.4.c2, ...), custom_call_target="tpu_custom_call" | custom-call | flops 1000000 | bytes 100000 | tf_op jit(solution)/shard_map/last/pallas_call | solution.py:513
  (32 shorter events, 0.1 us)
Async XLA Ops:
  0.6 16.2 %copy-start.3 = (bf16[4,64,704]{2,1,0:T(8,128)(2,1)S(1)}, bf16[4,64,704]{2,1,0:T(8,128)(2,1)}, u32[]{:S(2)}) copy-start(bf16[4,64,704]{2,1,0:T(8,128)(2,1)} %cot_in.3) | copy-start | bytes 1081348
  0.6 16.2 %copy-start.6 = (f32[49,704]{1,0:T(8,128)S(1)}, f32[49,704]{1,0:T(8,128)}, u32[]{:S(2)}) copy-start(f32[49,704]{1,0:T(8,128)} %kernel_in.1) | copy-start | bytes 413956
  0.7 16.2 %copy-start.10 = (s32[1,16]{1,0:T(1,128)S(1)}, s32[1,16]{1,0:T(1,128)}, u32[]{:S(2)}) copy-start(s32[1,16]{1,0:T(1,128)} %vis_in.2) | copy-start | bytes 196
  5.5 14.8 %collective-permute-start.2 = (bf16[3,64,704]{2,1,0:T(8,128)(2,1)}, bf16[3,64,704]{2,1,0:T(8,128)(2,1)S(1)}, u32[]{:S(2)}, u32[]{:S(2)}) collective-permute-start(bf16[3,64,704]{2,1,0:T(8,128)(2,1)} %get-tuple-element.51), channel_id=1, source_target_pairs={{0,1},{1,2},{2,3},{3,4},{4,5},{5,6},{6,7},{7,8},{8,9},{9,10},{10,1... | collective-permute-start | bytes 811016 | tf_op jit(solution)/shard_map/ppermute | solution.py:424
  9.0 11.3 %collective-permute-start.3 = (bf16[3,64,704]{2,1,0:T(8,128)(2,1)}, bf16[3,64,704]{2,1,0:T(8,128)(2,1)S(1)}, u32[]{:S(2)}, u32[]{:S(2)}) collective-permute-start(bf16[3,64,704]{2,1,0:T(8,128)(2,1)} %get-tuple-element.52), channel_id=1, source_target_pairs={{1,0},{2,1},{3,2},{4,3},{5,4},{6,5},{7,6},{8,7},{9,8},{10,9},{11,1... | collective-permute-start | bytes 811016 | tf_op jit(solution)/shard_map/ppermute | solution.py:425
  10.3 20.9 %collective-permute-start = (bf16[3,64,704]{2,1,0:T(8,128)(2,1)}, bf16[3,64,704]{2,1,0:T(8,128)(2,1)}, u32[]{:S(2)}, u32[]{:S(2)}) collective-permute-start(bf16[3,64,704]{2,1,0:T(8,128)(2,1)} %get-tuple-element.41), channel_id=1, source_target_pairs={{0,1},{1,2},{2,3},{3,4},{4,5},{5,6},{6,7},{7,8},{8,9},{9,10},{10,1... | collective-permute-start | bytes 811016 | tf_op jit(solution)/shard_map/ppermute | solution.py:426
  15.5 15.6 %collective-permute-start.1 = (bf16[3,64,704]{2,1,0:T(8,128)(2,1)}, bf16[3,64,704]{2,1,0:T(8,128)(2,1)}, u32[]{:S(2)}, u32[]{:S(2)}) collective-permute-start(bf16[3,64,704]{2,1,0:T(8,128)(2,1)} %get-tuple-element.42), channel_id=1, source_target_pairs={{1,0},{2,1},{3,2},{4,3},{5,4},{6,5},{7,6},{8,7},{9,8},{10,9},{11,1... | collective-permute-start | bytes 811016 | tf_op jit(solution)/shard_map/ppermute | solution.py:427
  20.2 1.8 %copy-start.4 = (bf16[1408,256]{1,0:T(8,128)(2,1)S(1)}, bf16[1408,256]{1,0:T(8,128)(2,1)}, u32[]{:S(2)}) copy-start(bf16[1408,256]{1,0:T(8,128)(2,1)} %get-tuple-element.50.patches) | copy-start | bytes 2162692
  20.2 10.9 %copy-start.1 = (bf16[4,64,704]{2,1,0:T(8,128)(2,1)S(1)}, bf16[4,64,704]{2,1,0:T(8,128)(2,1)}, u32[]{:S(2)}) copy-start(bf16[4,64,704]{2,1,0:T(8,128)(2,1)} %get-tuple-element.43.down) | copy-start | bytes 1081348
  24.4 27.6 %collective-permute-start.4 = (bf16[4,88,704]{2,1,0:T(8,128)(2,1)}, bf16[4,88,704]{2,1,0:T(8,128)(2,1)S(1)}, u32[]{:S(2)}, u32[]{:S(2)}) collective-permute-start(bf16[4,88,704]{2,1,0:T(8,128)(2,1)} %get-tuple-element.57), channel_id=1, source_target_pairs={{0,2},{1,3},{2,0},{3,1},{4,6},{5,7},{6,4},{7,5},{8,10},{9,11},{10,... | collective-permute-start | bytes 1486856 | tf_op jit(solution)/shard_map/ppermute | solution.py:371
  27.9 24.0 %collective-permute-start.5 = (bf16[4,88,704]{2,1,0:T(8,128)(2,1)}, bf16[4,88,704]{2,1,0:T(8,128)(2,1)S(1)}, u32[]{:S(2)}, u32[]{:S(2)}) collective-permute-start(bf16[4,88,704]{2,1,0:T(8,128)(2,1)} %get-tuple-element.58), channel_id=1, source_target_pairs={{0,1},{1,2},{2,3},{3,0},{4,5},{5,6},{6,7},{7,4},{8,9},{9,10},{10,1... | collective-permute-start | bytes 1486856 | tf_op jit(solution)/shard_map/ppermute | solution.py:371
  30.3 23.0 %collective-permute-start.6 = (bf16[4,88,704]{2,1,0:T(8,128)(2,1)}, bf16[4,88,704]{2,1,0:T(8,128)(2,1)S(1)}, u32[]{:S(2)}, u32[]{:S(2)}) collective-permute-start(bf16[4,88,704]{2,1,0:T(8,128)(2,1)} %get-tuple-element.59), channel_id=1, source_target_pairs={{0,3},{1,0},{2,1},{3,2},{4,7},{5,4},{6,5},{7,6},{8,11},{9,8},{10,9... | collective-permute-start | bytes 1486856 | tf_op jit(solution)/shard_map/ppermute | solution.py:371
  31.2 3.2 %copy-start = (bf16[1408,704]{0,1:T(8,128)(2,1)S(1)}, bf16[1408,704]{0,1:T(8,128)(2,1)}, u32[]{:S(2)}) copy-start(bf16[1408,704]{0,1:T(8,128)(2,1)} %param.11) | copy-start | bytes 5947396
  31.2 3.2 %copy-start.5 = (bf16[1408,256]{1,0:T(8,128)(2,1)S(1)}, bf16[1408,256]{1,0:T(8,128)(2,1)}, u32[]{:S(2)}) copy-start(bf16[1408,256]{1,0:T(8,128)(2,1)} %get-tuple-element.62.normed) | copy-start | bytes 2162692
  31.2 3.2 %copy-start.7 = (f32[8,256]{1,0:T(8,128)S(1)}, f32[8,256]{1,0:T(8,128)}, u32[]{:S(2)}) copy-start(f32[8,256]{1,0:T(8,128)} %get-tuple-element.46.rstd) | copy-start | bytes 24580
  31.2 3.1 %copy-start.8 = (f32[352]{0:T(512)S(1)}, f32[352]{0:T(512)}, u32[]{:S(2)}) copy-start(f32[352]{0:T(512)} %gain.1) | copy-start | bytes 4228
  36.7 26.3 %copy-start.9 = (f32[704]{0:T(1024)S(1)}, f32[704]{0:T(1024)}, u32[]{:S(2)}) copy-start(f32[704]{0:T(1024)} %bias.1) | copy-start | bytes 8452
  36.7 6.8 %collective-permute-start.10 = (bf16[56,704]{1,0:T(8,128)(2,1)S(1)}, bf16[56,704]{1,0:T(8,128)(2,1)S(1)}, u32[]{:S(2)}, u32[]{:S(2)}) collective-permute-start(bf16[56,704]{1,0:T(8,128)(2,1)S(1)} %get-tuple-element.67), channel_id=1, source_target_pairs={{0,8},{1,9},{2,10},{3,11},{4,12},{5,13},{6,14},{7,15},{8,0},{9,1},... | collective-permute-start | bytes 236552 | tf_op jit(solution)/shard_map/ppermute | solution.py:371
  41.0 8.1 %collective-permute-start.11 = (bf16[56,704]{1,0:T(8,128)(2,1)S(1)}, bf16[56,704]{1,0:T(8,128)(2,1)S(1)}, u32[]{:S(2)}, u32[]{:S(2)}) collective-permute-start(bf16[56,704]{1,0:T(8,128)(2,1)S(1)} %get-tuple-element.67), channel_id=1, source_target_pairs={{0,4},{1,5},{2,6},{3,7},{4,0},{5,1},{6,2},{7,3},{8,12},{9,13},{10,... | collective-permute-start | bytes 236552 | tf_op jit(solution)/shard_map/ppermute | solution.py:371
  43.5 8.1 %collective-permute-start.12 = (bf16[56,704]{1,0:T(8,128)(2,1)S(1)}, bf16[56,704]{1,0:T(8,128)(2,1)S(1)}, u32[]{:S(2)}, u32[]{:S(2)}) collective-permute-start(bf16[56,704]{1,0:T(8,128)(2,1)S(1)} %get-tuple-element.67), channel_id=1, source_target_pairs={{0,12},{1,13},{2,14},{3,15},{4,8},{5,9},{6,10},{7,11},{8,4},{9,5},... | collective-permute-start | bytes 236552 | tf_op jit(solution)/shard_map/ppermute | solution.py:371
  51.6 9.6 %collective-permute-start.13 = (bf16[56,704]{1,0:T(8,128)(2,1)S(1)}, bf16[56,704]{1,0:T(8,128)(2,1)}, u32[]{:S(2)}, u32[]{:S(2)}) collective-permute-start(bf16[56,704]{1,0:T(8,128)(2,1)S(1)} %add_convert_fusion.t0), channel_id=1, source_target_pairs={{0,1},{1,2},{2,3},{3,0},{4,5},{5,6},{6,7},{7,4},{8,9},{9,10},{10,1... | collective-permute-start | bytes 236552 | tf_op jit(solution)/shard_map/ppermute | solution.py:371
  51.9 11.1 %copy-start.2 = (bf16[4,64,704]{2,1,0:T(8,128)(2,1)S(1)}, bf16[4,64,704]{2,1,0:T(8,128)(2,1)}, u32[]{:S(2)}) copy-start(bf16[4,64,704]{2,1,0:T(8,128)(2,1)} %get-tuple-element.43.down) | copy-start | bytes 1081348
  53.5 15.6 %collective-permute-start.7 = (bf16[88,704]{1,0:T(8,128)(2,1)S(1)}, bf16[88,704]{1,0:T(8,128)(2,1)S(1)}, u32[]{:S(2)}, u32[]{:S(2)}) collective-permute-start(bf16[88,704]{1,0:T(8,128)(2,1)S(1)} %get-tuple-element.65), channel_id=1, source_target_pairs={{0,8},{1,9},{2,10},{3,11},{4,12},{5,13},{6,14},{7,15},{8,0},{9,1},... | collective-permute-start | bytes 371720 | tf_op jit(solution)/shard_map/ppermute | solution.py:371
  58.9 10.2 %collective-permute-start.8 = (bf16[88,704]{1,0:T(8,128)(2,1)S(1)}, bf16[88,704]{1,0:T(8,128)(2,1)S(1)}, u32[]{:S(2)}, u32[]{:S(2)}) collective-permute-start(bf16[88,704]{1,0:T(8,128)(2,1)S(1)} %get-tuple-element.66), channel_id=1, source_target_pairs={{0,12},{1,13},{2,14},{3,15},{4,8},{5,9},{6,10},{7,11},{8,4},{9,5},... | collective-permute-start | bytes 371720 | tf_op jit(solution)/shard_map/ppermute | solution.py:371
  60.3 8.8 %collective-permute-start.9 = (bf16[88,704]{1,0:T(8,128)(2,1)S(1)}, bf16[88,704]{1,0:T(8,128)(2,1)S(1)}, u32[]{:S(2)}, u32[]{:S(2)}) collective-permute-start(bf16[88,704]{1,0:T(8,128)(2,1)S(1)} %get-tuple-element.60), channel_id=1, source_target_pairs={{0,4},{1,5},{2,6},{3,7},{4,0},{5,1},{6,2},{7,3},{8,12},{9,13},{10,... | collective-permute-start | bytes 371720 | tf_op jit(solution)/shard_map/ppermute | solution.py:371
  60.8 7.1 %collective-permute-start.14 = (bf16[56,704]{1,0:T(8,128)(2,1)S(1)}, bf16[56,704]{1,0:T(8,128)(2,1)S(1)}, u32[]{:S(2)}, u32[]{:S(2)}) collective-permute-start(bf16[56,704]{1,0:T(8,128)(2,1)S(1)} %add_convert_fusion.t0), channel_id=1, source_target_pairs={{0,2},{1,3},{2,0},{3,1},{4,6},{5,7},{6,4},{7,5},{8,10},{9,11},{10,... | collective-permute-start | bytes 236552 | tf_op jit(solution)/shard_map/ppermute | solution.py:371
  61.2 6.7 %collective-permute-start.15 = (bf16[56,704]{1,0:T(8,128)(2,1)S(1)}, bf16[56,704]{1,0:T(8,128)(2,1)S(1)}, u32[]{:S(2)}, u32[]{:S(2)}) collective-permute-start(bf16[56,704]{1,0:T(8,128)(2,1)S(1)} %add_convert_fusion.t0), channel_id=1, source_target_pairs={{0,3},{1,0},{2,1},{3,2},{4,7},{5,4},{6,5},{7,6},{8,11},{9,8},{10,9... | collective-permute-start | bytes 236552 | tf_op jit(solution)/shard_map/ppermute | solution.py:371
